TPU v7x, 512 devices: a whole 4x8x8 slice. The times are simulated.
512 devices in a mesh: replica: 8 (over y), fsdp: 64 (over x, z, core).
Axes of the slice: x: 4, y: 8, z: 8, core: 2. Of those that a mesh axis runs over, the one named last changes fastest.
Arguments:
- grads: bfloat16 [8, 2, 1024, 8192], P('replica', None, 'fsdp'), may hold values from -16 to 16
- errors: float32 [8, 2, 1024, 8192], P('replica', None, 'fsdp'), may hold values from -4 to 4
- basis: float32 [8192, 2, 32], P('fsdp'), may hold values from -6 to 6
Outputs:
- new_errors: float32 [8, 2, 1024, 8192], P('replica', None, 'fsdp')
- left_factor: float32 [2, 1024, 32], P(None, 'fsdp')
- new_basis: float32 [8192, 2, 32], P('fsdp')
All inputs are finite; a program needn't handle non-finite values.
Results may differ from a plain program's by a relative error of at most 0.0003.
Values sent between devices are 32-bit elements; how exact they have to be, the bound alone decides.
No kernel may reach another device: no remote copies, remote signals or barrier semaphores. Data moves between devices by JAX's collectives and lax.ppermute only.
A program may use at most 64 MiB of HBM per device.

v0:
```python
import jax
import jax.numpy as jnp
from jax import lax
from jax.sharding import PartitionSpec as P


def shards(grads, errors, basis):
    highest = lax.Precision.HIGHEST
    merged = grads[0].astype(jnp.float32) + errors[0]
    replicas = lax.axis_size("replica")
    shard_cols = basis.shape[0]
    local_factor = jnp.einsum(
        "mrd,dmk->mrk", merged, lax.all_gather(basis, "fsdp", axis=0, tiled=True), precision=highest
    )
    factor = lax.psum(local_factor, "replica") / replicas
    local_gram = jnp.einsum("mrk,mrl->mkl", factor, factor, precision=highest)
    gram = lax.psum(local_gram, "fsdp")
    chol = jnp.linalg.cholesky(gram)

    def solve_one(lower, block):
        return jax.scipy.linalg.solve_triangular(lower, block.T, lower=True).T

    left_factor = jax.vmap(solve_one)(chol, factor)
    term = jnp.einsum("mrd,mrk->dmk", merged, left_factor, precision=highest)
    total = lax.psum(term, ("replica", "fsdp")) / replicas
    begin = lax.axis_index("fsdp") * shard_cols
    new_basis = lax.dynamic_slice_in_dim(total, begin, shard_cols, 0)
    approx = jnp.einsum("mrk,dmk->mrd", left_factor, total, precision=highest)
    new_errors = merged - approx
    return (new_errors[None], left_factor, new_basis)


def solution(mesh):
    in_specs = (
        P("replica", None, "fsdp", None),
        P("replica", None, "fsdp", None),
        P("fsdp", None, None),
    )
    out_specs = (P("replica", None, "fsdp", None), P(None, "fsdp", None), P("fsdp", None, None))
    return jax.shard_map(shards, mesh=mesh, in_specs=in_specs, out_specs=out_specs, check_vma=False)
```

profile of v0, /device:TPU:1, one launch (start us, length us, event | category | flops | bytes accessed | tf_op | source)
XLA Modules:
  0.0 672.1 jit_solution(13744252146841880075)
XLA Ops:
  7.2 0.0 all-gather.2.cloned.1.call-start
  7.2 0.7 all-gather.2.cloned.1.call-update
  7.9 0.0 all-reduce.2.cloned.1.call-start
  8.0 0.0 copy-start
  8.0 0.0 copy-start.2
  8.0 87.7 %all-gather.2.cloned.1.call-done = f32[8192,2,32]{0,2,1:T(8,128)} async-done(((f32[128,2,32]{0,2,1:T(8,128)}), f32[8192,2,32]{0,2,1:T(8,128)}) %all-gather.2.cloned.1.call-update) | async-done | bytes 2097168 | tf_op jit(solution)/shard_map/all_gather | solution.py:13
  95.7 4.0 fusion.2
  99.7 22.7 %psum.21 = f32[2,16,32]{2,1,0:T(8,128)S(1)} all-reduce(f32[2,16,32]{2,1,0:T(8,128)S(1)} %fusion.2), channel_id=1, replica_groups=mesh['replica'=8,'fsdp'=64] {'replica'}, use_global_device_ids=true, to_apply=%region_0.0 | all-reduce | flops 1024 | bytes 8192 | tf_op jit(solution)/shard_map/psum | solution.py:15
  122.4 0.2 fusion.8
  122.6 247.7 %psum.22 = f32[2,32,32]{1,2,0:T(8,128)S(1)} all-reduce(f32[2,32,32]{1,2,0:T(8,128)S(1)} %fusion.8), channel_id=1, replica_groups=mesh['replica'=8,'fsdp'=64] {'fsdp'}, use_global_device_ids=true, to_apply=%region_1.0 | all-reduce | flops 2048 | bytes 16384 | tf_op jit(solution)/shard_map/psum | solution.py:17
  370.4 0.1 copy.10
  370.4 5.9 custom-call.8
  376.3 0.1 compare_reduce_fusion
  376.5 0.1 select_bitcast_fusion
  376.5 4.9 custom-call.9
  381.5 0.2 fusion.4
  381.6 0.0 copy-done
  381.6 0.0 copy-done.2
  381.6 0.0 copy-start.3
  381.7 3.1 convolution_bitcast_fusion
  384.8 0.0 all-reduce.2.cloned.1.call-update
  384.8 275.7 %all-reduce.2.cloned.1.call-done = f32[8192,2,32]{0,2,1:T(8,128)} async-done(((f32[8192,2,32]{0,2,1:T(8,128)}), f32[8192,2,32]{0,2,1:T(8,128)}) %all-reduce.2.cloned.1.call-update) | async-done | bytes 2097168 | tf_op jit(solution)/shard_map/psum | solution.py:25
  660.5 0.0 copy-start.1
  660.5 1.9 broadcast_multiply_fusion
  662.4 0.6 constant_dynamic-slice_fusion
  663.1 0.0 copy-done.3
  663.1 0.0 copy-done.1
  663.1 2.2 fusion
  (4 shorter events, 0.1 us)
Async XLA Ops:
  7.2 88.5 %all-gather.2.cloned.1.call-start = ((), (), s32[]{:S(2)}) async-start(), calls=%async_computation | async-start | bytes 2129920 | tf_op jit(solution)/shard_map/all_gather | solution.py:13
  7.9 652.6 %all-reduce.2.cloned.1.call-start = ((), (), s32[]{:S(2)}) async-start(), calls=%async_computation.1 | async-start | bytes 4194304 | tf_op jit(solution)/shard_map/psum | solution.py:25
  8.0 373.7 %copy-start = (f32[1,2,16,8192]{3,2,1,0:T(8,128)S(1)}, f32[1,2,16,8192]{3,2,1,0:T(8,128)}, u32[]{:S(2)}) copy-start(f32[1,2,16,8192]{3,2,1,0:T(8,128)} %param.4) | copy-start | bytes 3145732
  8.0 373.7 %copy-start.2 = (bf16[1,2,16,8192]{3,2,1,0:T(8,128)(2,1)S(1)}, bf16[1,2,16,8192]{3,2,1,0:T(8,128)(2,1)}, u32[]{:S(2)}) copy-start(bf16[1,2,16,8192]{3,2,1,0:T(8,128)(2,1)} %param.3) | copy-start | bytes 1572868
  381.6 281.4 %copy-start.3 = (f32[2,32,16]{1,2,0:T(8,128)}, f32[2,32,16]{1,2,0:T(8,128)S(1)}, u32[]{:S(2)}) copy-start(f32[2,32,16]{1,2,0:T(8,128)S(1)} %fusion.4) | copy-start | bytes 12292
  660.5 2.5 copy-start.1
Sparse Core Ops, SparseCore 0:
  11.1 84.5 all-gather.1
  385.0 275.5 all-reduce.1
where the time goes:
time: 672 us
  waiting for transfers between devices  364 us (54%)
  blocking collectives  270 us (40%)
  between operations  14.1 us (2%)
  other arithmetic  12.9 us (2%)
  matrix products  9.7 us (1%)
    psum x1, waiting for transfers between devices, shards(): total = lax.psum(term, ('replica', 'fsdp')) / replicas  276 us
    psum x1, blocking collectives, shards(): gram = lax.psum(local_gram, 'fsdp')  248 us
    all_gather x1, waiting for transfers between devices, shards(): lax.all_gather(basis, 'fsdp', axis=0, tiled=True)  87.7 us
    psum x1, blocking collectives, shards(): factor = lax.psum(local_factor, 'replica') / replicas  22.7 us
  transfers between devices with their start and end apart: 2, of which 2 were waited for; matrix products, arithmetic and copies ran while one was open for 0% of the time, Pallas kernels for 0%

commit v1 on v0

v1 whole, which is shorter than its diff:
```python
import jax
import jax.numpy as jnp
from jax import lax
from jax.experimental import pallas as pl
from jax.experimental.pallas import tpu as pltpu
from jax.sharding import Mesh, PartitionSpec as P

NX, NZ, NC = 4, 8, 2
LANES = 128
HIGHEST = lax.Precision.HIGHEST
F32 = jnp.float32
VMEM = pl.BlockSpec(memory_space=pltpu.VMEM)


def cost(flops, moved):
    return pl.CostEstimate(flops=flops, bytes_accessed=moved, transcendentals=0)


def dot(a, b, dims):
    return lax.dot_general(a, b, (dims, ((), ())), precision=HIGHEST, preferred_element_type=F32)


def merge_kernel(grads, errors, out):
    for m in range(2):
        merged = grads[0, m].astype(F32) + errors[0, m]
        for block in range(16):
            out[block, 0, m] = merged[:, block * LANES : (block + 1) * LANES]


def merge(grads, errors):
    _, mats, rows, width = grads.shape
    part = width // NX
    return pl.pallas_call(
        merge_kernel,
        grid=(NX,),
        in_specs=[pl.BlockSpec((1, mats, rows, part), lambda i: (0, 0, 0, i))] * 2,
        out_specs=pl.BlockSpec((16, 1, mats, rows, LANES), lambda i: (0, i, 0, 0, 0)),
        out_shape=jax.ShapeDtypeStruct((16, NX, mats, rows, LANES), F32),
        cost_estimate=cost(2**19, 5 * 2**19),
        name="merge",
    )(grads, errors)


def factor_kernel(recv, b0, b1, b2, b3, mean_out, send):
    x = lax.axis_index("x")
    packed = jnp.stack([b0[...], b1[...], b2[...], b3[...]])
    columns, weights = [], []
    for part in range(NX):
        blocks = []
        for m in range(2):
            for c in range(NC):
                total = recv[c, part, m]
                for a in range(1, 8):
                    total = total + recv[2 * a + c, part, m]
                blocks.append(total)
        columns.append(jnp.concatenate(blocks, axis=0) * 0.125)
        back = lax.rem(x - part + NX, NX)
        chosen = packed[0]
        for k in range(1, NX):
            chosen = jnp.where(back == k, packed[k], chosen)
        weights.append(chosen[:, :64])
        weights.append(chosen[:, 64:])
    mean = jnp.concatenate(columns, axis=1)
    mean_out[...] = mean
    partial = dot(mean, jnp.concatenate(weights, axis=0), ((1,), (0,)))
    piece = jnp.concatenate(
        [
            partial[16 * (2 * m + c) : 16 * (2 * m + c + 1), 32 * m : 32 * (m + 1)]
            for m in range(2)
            for c in range(NC)
        ],
        axis=1,
    )
    for i in range(16):
        send[i] = piece


def factor_part(recv, shards):
    return pl.pallas_call(
        factor_kernel,
        in_specs=[VMEM] * 5,
        out_specs=[VMEM] * 2,
        out_shape=[
            jax.ShapeDtypeStruct((64, 512), F32),
            jax.ShapeDtypeStruct((16, 16, LANES), F32),
        ],
        cost_estimate=cost(2**22, 2**20 + 2**19),
        name="factor_part",
    )(recv, *shards)


def term_kernel(recv, mean, send):
    factor = recv[0]
    for i in range(1, 16):
        factor = factor + recv[i]
    blank = jnp.zeros((16, 32), F32)
    rows = []
    for m in range(2):
        for c in range(NC):
            piece = factor[:, 32 * (2 * m + c) : 32 * (2 * m + c + 1)]
            rows.append(jnp.concatenate([piece, blank] if m == 0 else [blank, piece], axis=1))
    blocked = jnp.concatenate(rows, axis=0)
    term = dot(mean[...], blocked, ((0,), (0,)))
    for g in range(NX * NZ):
        low = term[16 * g : 16 * g + 8]
        high = term[16 * g + 8 : 16 * g + 16]
        send[g, 0:8] = jnp.concatenate([low, high], axis=1)
        send[g, 8:24] = factor


def term_part(recv, mean):
    return pl.pallas_call(
        term_kernel,
        in_specs=[VMEM] * 2,
        out_specs=VMEM,
        out_shape=jax.ShapeDtypeStruct((NX * NZ, 24, LANES), F32),
        cost_estimate=cost(2**23, 2**20),
        name="term_part",
    )(recv, mean)


def spread_kernel(recv, send):
    total = recv[0]
    for g in range(1, NX * NZ):
        total = total + recv[g]
    for i in range(8 * NZ):
        send[i] = total


def spread(recv):
    return pl.pallas_call(
        spread_kernel,
        grid=(1,),
        in_specs=[pl.BlockSpec((NX * NZ, 8, LANES), lambda i: (0, 0, 0))],
        out_specs=pl.BlockSpec((8 * NZ, 8, LANES), lambda i: (0, 0, 0)),
        out_shape=jax.ShapeDtypeStruct((8 * NZ, 8, LANES), F32),
        cost_estimate=cost(2**15, 2**19),
        name="spread",
    )(recv)


def inverse_factors(gram):
    row = lax.broadcasted_iota(jnp.int32, (32, 64), 0)
    lane = lax.broadcasted_iota(jnp.int32, (32, 64), 1)
    left = lane < 32
    unit = jnp.where((lane == row) | (lane == row + 32), 1.0, 0.0).astype(F32)
    scale = jnp.zeros((32, 64), F32)
    for j in range(32):
        column = jnp.where(left, gram[:, j : j + 1], gram[:, 32 + j : 33 + j])
        pivot = column[j : j + 1]
        scale = jnp.where(row == j, pivot, scale)
        share = jnp.where(row > j, column / pivot, 0.0)
        gram = gram - share * gram[j : j + 1]
        unit = unit - share * unit[j : j + 1]
    return unit / jnp.sqrt(scale)


def solve_kernel(recv, solve_out, rows_out, left_out):
    x, z, c = lax.axis_index("x"), lax.axis_index("z"), lax.axis_index("c")
    whole = recv[:, 8:24, :].reshape(NX * NZ * 16, LANES)
    square = dot(whole, whole, ((0,), (0,)))
    grams = []
    for m in range(2):
        a, b = 64 * m, 64 * m + 32
        grams.append(square[a : a + 32, a : a + 32] + square[b : b + 32, b : b + 32])
    inverse = inverse_factors(jnp.concatenate(grams, axis=1))
    blank = jnp.zeros((32, 32), F32)
    parts = [inverse[:, :32], inverse[:, 32:]]
    solve_out[...] = jnp.concatenate(
        [jnp.concatenate([parts[0], blank], axis=1), jnp.concatenate([blank, parts[1]], axis=1)],
        axis=0,
    )
    wide = jnp.concatenate(
        [
            jnp.concatenate([parts[i // 2] if i == j else blank for j in range(4)], axis=1)
            for i in range(4)
        ],
        axis=0,
    )
    mine = jnp.concatenate([recv[part * NZ + z, 8:24, :] for part in range(NX)], axis=0)
    rows = dot(mine, wide, ((1,), (1,)))
    rows_out[...] = rows
    own = rows[0:16]
    for part in range(1, NX):
        own = jnp.where(x == part, rows[16 * part : 16 * part + 16], own)
    for m in range(2):
        left_out[m] = jnp.where(c == 0, own[:, 64 * m : 64 * m + 32], own[:, 64 * m + 32 : 64 * m + 64])


def solve(recv):
    return pl.pallas_call(
        solve_kernel,
        in_specs=[VMEM],
        out_specs=[VMEM] * 3,
        out_shape=[
            jax.ShapeDtypeStruct((64, 64), F32),
            jax.ShapeDtypeStruct((64, LANES), F32),
            jax.ShapeDtypeStruct((2, 16, 32), F32),
        ],
        cost_estimate=cost(2**24, 2**19),
        name="solve",
    )(recv)


def approx_kernel(recv, solver, rows, send, basis_out):
    z = lax.axis_index("z")
    packed = recv[...]
    term = jnp.concatenate([packed[:, :, :64], packed[:, :, 64:]], axis=1).reshape(1024, 64)
    turned = dot(solver[...], term, ((1,), (1,)))
    own = recv[pl.ds(z * NZ, NZ)]
    own = jnp.concatenate([own[:, :, :64], own[:, :, 64:]], axis=1).reshape(LANES, 64)
    basis = dot(own, solver[...], ((1,), (1,)))
    for m in range(2):
        basis_out[:, m, :] = basis[:, 32 * m : 32 * (m + 1)]
        blocks = []
        for part in range(NX):
            for c in range(NC):
                at = 32 * (2 * m + c)
                blocks.append(rows[16 * part : 16 * part + 16, at : at + 32])
        result = dot(jnp.concatenate(blocks, axis=0), turned[32 * m : 32 * (m + 1)], ((1,), (0,)))
        for i in range(NX * NC):
            send[i, m] = result[16 * i : 16 * i + 16]


def approx_part(recv, solver, rows):
    return pl.pallas_call(
        approx_kernel,
        in_specs=[VMEM] * 3,
        out_specs=[VMEM] * 2,
        out_shape=[
            jax.ShapeDtypeStruct((NX * NC, 2, 16, 1024), F32),
            jax.ShapeDtypeStruct((LANES, 2, 32), F32),
        ],
        cost_estimate=cost(2**26, 2**20),
        name="approx_part",
    )(recv, solver, rows)


def subtract_kernel(grads, errors, recv, out):
    for m in range(2):
        merged = grads[0, m].astype(F32) + errors[0, m]
        for a in range(8):
            for c in range(NC):
                at = slice((2 * a + c) * LANES, (2 * a + c + 1) * LANES)
                out[0, m, :, at] = merged[:, at] - recv[c, m, :, a * LANES : (a + 1) * LANES]


def subtract(grads, errors, recv):
    _, mats, rows, width = grads.shape
    part = width // NX
    spec = pl.BlockSpec((1, mats, rows, part), lambda i: (0, 0, 0, i))
    return pl.pallas_call(
        subtract_kernel,
        grid=(NX,),
        in_specs=[spec, spec, pl.BlockSpec((NC, mats, rows, 1024), lambda i: (i, 0, 0, 0))],
        out_specs=spec,
        out_shape=jax.ShapeDtypeStruct(grads.shape, F32),
        cost_estimate=cost(2**19, 7 * 2**19),
        name="subtract",
    )(grads, errors, recv)


def shards(grads, errors, basis):
    send = merge(grads, errors)
    flat = basis.reshape(LANES, 64)
    held = jnp.concatenate([flat[:64], flat[64:]], axis=1)
    held, send = lax.optimization_barrier((held, send))
    recv = lax.all_to_all(send, ("y", "c"), 0, 0)
    held = lax.ppermute(held, ("y", "z"), [(y * NZ + z, z * NZ + y) for y in range(8) for z in range(NZ)])
    parts = [held] + [
        lax.ppermute(held, "x", [(i, (i + k) % NX) for i in range(NX)]) for k in range(1, NX)
    ]
    mean, send = factor_part(recv, parts)
    recv = lax.all_to_all(send, ("y", "c"), 0, 0)
    send = term_part(recv, mean)
    recv = lax.all_to_all(send, ("x", "z"), 0, 0)
    gathered = lax.all_to_all(spread(recv), ("y", "z"), 0, 0)
    solver, rows, left_factor = solve(recv)
    send, new_basis = approx_part(gathered, solver, rows)
    recv = lax.all_to_all(send, ("x", "c"), 0, 0)
    return (subtract(grads, errors, recv), left_factor, new_basis)


def solution(mesh):
    fine = Mesh(mesh.devices.reshape(8, NX, NZ, NC), ("y", "x", "z", "c"))
    fsdp = ("x", "z", "c")
    in_specs = (P("y", None, fsdp, None), P("y", None, fsdp, None), P(fsdp, None, None))
    out_specs = (P("y", None, fsdp, None), P(None, fsdp, None), P(fsdp, None, None))
    return jax.shard_map(shards, mesh=fine, in_specs=in_specs, out_specs=out_specs, check_vma=False)
```

time: 672 us -> 156 us (0.23)
  waiting for transfers between devices: 364 us -> 41.1 us
  blocking collectives: 270 us -> 54.7 us
  starting transfers between devices: 0.08 us -> 31.6 us
  Pallas kernels: 0 us -> 22.4 us
  between operations: 14.1 us -> 0.74 us
  other arithmetic: 12.9 us -> 0.09 us
  matrix products: 9.7 us -> 0 us
    psum x1 -> x0, waiting for transfers between devices: 276 us -> none  [shards(): total = lax.psum(term, ('replica', 'fsdp')) / replicas]
    psum x2 -> x0, blocking collectives: 270 us -> none  [the longest x1 248 us: shards(): gram = lax.psum(local_gram, 'fsdp')]
    all_gather x1 -> x0, waiting for transfers between devices: 87.7 us -> none  [shards(): lax.all_gather(basis, 'fsdp', axis=0, tiled=True)]
    all_to_all x0 -> x2, blocking collectives: none -> 54.7 us  [the longest x1 35.2 us: shards(): recv = lax.all_to_all(send, ('y', 'c'), 0, 0)]
    all_to_all x0 -> x3, waiting for transfers between devices: none -> 37.5 us  [the longest x1 16 us: shards(): recv = lax.all_to_all(send, ('y', 'c'), 0, 0)]
    all_to_all x0 -> x3, starting transfers between devices: none -> 23.3 us  [the longest x1 10.3 us: shards(): recv = lax.all_to_all(send, ('y', 'c'), 0, 0)]
    pallas_call x0 -> x7, Pallas kernels: none -> 22.4 us  [the longest x1 5.4 us: solve(): pl.pallas_call(solve_kernel, in_specs=[VMEM], out_specs=[VMEM] * 3, out_s...]
    another operation x7 -> x0, other arithmetic: 11 us -> none  [the longest x4 6.03 us: shards(): chol = jnp.linalg.cholesky(gram)]
  transfers between devices with their start and end apart: 2 -> 7, of which waited for: 2 -> 5; matrix products, arithmetic and copies ran while one was open for 0% -> 0% of each run, Pallas kernels for 0% -> 3%
where the time goes in v1:
time: 156 us; the launch traced here: 155 us
  blocking collectives  54.7 us (35%)
  waiting for transfers between devices  41.1 us (26%)
  starting transfers between devices  31.6 us (20%)
  Pallas kernels  22.4 us (14%)
  local copies, waits for them, and re-layouts  4.42 us (3%)
    all_to_all x1, blocking collectives, shards(): recv = lax.all_to_all(send, ('y', 'c'), 0, 0)  35.2 us
    all_to_all x1, blocking collectives, shards(): recv = lax.all_to_all(send, ('x', 'z'), 0, 0)  19.5 us
    all_to_all x1, waiting for transfers between devices, shards(): recv = lax.all_to_all(send, ('y', 'c'), 0, 0)  16 us
    all_to_all x1, waiting for transfers between devices, shards(): recv = lax.all_to_all(send, ('x', 'c'), 0, 0)  14.4 us
    all_to_all x1, starting transfers between devices, shards(): recv = lax.all_to_all(send, ('y', 'c'), 0, 0)  10.3 us
    ppermute x3, starting transfers between devices, shards(): lax.ppermute(held, 'x', [(i, (i + k) % NX) for i in range(NX)])  7.66 us
    all_to_all x1, starting transfers between devices, shards(): recv = lax.all_to_all(send, ('x', 'c'), 0, 0)  7.12 us
    all_to_all x1, waiting for transfers between devices, shards(): gathered = lax.all_to_all(spread(recv), ('y', 'z'), 0, 0)  7.07 us
  transfers between devices with their start and end apart: 7, of which 5 were waited for; matrix products, arithmetic and copies ran while one was open for 0% of the time, Pallas kernels for 3%

profile of v1, /device:TPU:1, one launch (start us, length us, event | category | flops | bytes accessed | tf_op | source)
XLA Modules:
  0.0 154.9 jit_solution(2084281313337879877)
XLA Ops:
  0.6 0.9 fusion
  1.5 0.1 copy.9
  1.6 0.1 copy.10
  1.7 0.1 pad_maximum_fusion
  1.8 3.5 %merge.1 = f32[16,4,2,16,128]{4,3,2,1,0:T(8,128)} custom-call(bf16[1,2,16,8192]{3,2,1,0:T(8,128)(2,1)} %grads.3, f32[1,2,16,8192]{3,2,1,0:T(8,128)} %errors.3), custom_call_target="tpu_custom_call" | custom-call | flops 524288 | bytes 2621440 | tf_op jit(solution)/shard_map/merge/pallas_call | solution.py:33
  5.3 10.3 %all-to-all-start = ((f32[16,4,2,16,128]{4,3,2,1,0:T(8,128)}), f32[16,4,2,16,128]{4,3,2,1,0:T(8,128)S(1)}, u32[]{:S(2)}, u32[]{:S(2)}) async-start(f32[16,4,2,16,128]{4,3,2,1,0:T(8,128)} %merge.1), calls=%async_computation | async-start | bytes 2097152 | tf_op jit(solution)/shard_map/all_to_all | solution.py:268
  15.6 0.7 collective-permute-start
  16.3 0.0 collective-permute-done.b0
  16.3 0.0 copy-start.4
  16.3 2.7 %collective-permute-start.3 = (f32[64,128]{1,0:T(8,128)S(1)}, f32[64,128]{1,0:T(8,128)S(1)}, u32[]{:S(2)}, u32[]{:S(2)}) collective-permute-start(f32[64,128]{1,0:T(8,128)S(1)} %collective-permute-done.b0), channel_id=1, source_target_pairs={{0,48},{16,0},{32,16},{48,32},{1,49},{17,1},{33,17},{49,33},{2,50}... | collective-permute-start | bytes 98312 | tf_op jit(solution)/shard_map/ppermute | solution.py:271
  19.0 2.4 %collective-permute-start.2 = (f32[64,128]{1,0:T(8,128)S(1)}, f32[64,128]{1,0:T(8,128)S(1)}, u32[]{:S(2)}, u32[]{:S(2)}) collective-permute-start(f32[64,128]{1,0:T(8,128)S(1)} %collective-permute-done.b0), channel_id=1, source_target_pairs={{0,32},{16,48},{32,0},{48,16},{1,33},{17,49},{33,1},{49,17},{2,34}... | collective-permute-start | bytes 98312 | tf_op jit(solution)/shard_map/ppermute | solution.py:271
  21.5 2.5 %collective-permute-start.1 = (f32[64,128]{1,0:T(8,128)S(1)}, f32[64,128]{1,0:T(8,128)S(1)}, u32[]{:S(2)}, u32[]{:S(2)}) collective-permute-start(f32[64,128]{1,0:T(8,128)S(1)} %collective-permute-done.b0), channel_id=1, source_target_pairs={{0,16},{16,32},{32,48},{48,0},{1,17},{17,33},{33,49},{49,1},{2,18}... | collective-permute-start | bytes 98312 | tf_op jit(solution)/shard_map/ppermute | solution.py:271
  24.0 0.0 collective-permute-done.3.b3
  24.0 0.0 copy-start.5
  24.0 1.5 collective-permute-done.2.b2
  25.5 0.0 copy-start.6
  25.5 2.1 %collective-permute-done.1.b1 = f32[64,128]{1,0:T(8,128)S(1)} collective-permute-done((f32[64,128]{1,0:T(8,128)S(1)}, f32[64,128]{1,0:T(8,128)S(1)}, u32[]{:S(2)}, u32[]{:S(2)}) %collective-permute-start.1) | collective-permute-done | bytes 32800 | tf_op jit(solution)/shard_map/ppermute | solution.py:271
  27.6 0.0 copy-start.7
  27.6 16.0 %all-to-all-done.recv = f32[16,4,2,16,128]{4,3,2,1,0:T(8,128)S(1)} async-done(((f32[16,4,2,16,128]{4,3,2,1,0:T(8,128)}), f32[16,4,2,16,128]{4,3,2,1,0:T(8,128)S(1)}, u32[]{:S(2)}, u32[]{:S(2)}) %all-to-all-start) | async-done | bytes 1048608 | tf_op jit(solution)/shard_map/all_to_all | solution.py:268
  43.6 0.0 copy-done.4
  43.6 0.0 copy-done.5
  43.6 0.0 copy-done.6
  43.6 0.0 copy-done.7
  43.6 0.0 copy-start.1
  43.7 1.0 copy-done.1
  44.6 2.3 %factor_part.1 = (f32[64,512]{1,0:T(8,128)}, f32[16,16,128]{2,1,0:T(8,128)}) custom-call(f32[16,4,2,16,128]{4,3,2,1,0:T(8,128)} %copy-done.1, f32[64,128]{1,0:T(8,128)} %copy-done.4, f32[64,128]{1,0:T(8,128)} %copy-done.7, f32[64,128]{1,0:T(8,128)} %copy-done.6, f32[64,128]{1,0:T(8,128)} %copy-done.5), custom_call_target="tpu_custom_call" | custom-call | flops 4194304 | bytes 1572864 | tf_op jit(solution)/shard_map/factor_part/pallas_call | solution.py:79
  47.0 35.2 %all_to_all.25.recv = f32[16,16,128]{2,1,0:T(8,128)} all-to-all(f32[16,16,128]{2,1,0:T(8,128)} %get-tuple-element.14), channel_id=1, replica_groups=mesh['y'=8,'x'=4,'z'=8,'c'=2] {'y','c'}, dimensions={0} | all-to-all | bytes 262144 | tf_op jit(solution)/shard_map/all_to_all | solution.py:274
  82.2 2.2 %term_part.1 = f32[32,24,128]{2,1,0:T(8,128)} custom-call(f32[16,16,128]{2,1,0:T(8,128)} %all_to_all.25.recv, f32[64,512]{1,0:T(8,128)} %get-tuple-element.15.mean), custom_call_target="tpu_custom_call" | custom-call | flops 8388608 | bytes 1048576 | tf_op jit(solution)/shard_map/term_part/pallas_call | solution.py:112
  84.4 19.5 %all_to_all.26.recv = f32[32,24,128]{2,1,0:T(8,128)} all-to-all(f32[32,24,128]{2,1,0:T(8,128)} %term_part.1), channel_id=1, replica_groups=mesh['y'=8,'x'=4,'z'=8,'c'=2] {'x','z'}, dimensions={0} | all-to-all | bytes 786432 | tf_op jit(solution)/shard_map/all_to_all | solution.py:276
  103.9 1.7 %spread.1 = f32[64,8,128]{2,1,0:T(8,128)} custom-call(f32[32,24,128]{2,1,0:T(8,128)} %all_to_all.26.recv), custom_call_target="tpu_custom_call" | custom-call | flops 32768 | bytes 524288 | tf_op jit(solution)/shard_map/spread/pallas_call | solution.py:131
  105.5 5.8 %all-to-all-start.3 = ((f32[64,8,128]{2,1,0:T(8,128)}), f32[64,8,128]{2,1,0:T(8,128)S(1)}, u32[]{:S(2)}, u32[]{:S(2)}) async-start(f32[64,8,128]{2,1,0:T(8,128)} %spread.1), calls=%async_computation.3 | async-start | bytes 524288 | tf_op jit(solution)/shard_map/all_to_all | solution.py:277
  111.3 5.4 %solve.1 = (f32[64,64]{1,0:T(8,128)}, f32[64,128]{1,0:T(8,128)}, f32[2,16,32]{2,1,0:T(8,128)}) custom-call(f32[32,24,128]{2,1,0:T(8,128)} %all_to_all.26.recv), custom_call_target="tpu_custom_call" | custom-call | flops 16777216 | bytes 524288 | tf_op jit(solution)/shard_map/solve/pallas_call | solution.py:191
  116.7 7.1 %all-to-all-done.3.recv = f32[64,8,128]{2,1,0:T(8,128)S(1)} async-done(((f32[64,8,128]{2,1,0:T(8,128)}), f32[64,8,128]{2,1,0:T(8,128)S(1)}, u32[]{:S(2)}, u32[]{:S(2)}) %all-to-all-start.3) | async-done | bytes 262176 | tf_op jit(solution)/shard_map/all_to_all | solution.py:277
  123.8 0.0 copy-start.2
  123.8 0.7 copy-done.2
  124.5 3.5 %approx_part.1 = (f32[8,2,16,1024]{3,2,1,0:T(8,128)}, f32[128,2,32]{2,1,0:T(2,128)}) custom-call(f32[64,8,128]{2,1,0:T(8,128)} %copy-done.2, f32[64,64]{1,0:T(8,128)} %get-tuple-element.16.solver, f32[64,128]{1,0:T(8,128)} %get-tuple-element.17.rows), custom_call_target="tpu_custom_call" | custom-call | flops 67108864 | bytes 1048576 | tf_op jit(solution)/shard_map/approx_part/pallas_call | solution.py:226
  128.0 0.0 copy-start.3
  128.0 7.1 %all-to-all-start.4 = ((f32[8,2,16,1024]{3,2,1,0:T(8,128)}), f32[8,2,16,1024]{3,2,1,0:T(8,128)S(1)}, u32[]{:S(2)}, u32[]{:S(2)}) async-start(f32[8,2,16,1024]{3,2,1,0:T(8,128)} %get-tuple-element.18), calls=%async_computation.4 | async-start | bytes 2097152 | tf_op jit(solution)/shard_map/all_to_all | solution.py:280
  135.2 0.0 copy-done.3
  135.2 0.7 copy.11
  135.8 14.4 %all-to-all-done.4.recv = f32[8,2,16,1024]{3,2,1,0:T(8,128)S(1)} async-done(((f32[8,2,16,1024]{3,2,1,0:T(8,128)}), f32[8,2,16,1024]{3,2,1,0:T(8,128)S(1)}, u32[]{:S(2)}, u32[]{:S(2)}) %all-to-all-start.4) | async-done | bytes 1048608 | tf_op jit(solution)/shard_map/all_to_all | solution.py:280
  150.3 0.0 copy-start
  150.3 1.0 copy-done
  151.3 3.7 %subtract.1 = f32[1,2,16,8192]{3,2,1,0:T(8,128)} custom-call(bf16[1,2,16,8192]{3,2,1,0:T(8,128)(2,1)} %grads.3, f32[1,2,16,8192]{3,2,1,0:T(8,128)} %errors.3, f32[8,2,16,1024]{3,2,1,0:T(8,128)} %copy-done), custom_call_target="tpu_custom_call" | custom-call | flops 524288 | bytes 3670016 | tf_op jit(solution)/shard_map/subtract/pallas_call | solution.py:252
Async XLA Ops:
  5.3 38.3 %all-to-all-start = ((f32[16,4,2,16,128]{4,3,2,1,0:T(8,128)}), f32[16,4,2,16,128]{4,3,2,1,0:T(8,128)S(1)}, u32[]{:S(2)}, u32[]{:S(2)}) async-start(f32[16,4,2,16,128]{4,3,2,1,0:T(8,128)} %merge.1), calls=%async_computation | async-start | bytes 2097152 | tf_op jit(solution)/shard_map/all_to_all | solution.py:268
  15.6 0.7 collective-permute-start
  16.3 27.3 %copy-start.4 = (f32[64,128]{1,0:T(8,128)}, f32[64,128]{1,0:T(8,128)S(1)}, u32[]{:S(2)}) copy-start(f32[64,128]{1,0:T(8,128)S(1)} %collective-permute-done.b0) | copy-start | bytes 98308
  16.3 7.7 %collective-permute-start.3 = (f32[64,128]{1,0:T(8,128)S(1)}, f32[64,128]{1,0:T(8,128)S(1)}, u32[]{:S(2)}, u32[]{:S(2)}) collective-permute-start(f32[64,128]{1,0:T(8,128)S(1)} %collective-permute-done.b0), channel_id=1, source_target_pairs={{0,48},{16,0},{32,16},{48,32},{1,49},{17,1},{33,17},{49,33},{2,50}... | collective-permute-start | bytes 98312 | tf_op jit(solution)/shard_map/ppermute | solution.py:271
  19.0 6.5 %collective-permute-start.2 = (f32[64,128]{1,0:T(8,128)S(1)}, f32[64,128]{1,0:T(8,128)S(1)}, u32[]{:S(2)}, u32[]{:S(2)}) collective-permute-start(f32[64,128]{1,0:T(8,128)S(1)} %collective-permute-done.b0), channel_id=1, source_target_pairs={{0,32},{16,48},{32,0},{48,16},{1,33},{17,49},{33,1},{49,17},{2,34}... | collective-permute-start | bytes 98312 | tf_op jit(solution)/shard_map/ppermute | solution.py:271
  21.5 6.2 %collective-permute-start.1 = (f32[64,128]{1,0:T(8,128)S(1)}, f32[64,128]{1,0:T(8,128)S(1)}, u32[]{:S(2)}, u32[]{:S(2)}) collective-permute-start(f32[64,128]{1,0:T(8,128)S(1)} %collective-permute-done.b0), channel_id=1, source_target_pairs={{0,16},{16,32},{32,48},{48,0},{1,17},{17,33},{33,49},{49,1},{2,18}... | collective-permute-start | bytes 98312 | tf_op jit(solution)/shard_map/ppermute | solution.py:271
  24.0 19.6 %copy-start.5 = (f32[64,128]{1,0:T(8,128)}, f32[64,128]{1,0:T(8,128)S(1)}, u32[]{:S(2)}) copy-start(f32[64,128]{1,0:T(8,128)S(1)} %collective-permute-done.3.b3) | copy-start | bytes 98308
  25.5 18.1 %copy-start.6 = (f32[64,128]{1,0:T(8,128)}, f32[64,128]{1,0:T(8,128)S(1)}, u32[]{:S(2)}) copy-start(f32[64,128]{1,0:T(8,128)S(1)} %collective-permute-done.2.b2) | copy-start | bytes 98308
  27.6 16.0 %copy-start.7 = (f32[64,128]{1,0:T(8,128)}, f32[64,128]{1,0:T(8,128)S(1)}, u32[]{:S(2)}) copy-start(f32[64,128]{1,0:T(8,128)S(1)} %collective-permute-done.1.b1) | copy-start | bytes 98308
  43.6 1.0 copy-start.1
  105.5 18.3 %all-to-all-start.3 = ((f32[64,8,128]{2,1,0:T(8,128)}), f32[64,8,128]{2,1,0:T(8,128)S(1)}, u32[]{:S(2)}, u32[]{:S(2)}) async-start(f32[64,8,128]{2,1,0:T(8,128)} %spread.1), calls=%async_computation.3 | async-start | bytes 524288 | tf_op jit(solution)/shard_map/all_to_all | solution.py:277
  123.8 0.7 copy-start.2
  128.0 7.1 %copy-start.3 = (f32[128,2,32]{2,1,0:T(2,128)S(1)}, f32[128,2,32]{2,1,0:T(2,128)}, u32[]{:S(2)}) copy-start(f32[128,2,32]{2,1,0:T(2,128)} %get-tuple-element.26) | copy-start | bytes 98308
  128.0 22.2 %all-to-all-start.4 = ((f32[8,2,16,1024]{3,2,1,0:T(8,128)}), f32[8,2,16,1024]{3,2,1,0:T(8,128)S(1)}, u32[]{:S(2)}, u32[]{:S(2)}) async-start(f32[8,2,16,1024]{3,2,1,0:T(8,128)} %get-tuple-element.18), calls=%async_computation.4 | async-start | bytes 2097152 | tf_op jit(solution)/shard_map/all_to_all | solution.py:280
  150.3 1.0 copy-start

commit v2 on v1

--- a/solution.py
+++ b/solution.py
@@ -10,6 +10,8 @@
 HIGHEST = lax.Precision.HIGHEST
 F32 = jnp.float32
 VMEM = pl.BlockSpec(memory_space=pltpu.VMEM)
+HBM = pl.BlockSpec(memory_space=pltpu.HBM)
+PARAMS = pltpu.CompilerParams(vmem_limit_bytes=16 * 2**20)
 
 
 def cost(flops, moved):
@@ -20,22 +22,41 @@
     return lax.dot_general(a, b, (dims, ((), ())), precision=HIGHEST, preferred_element_type=F32)
 
 
-def merge_kernel(grads, errors, out):
-    for m in range(2):
-        merged = grads[0, m].astype(F32) + errors[0, m]
-        for block in range(16):
-            out[block, 0, m] = merged[:, block * LANES : (block + 1) * LANES]
+def chunk(x):
+    return pl.ds(x * 16 * LANES, 16 * LANES)
+
+
+def merge_kernel(grads, errors, out, grads_in, errors_in, sems):
+    copies = []
+    for x in range(NX):
+        for k, (source, target) in enumerate(((grads, grads_in), (errors, errors_in))):
+            copy = pltpu.make_async_copy(
+                source.at[0, :, :, chunk(x)], target.at[:, :, chunk(x)], sems.at[k, x]
+            )
+            copy.start()
+            copies.append(copy)
+    for x in range(NX):
+        copies[2 * x].wait()
+        copies[2 * x + 1].wait()
+        for m in range(2):
+            for block in range(16):
+                at = pl.ds((x * 16 + block) * LANES, LANES)
+                out[block, x, m] = grads_in[m, :, at].astype(F32) + errors_in[m, :, at]
 
 
 def merge(grads, errors):
     _, mats, rows, width = grads.shape
-    part = width // NX
     return pl.pallas_call(
         merge_kernel,
-        grid=(NX,),
-        in_specs=[pl.BlockSpec((1, mats, rows, part), lambda i: (0, 0, 0, i))] * 2,
-        out_specs=pl.BlockSpec((16, 1, mats, rows, LANES), lambda i: (0, i, 0, 0, 0)),
+        in_specs=[HBM] * 2,
+        out_specs=VMEM,
         out_shape=jax.ShapeDtypeStruct((16, NX, mats, rows, LANES), F32),
+        scratch_shapes=[
+            pltpu.VMEM((mats, rows, width), grads.dtype),
+            pltpu.VMEM((mats, rows, width), errors.dtype),
+            pltpu.SemaphoreType.DMA((2, NX)),
+        ],
+        compiler_params=PARAMS,
         cost_estimate=cost(2**19, 5 * 2**19),
         name="merge",
     )(grads, errors)
@@ -58,11 +79,10 @@
         chosen = packed[0]
         for k in range(1, NX):
             chosen = jnp.where(back == k, packed[k], chosen)
-        weights.append(chosen[:, :64])
-        weights.append(chosen[:, 64:])
+        weights.append(chosen)
     mean = jnp.concatenate(columns, axis=1)
     mean_out[...] = mean
-    partial = dot(mean, jnp.concatenate(weights, axis=0), ((1,), (0,)))
+    partial = dot(mean, jnp.concatenate(weights, axis=1), ((1,), (1,)))
     piece = jnp.concatenate(
         [
             partial[16 * (2 * m + c) : 16 * (2 * m + c + 1), 32 * m : 32 * (m + 1)]
@@ -84,6 +104,7 @@
             jax.ShapeDtypeStruct((64, 512), F32),
             jax.ShapeDtypeStruct((16, 16, LANES), F32),
         ],
+        compiler_params=PARAMS,
         cost_estimate=cost(2**22, 2**20 + 2**19),
         name="factor_part",
     )(recv, *shards)
@@ -100,12 +121,11 @@
             piece = factor[:, 32 * (2 * m + c) : 32 * (2 * m + c + 1)]
             rows.append(jnp.concatenate([piece, blank] if m == 0 else [blank, piece], axis=1))
     blocked = jnp.concatenate(rows, axis=0)
-    term = dot(mean[...], blocked, ((0,), (0,)))
-    for g in range(NX * NZ):
-        low = term[16 * g : 16 * g + 8]
-        high = term[16 * g + 8 : 16 * g + 16]
-        send[g, 0:8] = jnp.concatenate([low, high], axis=1)
-        send[g, 8:24] = factor
+    term = dot(blocked, mean[...], ((0,), (0,)))
+    for x in range(NX):
+        for z in range(NZ):
+            send[x * NZ + z, 0:8] = term[8 * z : 8 * z + 8, x * LANES : (x + 1) * LANES]
+            send[x * NZ + z, 8:24] = factor
 
 
 def term_part(recv, mean):
@@ -114,15 +134,16 @@
         in_specs=[VMEM] * 2,
         out_specs=VMEM,
         out_shape=jax.ShapeDtypeStruct((NX * NZ, 24, LANES), F32),
+        compiler_params=PARAMS,
         cost_estimate=cost(2**23, 2**20),
         name="term_part",
     )(recv, mean)
 
 
 def spread_kernel(recv, send):
-    total = recv[0]
+    total = recv[0, 0:8]
     for g in range(1, NX * NZ):
-        total = total + recv[g]
+        total = total + recv[g, 0:8]
     for i in range(8 * NZ):
         send[i] = total
 
@@ -130,10 +151,10 @@
 def spread(recv):
     return pl.pallas_call(
         spread_kernel,
-        grid=(1,),
-        in_specs=[pl.BlockSpec((NX * NZ, 8, LANES), lambda i: (0, 0, 0))],
-        out_specs=pl.BlockSpec((8 * NZ, 8, LANES), lambda i: (0, 0, 0)),
+        in_specs=[VMEM],
+        out_specs=VMEM,
         out_shape=jax.ShapeDtypeStruct((8 * NZ, 8, LANES), F32),
+        compiler_params=PARAMS,
         cost_estimate=cost(2**15, 2**19),
         name="spread",
     )(recv)
@@ -197,6 +218,7 @@
             jax.ShapeDtypeStruct((64, LANES), F32),
             jax.ShapeDtypeStruct((2, 16, 32), F32),
         ],
+        compiler_params=PARAMS,
         cost_estimate=cost(2**24, 2**19),
         name="solve",
     )(recv)
@@ -204,14 +226,15 @@
 
 def approx_kernel(recv, solver, rows, send, basis_out):
     z = lax.axis_index("z")
-    packed = recv[...]
-    term = jnp.concatenate([packed[:, :, :64], packed[:, :, 64:]], axis=1).reshape(1024, 64)
-    turned = dot(solver[...], term, ((1,), (1,)))
-    own = recv[pl.ds(z * NZ, NZ)]
-    own = jnp.concatenate([own[:, :, :64], own[:, :, 64:]], axis=1).reshape(LANES, 64)
-    basis = dot(own, solver[...], ((1,), (1,)))
+    term = jnp.concatenate(
+        [recv[a * NZ : (a + 1) * NZ].reshape(64, LANES) for a in range(8)], axis=1
+    )
+    turned = dot(solver[...], term, ((1,), (0,)))
+    own = turned[:, :LANES]
+    for a in range(1, 8):
+        own = jnp.where(z == a, turned[:, a * LANES : (a + 1) * LANES], own)
+    basis_out[...] = own
     for m in range(2):
-        basis_out[:, m, :] = basis[:, 32 * m : 32 * (m + 1)]
         blocks = []
         for part in range(NX):
             for c in range(NC):
@@ -229,44 +252,52 @@
         out_specs=[VMEM] * 2,
         out_shape=[
             jax.ShapeDtypeStruct((NX * NC, 2, 16, 1024), F32),
-            jax.ShapeDtypeStruct((LANES, 2, 32), F32),
-        ],
+            jax.ShapeDtypeStruct((64, LANES), F32),
+        ],
+        compiler_params=PARAMS,
         cost_estimate=cost(2**26, 2**20),
         name="approx_part",
     )(recv, solver, rows)
 
 
-def subtract_kernel(grads, errors, recv, out):
-    for m in range(2):
-        merged = grads[0, m].astype(F32) + errors[0, m]
-        for a in range(8):
-            for c in range(NC):
-                at = slice((2 * a + c) * LANES, (2 * a + c + 1) * LANES)
-                out[0, m, :, at] = merged[:, at] - recv[c, m, :, a * LANES : (a + 1) * LANES]
-
-
-def subtract(grads, errors, recv):
-    _, mats, rows, width = grads.shape
-    part = width // NX
-    spec = pl.BlockSpec((1, mats, rows, part), lambda i: (0, 0, 0, i))
+def subtract_kernel(merged, recv, out, result, sems):
+    copies = []
+    for x in range(NX):
+        for m in range(2):
+            for a in range(8):
+                for c in range(NC):
+                    at = pl.ds((x * 16 + 2 * a + c) * LANES, LANES)
+                    approx = recv[NC * x + c, m, :, a * LANES : (a + 1) * LANES]
+                    result[m, :, at] = merged[2 * a + c, x, m] - approx
+        copy = pltpu.make_async_copy(
+            result.at[:, :, chunk(x)], out.at[0, :, :, chunk(x)], sems.at[x]
+        )
+        copy.start()
+        copies.append(copy)
+    for copy in copies:
+        copy.wait()
+
+
+def subtract(merged, recv):
+    _, _, mats, rows, _ = merged.shape
+    width = NX * 16 * LANES
     return pl.pallas_call(
         subtract_kernel,
-        grid=(NX,),
-        in_specs=[spec, spec, pl.BlockSpec((NC, mats, rows, 1024), lambda i: (i, 0, 0, 0))],
-        out_specs=spec,
-        out_shape=jax.ShapeDtypeStruct(grads.shape, F32),
+        in_specs=[VMEM] * 2,
+        out_specs=HBM,
+        out_shape=jax.ShapeDtypeStruct((1, mats, rows, width), F32),
+        scratch_shapes=[pltpu.VMEM((mats, rows, width), F32), pltpu.SemaphoreType.DMA((NX,))],
+        compiler_params=PARAMS,
         cost_estimate=cost(2**19, 7 * 2**19),
         name="subtract",
-    )(grads, errors, recv)
+    )(merged, recv)
 
 
 def shards(grads, errors, basis):
-    send = merge(grads, errors)
-    flat = basis.reshape(LANES, 64)
-    held = jnp.concatenate([flat[:64], flat[64:]], axis=1)
-    held, send = lax.optimization_barrier((held, send))
-    recv = lax.all_to_all(send, ("y", "c"), 0, 0)
+    held = basis.transpose(1, 2, 0).reshape(64, LANES)
     held = lax.ppermute(held, ("y", "z"), [(y * NZ + z, z * NZ + y) for y in range(8) for z in range(NZ)])
+    merged = merge(grads, errors)
+    recv = lax.all_to_all(merged, ("y", "c"), 0, 0)
     parts = [held] + [
         lax.ppermute(held, "x", [(i, (i + k) % NX) for i in range(NX)]) for k in range(1, NX)
     ]
@@ -278,7 +309,8 @@
     solver, rows, left_factor = solve(recv)
     send, new_basis = approx_part(gathered, solver, rows)
     recv = lax.all_to_all(send, ("x", "c"), 0, 0)
-    return (subtract(grads, errors, recv), left_factor, new_basis)
+    new_basis = new_basis.reshape(2, 32, LANES).transpose(2, 0, 1)
+    return (subtract(merged, recv), left_factor, new_basis)
 
 
 def solution(mesh):

time: 156 us -> 141 us (0.904)
  blocking collectives: 54.7 us -> 74.9 us
  waiting for transfers between devices: 41.1 us -> 27.7 us
  Pallas kernels: 22.4 us -> 10.8 us
  starting transfers between devices: 31.6 us -> 24.5 us
  local copies, waits for them, and re-layouts: 4.42 us -> 2.27 us
    all_to_all x0 -> x1, blocking collectives: none -> 21.5 us  [shards(): recv = lax.all_to_all(send, ('x', 'c'), 0, 0)]
    all_to_all x2 -> x1, waiting for transfers between devices: 30.4 us -> 16 us  [shards(): recv = lax.all_to_all(merged, ('y', 'c'), 0, 0)]
    all_to_all x2 -> x1, starting transfers between devices: 17.4 us -> 10.3 us  [shards(): recv = lax.all_to_all(merged, ('y', 'c'), 0, 0)]
    pallas_call x3, Pallas kernels: 8.87 us -> 4.38 us  [the longest x1 2.25 us: subtract(): pl.pallas_call(subtract_kernel, in_specs=[VMEM] * 2, out_specs=HBM, out_s...]
    pallas_call x1, Pallas kernels: 3.53 us -> 1.19 us  [approx_part(): pl.pallas_call(approx_kernel, in_specs=[VMEM] * 3, out_specs=[VMEM] * 2,...]
    pallas_call x1, Pallas kernels: 2.35 us -> 0.41 us  [factor_part(): pl.pallas_call(factor_kernel, in_specs=[VMEM] * 5, out_specs=[VMEM] * 2,...]
    pallas_call x1, Pallas kernels: 2.23 us -> 0.39 us  [term_part(): pl.pallas_call(term_kernel, in_specs=[VMEM] * 2, out_specs=VMEM, out_shap...]
    unnamed x17 -> x6, local copies, waits for them, and re-layouts: 3.36 us -> 2.27 us
  transfers between devices with their start and end apart: 7 -> 6, of which waited for: 5 -> 4; matrix products, arithmetic and copies ran while one was open for 0% -> 0% of each run, Pallas kernels for 3% -> 3%
where the time goes in v2:
time: 141 us
  blocking collectives  74.9 us (53%)
  waiting for transfers between devices  27.7 us (20%)
  starting transfers between devices  24.5 us (17%)
  Pallas kernels  10.8 us (8%)
  local copies, waits for them, and re-layouts  2.27 us (2%)
    all_to_all x1, blocking collectives, shards(): recv = lax.all_to_all(send, ('y', 'c'), 0, 0)  34.3 us
    all_to_all x1, blocking collectives, shards(): recv = lax.all_to_all(send, ('x', 'c'), 0, 0)  21.5 us
    all_to_all x1, blocking collectives, shards(): recv = lax.all_to_all(send, ('x', 'z'), 0, 0)  19.1 us
    all_to_all x1, waiting for transfers between devices, shards(): recv = lax.all_to_all(merged, ('y', 'c'), 0, 0)  16 us
    all_to_all x1, starting transfers between devices, shards(): recv = lax.all_to_all(merged, ('y', 'c'), 0, 0)  10.3 us
    all_to_all x1, waiting for transfers between devices, shards(): gathered = lax.all_to_all(spread(recv), ('y', 'z'), 0, 0)  8.06 us
    ppermute x3, starting transfers between devices, shards(): lax.ppermute(held, 'x', [(i, (i + k) % NX) for i in range(NX)])  7.65 us
    all_to_all x1, starting transfers between devices, shards(): gathered = lax.all_to_all(spread(recv), ('y', 'z'), 0, 0)  5.82 us
  transfers between devices with their start and end apart: 6, of which 4 were waited for; matrix products, arithmetic and copies ran while one was open for 0% of the time, Pallas kernels for 3%

profile of v2, /device:TPU:1, one launch (start us, length us, event | category | flops | bytes accessed | tf_op | source)
XLA Modules:
  0.0 140.9 jit_solution(11421698708188162002)
XLA Ops:
  0.6 0.0 copy-start
  0.6 1.2 copy-done
  1.9 0.0 copy-start.1
  1.9 1.0 copy-done.1
  2.9 1.4 merge.1.merged
  4.3 0.0 copy-start.2
  4.3 10.3 %all-to-all-start = ((f32[16,4,2,16,128]{4,3,2,1,0:T(8,128)}), f32[16,4,2,16,128]{4,3,2,1,0:T(8,128)S(1)}, u32[]{:S(2)}, u32[]{:S(2)}) async-start(f32[16,4,2,16,128]{4,3,2,1,0:T(8,128)} %merge.1.merged), calls=%async_computation | async-start | bytes 2097152 | tf_op jit(solution)/shard_map/all_to_all | solution.py:300
  14.6 0.0 copy-done.2
  14.6 0.7 collective-permute-start
  15.3 0.0 collective-permute-done.b0
  15.3 2.7 %collective-permute-start.3 = (f32[64,128]{1,0:T(8,128)S(1)}, f32[64,128]{1,0:T(8,128)S(1)}, u32[]{:S(2)}, u32[]{:S(2)}) collective-permute-start(f32[64,128]{1,0:T(8,128)S(1)} %collective-permute-done.b0), channel_id=1, source_target_pairs={{0,48},{16,0},{32,16},{48,32},{1,49},{17,1},{33,17},{49,33},{2,50}... | collective-permute-start | bytes 98312 | tf_op jit(solution)/shard_map/ppermute | solution.py:302
  18.0 2.4 %collective-permute-start.2 = (f32[64,128]{1,0:T(8,128)S(1)}, f32[64,128]{1,0:T(8,128)S(1)}, u32[]{:S(2)}, u32[]{:S(2)}) collective-permute-start(f32[64,128]{1,0:T(8,128)S(1)} %collective-permute-done.b0), channel_id=1, source_target_pairs={{0,32},{16,48},{32,0},{48,16},{1,33},{17,49},{33,1},{49,17},{2,34}... | collective-permute-start | bytes 98312 | tf_op jit(solution)/shard_map/ppermute | solution.py:302
  20.5 2.5 %collective-permute-start.1 = (f32[64,128]{1,0:T(8,128)S(1)}, f32[64,128]{1,0:T(8,128)S(1)}, u32[]{:S(2)}, u32[]{:S(2)}) collective-permute-start(f32[64,128]{1,0:T(8,128)S(1)} %collective-permute-done.b0), channel_id=1, source_target_pairs={{0,16},{16,32},{32,48},{48,0},{1,17},{17,33},{33,49},{49,1},{2,18}... | collective-permute-start | bytes 98312 | tf_op jit(solution)/shard_map/ppermute | solution.py:302
  23.0 0.0 collective-permute-done.3.b3
  23.0 1.5 %collective-permute-done.2.b2 = f32[64,128]{1,0:T(8,128)S(1)} collective-permute-done((f32[64,128]{1,0:T(8,128)S(1)}, f32[64,128]{1,0:T(8,128)S(1)}, u32[]{:S(2)}, u32[]{:S(2)}) %collective-permute-start.2) | collective-permute-done | bytes 32800 | tf_op jit(solution)/shard_map/ppermute | solution.py:302
  24.5 2.1 %collective-permute-done.1.b1 = f32[64,128]{1,0:T(8,128)S(1)} collective-permute-done((f32[64,128]{1,0:T(8,128)S(1)}, f32[64,128]{1,0:T(8,128)S(1)}, u32[]{:S(2)}, u32[]{:S(2)}) %collective-permute-start.1) | collective-permute-done | bytes 32800 | tf_op jit(solution)/shard_map/ppermute | solution.py:302
  26.6 16.0 %all-to-all-done.recv = f32[16,4,2,16,128]{4,3,2,1,0:T(8,128)S(1)} async-done(((f32[16,4,2,16,128]{4,3,2,1,0:T(8,128)}), f32[16,4,2,16,128]{4,3,2,1,0:T(8,128)S(1)}, u32[]{:S(2)}, u32[]{:S(2)}) %all-to-all-start) | async-done | bytes 1048608 | tf_op jit(solution)/shard_map/all_to_all | solution.py:300
  42.6 0.4 factor_part.1
  43.0 34.3 %all_to_all.25.recv = f32[16,16,128]{2,1,0:T(8,128)S(1)} all-to-all(f32[16,16,128]{2,1,0:T(8,128)S(1)} %get-tuple-element.10), channel_id=1, replica_groups=mesh['y'=8,'x'=4,'z'=8,'c'=2] {'y','c'}, dimensions={0} | all-to-all | bytes 262144 | tf_op jit(solution)/shard_map/all_to_all | solution.py:305
  77.4 0.4 term_part.1
  77.7 19.1 %all_to_all.26.recv = f32[32,24,128]{2,1,0:T(8,128)S(1)} all-to-all(f32[32,24,128]{2,1,0:T(8,128)S(1)} %term_part.1), channel_id=1, replica_groups=mesh['y'=8,'x'=4,'z'=8,'c'=2] {'x','z'}, dimensions={0} | all-to-all | bytes 786432 | tf_op jit(solution)/shard_map/all_to_all | solution.py:307
  96.9 0.8 spread.1
  97.6 5.8 %all-to-all-start.3 = ((f32[64,8,128]{2,1,0:T(8,128)}), f32[64,8,128]{2,1,0:T(8,128)S(1)}, u32[]{:S(2)}, u32[]{:S(2)}) async-start(f32[64,8,128]{2,1,0:T(8,128)} %spread.1), calls=%async_computation.3 | async-start | bytes 524288 | tf_op jit(solution)/shard_map/all_to_all | solution.py:308
  103.5 4.4 %solve.1 = (f32[64,64]{1,0:T(8,128)S(1)}, f32[64,128]{1,0:T(8,128)S(1)}, f32[2,16,32]{2,1,0:T(8,128)}) custom-call(f32[32,24,128]{2,1,0:T(8,128)S(1)} %all_to_all.26.recv), custom_call_target="tpu_custom_call" | custom-call | flops 16777216 | bytes 524288 | tf_op jit(solution)/shard_map/solve/pallas_call | solution.py:212
  107.9 8.1 %all-to-all-done.3.recv = f32[64,8,128]{2,1,0:T(8,128)S(1)} async-done(((f32[64,8,128]{2,1,0:T(8,128)}), f32[64,8,128]{2,1,0:T(8,128)S(1)}, u32[]{:S(2)}, u32[]{:S(2)}) %all-to-all-start.3) | async-done | bytes 262176 | tf_op jit(solution)/shard_map/all_to_all | solution.py:308
  115.9 1.2 approx_part.1
  117.1 21.5 %all_to_all.27.recv = f32[8,2,16,1024]{3,2,1,0:T(8,128)S(1)} all-to-all(f32[8,2,16,1024]{3,2,1,0:T(8,128)S(1)} %get-tuple-element.14), channel_id=1, replica_groups=mesh['y'=8,'x'=4,'z'=8,'c'=2] {'x','c'}, dimensions={0} | all-to-all | bytes 2097152 | tf_op jit(solution)/shard_map/all_to_all | solution.py:311
  138.6 2.2 %subtract.1 = f32[1,2,16,8192]{3,2,1,0:T(8,128)} custom-call(f32[16,4,2,16,128]{4,3,2,1,0:T(8,128)} %merge.1.merged, f32[8,2,16,1024]{3,2,1,0:T(8,128)S(1)} %all_to_all.27.recv), custom_call_target="tpu_custom_call" | custom-call | flops 524288 | bytes 3670016 | tf_op jit(solution)/shard_map/subtract/pallas_call | solution.py:284
Async XLA Ops:
  0.6 1.2 copy-start
  1.9 1.0 copy-start.1
  4.3 10.3 %copy-start.2 = (f32[128,2,32]{0,2,1:T(8,128)S(1)}, f32[128,2,32]{0,2,1:T(8,128)}, u32[]{:S(2)}) copy-start(f32[128,2,32]{0,2,1:T(8,128)} %param.5) | copy-start | bytes 98308
  4.3 38.3 %all-to-all-start = ((f32[16,4,2,16,128]{4,3,2,1,0:T(8,128)}), f32[16,4,2,16,128]{4,3,2,1,0:T(8,128)S(1)}, u32[]{:S(2)}, u32[]{:S(2)}) async-start(f32[16,4,2,16,128]{4,3,2,1,0:T(8,128)} %merge.1.merged), calls=%async_computation | async-start | bytes 2097152 | tf_op jit(solution)/shard_map/all_to_all | solution.py:300
  14.6 0.7 collective-permute-start
  15.3 7.7 %collective-permute-start.3 = (f32[64,128]{1,0:T(8,128)S(1)}, f32[64,128]{1,0:T(8,128)S(1)}, u32[]{:S(2)}, u32[]{:S(2)}) collective-permute-start(f32[64,128]{1,0:T(8,128)S(1)} %collective-permute-done.b0), channel_id=1, source_target_pairs={{0,48},{16,0},{32,16},{48,32},{1,49},{17,1},{33,17},{49,33},{2,50}... | collective-permute-start | bytes 98312 | tf_op jit(solution)/shard_map/ppermute | solution.py:302
  18.0 6.5 %collective-permute-start.2 = (f32[64,128]{1,0:T(8,128)S(1)}, f32[64,128]{1,0:T(8,128)S(1)}, u32[]{:S(2)}, u32[]{:S(2)}) collective-permute-start(f32[64,128]{1,0:T(8,128)S(1)} %collective-permute-done.b0), channel_id=1, source_target_pairs={{0,32},{16,48},{32,0},{48,16},{1,33},{17,49},{33,1},{49,17},{2,34}... | collective-permute-start | bytes 98312 | tf_op jit(solution)/shard_map/ppermute | solution.py:302
  20.5 6.2 %collective-permute-start.1 = (f32[64,128]{1,0:T(8,128)S(1)}, f32[64,128]{1,0:T(8,128)S(1)}, u32[]{:S(2)}, u32[]{:S(2)}) collective-permute-start(f32[64,128]{1,0:T(8,128)S(1)} %collective-permute-done.b0), channel_id=1, source_target_pairs={{0,16},{16,32},{32,48},{48,0},{1,17},{17,33},{33,49},{49,1},{2,18}... | collective-permute-start | bytes 98312 | tf_op jit(solution)/shard_map/ppermute | solution.py:302
  97.6 18.3 %all-to-all-start.3 = ((f32[64,8,128]{2,1,0:T(8,128)}), f32[64,8,128]{2,1,0:T(8,128)S(1)}, u32[]{:S(2)}, u32[]{:S(2)}) async-start(f32[64,8,128]{2,1,0:T(8,128)} %spread.1), calls=%async_computation.3 | async-start | bytes 524288 | tf_op jit(solution)/shard_map/all_to_all | solution.py:308

commit v3 on v2

--- a/solution.py
+++ b/solution.py
@@ -56,16 +56,51 @@
             pltpu.VMEM((mats, rows, width), errors.dtype),
             pltpu.SemaphoreType.DMA((2, NX)),
         ],
-        compiler_params=PARAMS,
         cost_estimate=cost(2**19, 5 * 2**19),
         name="merge",
     )(grads, errors)
 
 
-def factor_kernel(recv, b0, b1, b2, b3, mean_out, send):
+def relay_kernel(block, out):
+    out[...] = block[...]
+
+
+def relay(block):
+    return pl.pallas_call(
+        relay_kernel,
+        in_specs=[VMEM],
+        out_specs=VMEM,
+        out_shape=jax.ShapeDtypeStruct(block.shape, F32),
+        compiler_params=PARAMS,
+        cost_estimate=cost(2**35, 2**16),
+        name="relay",
+    )(block)
+
+
+def arrange_kernel(b0, b1, b2, b3, out):
     x = lax.axis_index("x")
-    packed = jnp.stack([b0[...], b1[...], b2[...], b3[...]])
-    columns, weights = [], []
+    for part in range(NX):
+        back = lax.rem(x - part + NX, NX)
+        chosen = b0[...]
+        for k, block in ((1, b1), (2, b2), (3, b3)):
+            chosen = jnp.where(back == k, block[...], chosen)
+        out[:, part * LANES : (part + 1) * LANES] = chosen
+
+
+def arrange(shards):
+    return pl.pallas_call(
+        arrange_kernel,
+        in_specs=[VMEM] * 4,
+        out_specs=VMEM,
+        out_shape=jax.ShapeDtypeStruct((64, NX * LANES), F32),
+        compiler_params=PARAMS,
+        cost_estimate=cost(2**20, 2**18),
+        name="arrange",
+    )(*shards)
+
+
+def factor_kernel(recv, weights, mean_out, send):
+    columns = []
     for part in range(NX):
         blocks = []
         for m in range(2):
@@ -75,14 +110,9 @@
                     total = total + recv[2 * a + c, part, m]
                 blocks.append(total)
         columns.append(jnp.concatenate(blocks, axis=0) * 0.125)
-        back = lax.rem(x - part + NX, NX)
-        chosen = packed[0]
-        for k in range(1, NX):
-            chosen = jnp.where(back == k, packed[k], chosen)
-        weights.append(chosen)
     mean = jnp.concatenate(columns, axis=1)
     mean_out[...] = mean
-    partial = dot(mean, jnp.concatenate(weights, axis=1), ((1,), (1,)))
+    partial = dot(mean, weights[...], ((1,), (1,)))
     piece = jnp.concatenate(
         [
             partial[16 * (2 * m + c) : 16 * (2 * m + c + 1), 32 * m : 32 * (m + 1)]
@@ -95,10 +125,10 @@
         send[i] = piece
 
 
-def factor_part(recv, shards):
+def factor_part(recv, weights):
     return pl.pallas_call(
         factor_kernel,
-        in_specs=[VMEM] * 5,
+        in_specs=[VMEM] * 2,
         out_specs=[VMEM] * 2,
         out_shape=[
             jax.ShapeDtypeStruct((64, 512), F32),
@@ -107,7 +137,7 @@
         compiler_params=PARAMS,
         cost_estimate=cost(2**22, 2**20 + 2**19),
         name="factor_part",
-    )(recv, *shards)
+    )(recv, weights)
 
 
 def term_kernel(recv, mean, send):
@@ -293,15 +323,25 @@
     )(merged, recv)
 
 
+def transposition():
+    far = {0: 4, 1: 3, 2: 2, 3: 1, 4: 0, 5: 7, 6: 6, 7: 5}
+    pairs = []
+    for a in range(8):
+        for d in range(NZ):
+            pairs.append((((a + far[d]) % 8) * NZ + a, a * NZ + (a + d) % NZ))
+    return pairs
+
+
 def shards(grads, errors, basis):
     held = basis.transpose(1, 2, 0).reshape(64, LANES)
-    held = lax.ppermute(held, ("y", "z"), [(y * NZ + z, z * NZ + y) for y in range(8) for z in range(NZ)])
+    held = lax.ppermute(held, ("y", "z"), transposition())
+    held = relay(held)
     merged = merge(grads, errors)
     recv = lax.all_to_all(merged, ("y", "c"), 0, 0)
     parts = [held] + [
         lax.ppermute(held, "x", [(i, (i + k) % NX) for i in range(NX)]) for k in range(1, NX)
     ]
-    mean, send = factor_part(recv, parts)
+    mean, send = factor_part(recv, arrange(parts))
     recv = lax.all_to_all(send, ("y", "c"), 0, 0)
     send = term_part(recv, mean)
     recv = lax.all_to_all(send, ("x", "z"), 0, 0)

time: 141 us -> 127 us (0.901)
  blocking collectives: 74.9 us -> 55.6 us
  starting transfers between devices: 24.5 us -> 33.4 us
  local copies, waits for them, and re-layouts: 2.27 us -> 0.01 us
    all_to_all x1, blocking collectives: 34.3 us -> 12.5 us  [shards(): recv = lax.all_to_all(send, ('y', 'c'), 0, 0)]
    ppermute x1, starting transfers between devices: 0.66 us -> 11.5 us  [shards(): held = lax.ppermute(held, ('y', 'z'), transposition())]
    all_to_all x1, starting transfers between devices: 10.3 us -> 6.76 us  [shards(): recv = lax.all_to_all(merged, ('y', 'c'), 0, 0)]
    all_to_all x1, blocking collectives: 19.1 us -> 21.5 us  [shards(): recv = lax.all_to_all(send, ('x', 'z'), 0, 0)]
    unnamed x6 -> x2, local copies, waits for them, and re-layouts: 2.27 us -> 0.01 us
    ppermute x3, starting transfers between devices: 7.65 us -> 9.35 us  [shards(): lax.ppermute(held, 'x', [(i, (i + k) % NX) for i in range(NX)])]
  transfers between devices with their start and end apart: 6 -> 6, of which waited for: 4 -> 4; matrix products, arithmetic and copies ran while one was open for 0% -> 0% of each run, Pallas kernels for 3% -> 5%
where the time goes in v3:
time: 127 us
  blocking collectives  55.6 us (44%)
  starting transfers between devices  33.4 us (26%)
  waiting for transfers between devices  26.6 us (21%)
  Pallas kernels  10.7 us (8%)
    all_to_all x1, blocking collectives, shards(): recv = lax.all_to_all(send, ('x', 'c'), 0, 0)  21.6 us
    all_to_all x1, blocking collectives, shards(): recv = lax.all_to_all(send, ('x', 'z'), 0, 0)  21.5 us
    all_to_all x1, waiting for transfers between devices, shards(): recv = lax.all_to_all(merged, ('y', 'c'), 0, 0)  14.9 us
    all_to_all x1, blocking collectives, shards(): recv = lax.all_to_all(send, ('y', 'c'), 0, 0)  12.5 us
    ppermute x1, starting transfers between devices, shards(): held = lax.ppermute(held, ('y', 'z'), transposition())  11.5 us
    ppermute x3, starting transfers between devices, shards(): lax.ppermute(held, 'x', [(i, (i + k) % NX) for i in range(NX)])  9.35 us
    all_to_all x1, waiting for transfers between devices, shards(): gathered = lax.all_to_all(spread(recv), ('y', 'z'), 0, 0)  8.06 us
    all_to_all x1, starting transfers between devices, shards(): recv = lax.all_to_all(merged, ('y', 'c'), 0, 0)  6.76 us
  transfers between devices with their start and end apart: 6, of which 4 were waited for; matrix products, arithmetic and copies ran while one was open for 0% of the time, Pallas kernels for 5%

profile of v3, /device:TPU:1, one launch (start us, length us, event | category | flops | bytes accessed | tf_op | source)
XLA Modules:
  0.0 126.9 jit_solution(14874460900690290198)
XLA Ops:
  0.6 11.5 %collective-permute-start = (f32[64,128]{1,0:T(8,128)}, f32[64,128]{1,0:T(8,128)S(1)}, u32[]{:S(2)}, u32[]{:S(2)}) collective-permute-start(f32[64,128]{1,0:T(8,128)} %bitcast.6), channel_id=1, source_target_pairs={{256,0},{192,2},{128,4},{64,6},{0,8},{448,10},{384,12},{320,14},{3... | collective-permute-start | bytes 98312 | tf_op jit(solution)/shard_map/ppermute | solution.py:337
  12.1 2.5 %merge.1.merged = f32[16,4,2,16,128]{4,3,2,1,0:T(8,128)} custom-call(bf16[1,2,16,8192]{3,2,1,0:T(8,128)(2,1)} %grads.1, f32[1,2,16,8192]{3,2,1,0:T(8,128)} %errors.1), custom_call_target="tpu_custom_call" | custom-call | flops 524288 | bytes 2621440 | tf_op jit(solution)/shard_map/merge/pallas_call | solution.py:49
  14.6 6.8 %all-to-all-start = ((f32[16,4,2,16,128]{4,3,2,1,0:T(8,128)}), f32[16,4,2,16,128]{4,3,2,1,0:T(8,128)S(1)}, u32[]{:S(2)}, u32[]{:S(2)}) async-start(f32[16,4,2,16,128]{4,3,2,1,0:T(8,128)} %merge.1.merged), calls=%async_computation | async-start | bytes 2097152 | tf_op jit(solution)/shard_map/all_to_all | solution.py:340
  21.3 0.0 collective-permute-done.block
  21.4 4.4 %collective-permute-start.3 = (f32[64,128]{1,0:T(8,128)S(1)}, f32[64,128]{1,0:T(8,128)S(1)}, u32[]{:S(2)}, u32[]{:S(2)}) collective-permute-start(f32[64,128]{1,0:T(8,128)S(1)} %relay.1.b0), channel_id=1, source_target_pairs={{0,48},{16,0},{32,16},{48,32},{1,49},{17,1},{33,17},{49,33},{2,50}... | collective-permute-start | bytes 98312 | tf_op jit(solution)/shard_map/ppermute | solution.py:342
  25.8 2.4 %collective-permute-start.2 = (f32[64,128]{1,0:T(8,128)S(1)}, f32[64,128]{1,0:T(8,128)S(1)}, u32[]{:S(2)}, u32[]{:S(2)}) collective-permute-start(f32[64,128]{1,0:T(8,128)S(1)} %relay.1.b0), channel_id=1, source_target_pairs={{0,32},{16,48},{32,0},{48,16},{1,33},{17,49},{33,1},{49,17},{2,34}... | collective-permute-start | bytes 98312 | tf_op jit(solution)/shard_map/ppermute | solution.py:342
  28.2 2.5 %collective-permute-start.1 = (f32[64,128]{1,0:T(8,128)S(1)}, f32[64,128]{1,0:T(8,128)S(1)}, u32[]{:S(2)}, u32[]{:S(2)}) collective-permute-start(f32[64,128]{1,0:T(8,128)S(1)} %relay.1.b0), channel_id=1, source_target_pairs={{0,16},{16,32},{32,48},{48,0},{1,17},{17,33},{33,49},{49,1},{2,18}... | collective-permute-start | bytes 98312 | tf_op jit(solution)/shard_map/ppermute | solution.py:342
  30.7 0.0 collective-permute-done.3.b3
  30.7 1.5 %collective-permute-done.2.b2 = f32[64,128]{1,0:T(8,128)S(1)} collective-permute-done((f32[64,128]{1,0:T(8,128)S(1)}, f32[64,128]{1,0:T(8,128)S(1)}, u32[]{:S(2)}, u32[]{:S(2)}) %collective-permute-start.2) | collective-permute-done | bytes 32800 | tf_op jit(solution)/shard_map/ppermute | solution.py:342
  32.2 2.1 %collective-permute-done.1.b1 = f32[64,128]{1,0:T(8,128)S(1)} collective-permute-done((f32[64,128]{1,0:T(8,128)S(1)}, f32[64,128]{1,0:T(8,128)S(1)}, u32[]{:S(2)}, u32[]{:S(2)}) %collective-permute-start.1) | collective-permute-done | bytes 32800 | tf_op jit(solution)/shard_map/ppermute | solution.py:342
  34.4 14.9 %all-to-all-done.recv = f32[16,4,2,16,128]{4,3,2,1,0:T(8,128)S(1)} async-done(((f32[16,4,2,16,128]{4,3,2,1,0:T(8,128)}), f32[16,4,2,16,128]{4,3,2,1,0:T(8,128)S(1)}, u32[]{:S(2)}, u32[]{:S(2)}) %all-to-all-start) | async-done | bytes 1048608 | tf_op jit(solution)/shard_map/all_to_all | solution.py:340
  49.3 0.4 factor_part.1
  49.7 12.5 %all_to_all.25.recv = f32[16,16,128]{2,1,0:T(8,128)S(1)} all-to-all(f32[16,16,128]{2,1,0:T(8,128)S(1)} %get-tuple-element.10), channel_id=1, replica_groups=mesh['y'=8,'x'=4,'z'=8,'c'=2] {'y','c'}, dimensions={0} | all-to-all | bytes 262144 | tf_op jit(solution)/shard_map/all_to_all | solution.py:345
  62.2 0.4 term_part.1
  62.6 21.5 %all_to_all.26.recv = f32[32,24,128]{2,1,0:T(8,128)S(1)} all-to-all(f32[32,24,128]{2,1,0:T(8,128)S(1)} %term_part.1), channel_id=1, replica_groups=mesh['y'=8,'x'=4,'z'=8,'c'=2] {'x','z'}, dimensions={0} | all-to-all | bytes 786432 | tf_op jit(solution)/shard_map/all_to_all | solution.py:347
  84.1 0.8 spread.1
  84.8 5.8 %all-to-all-start.3 = ((f32[64,8,128]{2,1,0:T(8,128)}), f32[64,8,128]{2,1,0:T(8,128)S(1)}, u32[]{:S(2)}, u32[]{:S(2)}) async-start(f32[64,8,128]{2,1,0:T(8,128)} %spread.1), calls=%async_computation.3 | async-start | bytes 524288 | tf_op jit(solution)/shard_map/all_to_all | solution.py:348
  90.6 4.4 %solve.1 = (f32[64,64]{1,0:T(8,128)S(1)}, f32[64,128]{1,0:T(8,128)S(1)}, f32[2,16,32]{2,1,0:T(8,128)}) custom-call(f32[32,24,128]{2,1,0:T(8,128)S(1)} %all_to_all.26.recv), custom_call_target="tpu_custom_call" | custom-call | flops 16777216 | bytes 524288 | tf_op jit(solution)/shard_map/solve/pallas_call | solution.py:242
  95.0 8.1 %all-to-all-done.3.recv = f32[64,8,128]{2,1,0:T(8,128)S(1)} async-done(((f32[64,8,128]{2,1,0:T(8,128)}), f32[64,8,128]{2,1,0:T(8,128)S(1)}, u32[]{:S(2)}, u32[]{:S(2)}) %all-to-all-start.3) | async-done | bytes 262176 | tf_op jit(solution)/shard_map/all_to_all | solution.py:348
  103.1 1.2 approx_part.1
  104.3 0.0 copy-start
  104.3 21.6 %all_to_all.27.recv = f32[8,2,16,1024]{3,2,1,0:T(8,128)S(1)} all-to-all(f32[8,2,16,1024]{3,2,1,0:T(8,128)S(1)} %get-tuple-element.14), channel_id=1, replica_groups=mesh['y'=8,'x'=4,'z'=8,'c'=2] {'x','c'}, dimensions={0} | all-to-all | bytes 2097152 | tf_op jit(solution)/shard_map/all_to_all | solution.py:351
  125.9 0.0 copy-done
  125.9 1.0 subtract.1
  (2 shorter events, 0.0 us)
Async XLA Ops:
  0.6 20.7 %collective-permute-start = (f32[64,128]{1,0:T(8,128)}, f32[64,128]{1,0:T(8,128)S(1)}, u32[]{:S(2)}, u32[]{:S(2)}) collective-permute-start(f32[64,128]{1,0:T(8,128)} %bitcast.6), channel_id=1, source_target_pairs={{256,0},{192,2},{128,4},{64,6},{0,8},{448,10},{384,12},{320,14},{3... | collective-permute-start | bytes 98312 | tf_op jit(solution)/shard_map/ppermute | solution.py:337
  14.6 34.7 %all-to-all-start = ((f32[16,4,2,16,128]{4,3,2,1,0:T(8,128)}), f32[16,4,2,16,128]{4,3,2,1,0:T(8,128)S(1)}, u32[]{:S(2)}, u32[]{:S(2)}) async-start(f32[16,4,2,16,128]{4,3,2,1,0:T(8,128)} %merge.1.merged), calls=%async_computation | async-start | bytes 2097152 | tf_op jit(solution)/shard_map/all_to_all | solution.py:340
  21.4 9.4 %collective-permute-start.3 = (f32[64,128]{1,0:T(8,128)S(1)}, f32[64,128]{1,0:T(8,128)S(1)}, u32[]{:S(2)}, u32[]{:S(2)}) collective-permute-start(f32[64,128]{1,0:T(8,128)S(1)} %relay.1.b0), channel_id=1, source_target_pairs={{0,48},{16,0},{32,16},{48,32},{1,49},{17,1},{33,17},{49,33},{2,50}... | collective-permute-start | bytes 98312 | tf_op jit(solution)/shard_map/ppermute | solution.py:342
  25.8 6.5 %collective-permute-start.2 = (f32[64,128]{1,0:T(8,128)S(1)}, f32[64,128]{1,0:T(8,128)S(1)}, u32[]{:S(2)}, u32[]{:S(2)}) collective-permute-start(f32[64,128]{1,0:T(8,128)S(1)} %relay.1.b0), channel_id=1, source_target_pairs={{0,32},{16,48},{32,0},{48,16},{1,33},{17,49},{33,1},{49,17},{2,34}... | collective-permute-start | bytes 98312 | tf_op jit(solution)/shard_map/ppermute | solution.py:342
  28.2 6.2 %collective-permute-start.1 = (f32[64,128]{1,0:T(8,128)S(1)}, f32[64,128]{1,0:T(8,128)S(1)}, u32[]{:S(2)}, u32[]{:S(2)}) collective-permute-start(f32[64,128]{1,0:T(8,128)S(1)} %relay.1.b0), channel_id=1, source_target_pairs={{0,16},{16,32},{32,48},{48,0},{1,17},{17,33},{33,49},{49,1},{2,18}... | collective-permute-start | bytes 98312 | tf_op jit(solution)/shard_map/ppermute | solution.py:342
  84.8 18.3 %all-to-all-start.3 = ((f32[64,8,128]{2,1,0:T(8,128)}), f32[64,8,128]{2,1,0:T(8,128)S(1)}, u32[]{:S(2)}, u32[]{:S(2)}) async-start(f32[64,8,128]{2,1,0:T(8,128)} %spread.1), calls=%async_computation.3 | async-start | bytes 524288 | tf_op jit(solution)/shard_map/all_to_all | solution.py:348
  104.3 21.6 %copy-start = (f32[16,4,2,16,128]{4,3,2,1,0:T(8,128)S(1)}, f32[16,4,2,16,128]{4,3,2,1,0:T(8,128)}, u32[]{:S(2)}) copy-start(f32[16,4,2,16,128]{4,3,2,1,0:T(8,128)} %merge.1.merged) | copy-start | bytes 3145732

commit v4 on v3

--- a/solution.py
+++ b/solution.py
@@ -6,6 +6,7 @@
 from jax.sharding import Mesh, PartitionSpec as P
 
 NX, NZ, NC = 4, 8, 2
+LOOP = [(x, 0) for x in range(NX)] + [(x, 1) for x in reversed(range(NX))]
 LANES = 128
 HIGHEST = lax.Precision.HIGHEST
 F32 = jnp.float32
@@ -26,8 +27,8 @@
     return pl.ds(x * 16 * LANES, 16 * LANES)
 
 
-def merge_kernel(grads, errors, out, grads_in, errors_in, sems):
-    copies = []
+def merge_kernel(grads, errors, out, grads_in, errors_in, blocks, sems):
+    copies, results = [], []
     for x in range(NX):
         for k, (source, target) in enumerate(((grads, grads_in), (errors, errors_in))):
             copy = pltpu.make_async_copy(
@@ -41,7 +42,12 @@
         for m in range(2):
             for block in range(16):
                 at = pl.ds((x * 16 + block) * LANES, LANES)
-                out[block, x, m] = grads_in[m, :, at].astype(F32) + errors_in[m, :, at]
+                blocks[block, x, m] = grads_in[m, :, at].astype(F32) + errors_in[m, :, at]
+        copy = pltpu.make_async_copy(blocks.at[:, x], out.at[:, x], sems.at[2, x])
+        copy.start()
+        results.append(copy)
+    for copy in results:
+        copy.wait()
 
 
 def merge(grads, errors):
@@ -49,12 +55,13 @@
     return pl.pallas_call(
         merge_kernel,
         in_specs=[HBM] * 2,
-        out_specs=VMEM,
+        out_specs=HBM,
         out_shape=jax.ShapeDtypeStruct((16, NX, mats, rows, LANES), F32),
         scratch_shapes=[
             pltpu.VMEM((mats, rows, width), grads.dtype),
             pltpu.VMEM((mats, rows, width), errors.dtype),
-            pltpu.SemaphoreType.DMA((2, NX)),
+            pltpu.VMEM((16, NX, mats, rows, LANES), F32),
+            pltpu.SemaphoreType.DMA((3, NX)),
         ],
         cost_estimate=cost(2**19, 5 * 2**19),
         name="merge",
@@ -151,11 +158,13 @@
             piece = factor[:, 32 * (2 * m + c) : 32 * (2 * m + c + 1)]
             rows.append(jnp.concatenate([piece, blank] if m == 0 else [blank, piece], axis=1))
     blocked = jnp.concatenate(rows, axis=0)
+    half = jnp.where(lax.axis_index("c") == 0, factor[:, :64], factor[:, 64:])
+    half = jnp.concatenate([half[:8], half[8:]], axis=1)
     term = dot(blocked, mean[...], ((0,), (0,)))
     for x in range(NX):
         for z in range(NZ):
             send[x * NZ + z, 0:8] = term[8 * z : 8 * z + 8, x * LANES : (x + 1) * LANES]
-            send[x * NZ + z, 8:24] = factor
+            send[x * NZ + z, 8:16] = half
 
 
 def term_part(recv, mean):
@@ -163,7 +172,7 @@
         term_kernel,
         in_specs=[VMEM] * 2,
         out_specs=VMEM,
-        out_shape=jax.ShapeDtypeStruct((NX * NZ, 24, LANES), F32),
+        out_shape=jax.ShapeDtypeStruct((NX * NZ, 16, LANES), F32),
         compiler_params=PARAMS,
         cost_estimate=cost(2**23, 2**20),
         name="term_part",
@@ -190,14 +199,13 @@
     )(recv)
 
 
-def inverse_factors(gram):
-    row = lax.broadcasted_iota(jnp.int32, (32, 64), 0)
-    lane = lax.broadcasted_iota(jnp.int32, (32, 64), 1)
-    left = lane < 32
-    unit = jnp.where((lane == row) | (lane == row + 32), 1.0, 0.0).astype(F32)
-    scale = jnp.zeros((32, 64), F32)
+def inverse_factor(gram):
+    row = lax.broadcasted_iota(jnp.int32, (32, 32), 0)
+    lane = lax.broadcasted_iota(jnp.int32, (32, 32), 1)
+    unit = jnp.where(lane == row, 1.0, 0.0).astype(F32)
+    scale = jnp.zeros((32, 32), F32)
     for j in range(32):
-        column = jnp.where(left, gram[:, j : j + 1], gram[:, 32 + j : 33 + j])
+        column = gram[:, j : j + 1]
         pivot = column[j : j + 1]
         scale = jnp.where(row == j, pivot, scale)
         share = jnp.where(row > j, column / pivot, 0.0)
@@ -206,88 +214,73 @@
     return unit / jnp.sqrt(scale)
 
 
-def solve_kernel(recv, solve_out, rows_out, left_out):
-    x, z, c = lax.axis_index("x"), lax.axis_index("z"), lax.axis_index("c")
-    whole = recv[:, 8:24, :].reshape(NX * NZ * 16, LANES)
-    square = dot(whole, whole, ((0,), (0,)))
-    grams = []
-    for m in range(2):
-        a, b = 64 * m, 64 * m + 32
-        grams.append(square[a : a + 32, a : a + 32] + square[b : b + 32, b : b + 32])
-    inverse = inverse_factors(jnp.concatenate(grams, axis=1))
+def solve_kernel(recv, out):
+    z = lax.axis_index("z")
+    packed = recv[:, 8:16, :].reshape(NX * NZ * 8, LANES)
+    low, high = packed[:, :64], packed[:, 64:]
+    square = dot(low, low, ((0,), (0,))) + dot(high, high, ((0,), (0,)))
+    inverse = inverse_factor(square[:32, :32] + square[32:, 32:])
     blank = jnp.zeros((32, 32), F32)
-    parts = [inverse[:, :32], inverse[:, 32:]]
-    solve_out[...] = jnp.concatenate(
-        [jnp.concatenate([parts[0], blank], axis=1), jnp.concatenate([blank, parts[1]], axis=1)],
+    wide = jnp.concatenate(
+        [jnp.concatenate([inverse, blank], axis=1), jnp.concatenate([blank, inverse], axis=1)],
         axis=0,
     )
-    wide = jnp.concatenate(
-        [
-            jnp.concatenate([parts[i // 2] if i == j else blank for j in range(4)], axis=1)
-            for i in range(4)
-        ],
-        axis=0,
-    )
-    mine = jnp.concatenate([recv[part * NZ + z, 8:24, :] for part in range(NX)], axis=0)
-    rows = dot(mine, wide, ((1,), (1,)))
-    rows_out[...] = rows
-    own = rows[0:16]
-    for part in range(1, NX):
-        own = jnp.where(x == part, rows[16 * part : 16 * part + 16], own)
-    for m in range(2):
-        left_out[m] = jnp.where(c == 0, own[:, 64 * m : 64 * m + 32], own[:, 64 * m + 32 : 64 * m + 64])
+    mine = []
+    for part in range(NX):
+        block = recv[part * NZ + z, 8:16]
+        mine += [block[:, :64], block[:, 64:]]
+    out[:, :64] = dot(jnp.concatenate(mine, axis=0), wide, ((1,), (1,)))
+    out[:, 64:] = wide
 
 
 def solve(recv):
     return pl.pallas_call(
         solve_kernel,
         in_specs=[VMEM],
+        out_specs=VMEM,
+        out_shape=jax.ShapeDtypeStruct((64, LANES), F32),
+        compiler_params=PARAMS,
+        cost_estimate=cost(2**24, 2**19),
+        name="solve",
+    )(recv)
+
+
+def approx_kernel(recv, mine, other, send, basis_out, left_out):
+    x, z, c = lax.axis_index("x"), lax.axis_index("z"), lax.axis_index("c")
+    for m in range(2):
+        solved = jnp.where(c == m, mine[...], other[...])
+        term = jnp.concatenate(
+            [recv[a * NZ + 4 * m : a * NZ + 4 * m + 4].reshape(32, LANES) for a in range(8)], axis=1
+        )
+        turned = dot(solved[:32, 64:96], term, ((1,), (0,)))
+        own = turned[:, :LANES]
+        for a in range(1, 8):
+            own = jnp.where(z == a, turned[:, a * LANES : (a + 1) * LANES], own)
+        basis_out[32 * m : 32 * (m + 1)] = own
+        rows = [solved[16 * at : 16 * at + 16, 32 * core : 32 * core + 32] for at, core in LOOP]
+        left = rows[0]
+        for i, (at, core) in enumerate(LOOP):
+            left = jnp.where((x == at) & (c == core), rows[i], left)
+        left_out[m] = left
+        result = dot(jnp.concatenate(rows, axis=0), turned, ((1,), (0,)))
+        for i in range(NX * NC):
+            send[i, m] = result[16 * i : 16 * i + 16]
+
+
+def approx_part(recv, mine, other):
+    return pl.pallas_call(
+        approx_kernel,
+        in_specs=[VMEM] * 3,
         out_specs=[VMEM] * 3,
         out_shape=[
-            jax.ShapeDtypeStruct((64, 64), F32),
+            jax.ShapeDtypeStruct((NX * NC, 2, 16, 1024), F32),
             jax.ShapeDtypeStruct((64, LANES), F32),
             jax.ShapeDtypeStruct((2, 16, 32), F32),
         ],
         compiler_params=PARAMS,
-        cost_estimate=cost(2**24, 2**19),
-        name="solve",
-    )(recv)
-
-
-def approx_kernel(recv, solver, rows, send, basis_out):
-    z = lax.axis_index("z")
-    term = jnp.concatenate(
-        [recv[a * NZ : (a + 1) * NZ].reshape(64, LANES) for a in range(8)], axis=1
-    )
-    turned = dot(solver[...], term, ((1,), (0,)))
-    own = turned[:, :LANES]
-    for a in range(1, 8):
-        own = jnp.where(z == a, turned[:, a * LANES : (a + 1) * LANES], own)
-    basis_out[...] = own
-    for m in range(2):
-        blocks = []
-        for part in range(NX):
-            for c in range(NC):
-                at = 32 * (2 * m + c)
-                blocks.append(rows[16 * part : 16 * part + 16, at : at + 32])
-        result = dot(jnp.concatenate(blocks, axis=0), turned[32 * m : 32 * (m + 1)], ((1,), (0,)))
-        for i in range(NX * NC):
-            send[i, m] = result[16 * i : 16 * i + 16]
-
-
-def approx_part(recv, solver, rows):
-    return pl.pallas_call(
-        approx_kernel,
-        in_specs=[VMEM] * 3,
-        out_specs=[VMEM] * 2,
-        out_shape=[
-            jax.ShapeDtypeStruct((NX * NC, 2, 16, 1024), F32),
-            jax.ShapeDtypeStruct((64, LANES), F32),
-        ],
-        compiler_params=PARAMS,
         cost_estimate=cost(2**26, 2**20),
         name="approx_part",
-    )(recv, solver, rows)
+    )(recv, mine, other)
 
 
 def subtract_kernel(merged, recv, out, result, sems):
@@ -297,7 +290,7 @@
             for a in range(8):
                 for c in range(NC):
                     at = pl.ds((x * 16 + 2 * a + c) * LANES, LANES)
-                    approx = recv[NC * x + c, m, :, a * LANES : (a + 1) * LANES]
+                    approx = recv[LOOP.index((x, c)), m, :, a * LANES : (a + 1) * LANES]
                     result[m, :, at] = merged[2 * a + c, x, m] - approx
         copy = pltpu.make_async_copy(
             result.at[:, :, chunk(x)], out.at[0, :, :, chunk(x)], sems.at[x]
@@ -346,9 +339,11 @@
     send = term_part(recv, mean)
     recv = lax.all_to_all(send, ("x", "z"), 0, 0)
     gathered = lax.all_to_all(spread(recv), ("y", "z"), 0, 0)
-    solver, rows, left_factor = solve(recv)
-    send, new_basis = approx_part(gathered, solver, rows)
-    recv = lax.all_to_all(send, ("x", "c"), 0, 0)
+    mine = solve(recv)
+    other = lax.ppermute(mine, "c", [(0, 1), (1, 0)])
+    send, new_basis, left_factor = approx_part(gathered, mine, other)
+    groups = [[x * NC + c for x, c in LOOP]]
+    recv = lax.all_to_all(send, ("x", "c"), 0, 0, axis_index_groups=groups)
     new_basis = new_basis.reshape(2, 32, LANES).transpose(2, 0, 1)
     return (subtract(merged, recv), left_factor, new_basis)
 

time: 127 us -> 125 us (0.984)
  starting transfers between devices: 33.4 us -> 36.7 us
  blocking collectives: 55.6 us -> 52.5 us
  waiting for transfers between devices: 26.6 us -> 24.4 us
    ppermute x0 -> x1, starting transfers between devices: none -> 3.18 us  [shards(): other = lax.ppermute(mine, 'c', [(0, 1), (1, 0)])]
    all_to_all x1, waiting for transfers between devices: 8.06 us -> 5.03 us  [shards(): gathered = lax.all_to_all(spread(recv), ('y', 'z'), 0, 0)]
    all_to_all x1, blocking collectives: 21.5 us -> 19 us  [shards(): recv = lax.all_to_all(send, ('x', 'z'), 0, 0)]
  transfers between devices with their start and end apart: 6 -> 7, of which waited for: 4 -> 5; matrix products, arithmetic and copies ran while one was open for 0% -> 0% of each run, Pallas kernels for 5% -> 5%
where the time goes in v4:
time: 125 us
  blocking collectives  52.5 us (42%)
  starting transfers between devices  36.7 us (29%)
  waiting for transfers between devices  24.4 us (20%)
  Pallas kernels  10.1 us (8%)
    all_to_all x1, blocking collectives, shards(): recv = lax.all_to_all(send, ('x', 'c'), 0, 0, axis_index_groups=groups)  21.1 us
    all_to_all x1, blocking collectives, shards(): recv = lax.all_to_all(send, ('x', 'z'), 0, 0)  19 us
    all_to_all x1, waiting for transfers between devices, shards(): recv = lax.all_to_all(merged, ('y', 'c'), 0, 0)  14.9 us
    all_to_all x1, blocking collectives, shards(): recv = lax.all_to_all(send, ('y', 'c'), 0, 0)  12.5 us
    ppermute x1, starting transfers between devices, shards(): held = lax.ppermute(held, ('y', 'z'), transposition())  11.5 us
    ppermute x3, starting transfers between devices, shards(): lax.ppermute(held, 'x', [(i, (i + k) % NX) for i in range(NX)])  9.35 us
    all_to_all x1, starting transfers between devices, shards(): recv = lax.all_to_all(merged, ('y', 'c'), 0, 0)  6.76 us
    all_to_all x1, starting transfers between devices, shards(): gathered = lax.all_to_all(spread(recv), ('y', 'z'), 0, 0)  5.99 us
  transfers between devices with their start and end apart: 7, of which 5 were waited for; matrix products, arithmetic and copies ran while one was open for 0% of the time, Pallas kernels for 5%

profile of v4, /device:TPU:1, one launch (start us, length us, event | category | flops | bytes accessed | tf_op | source)
XLA Modules:
  0.0 124.5 jit_solution(5885692764703381184)
XLA Ops:
  0.6 11.5 %collective-permute-start = (f32[64,128]{1,0:T(8,128)}, f32[64,128]{1,0:T(8,128)S(1)}, u32[]{:S(2)}, u32[]{:S(2)}) collective-permute-start(f32[64,128]{1,0:T(8,128)} %bitcast.6), channel_id=1, source_target_pairs={{256,0},{192,2},{128,4},{64,6},{0,8},{448,10},{384,12},{320,14},{3... | collective-permute-start | bytes 98312 | tf_op jit(solution)/shard_map/ppermute | solution.py:330
  12.1 2.2 %merge.1.merged = f32[16,4,2,16,128]{4,3,2,1,0:T(8,128)} custom-call(bf16[1,2,16,8192]{3,2,1,0:T(8,128)(2,1)} %grads.1, f32[1,2,16,8192]{3,2,1,0:T(8,128)} %errors.1), custom_call_target="tpu_custom_call" | custom-call | flops 524288 | bytes 2621440 | tf_op jit(solution)/shard_map/merge/pallas_call | solution.py:55
  14.3 6.8 %all-to-all-start = ((f32[16,4,2,16,128]{4,3,2,1,0:T(8,128)}), f32[16,4,2,16,128]{4,3,2,1,0:T(8,128)S(1)}, u32[]{:S(2)}, u32[]{:S(2)}) async-start(f32[16,4,2,16,128]{4,3,2,1,0:T(8,128)} %merge.1.merged), calls=%async_computation | async-start | bytes 2097152 | tf_op jit(solution)/shard_map/all_to_all | solution.py:333
  21.1 0.0 collective-permute-done.block
  21.1 4.4 %collective-permute-start.3 = (f32[64,128]{1,0:T(8,128)S(1)}, f32[64,128]{1,0:T(8,128)S(1)}, u32[]{:S(2)}, u32[]{:S(2)}) collective-permute-start(f32[64,128]{1,0:T(8,128)S(1)} %relay.1.b0), channel_id=1, source_target_pairs={{0,48},{16,0},{32,16},{48,32},{1,49},{17,1},{33,17},{49,33},{2,50}... | collective-permute-start | bytes 98312 | tf_op jit(solution)/shard_map/ppermute | solution.py:335
  25.5 2.4 %collective-permute-start.2 = (f32[64,128]{1,0:T(8,128)S(1)}, f32[64,128]{1,0:T(8,128)S(1)}, u32[]{:S(2)}, u32[]{:S(2)}) collective-permute-start(f32[64,128]{1,0:T(8,128)S(1)} %relay.1.b0), channel_id=1, source_target_pairs={{0,32},{16,48},{32,0},{48,16},{1,33},{17,49},{33,1},{49,17},{2,34}... | collective-permute-start | bytes 98312 | tf_op jit(solution)/shard_map/ppermute | solution.py:335
  28.0 2.5 %collective-permute-start.1 = (f32[64,128]{1,0:T(8,128)S(1)}, f32[64,128]{1,0:T(8,128)S(1)}, u32[]{:S(2)}, u32[]{:S(2)}) collective-permute-start(f32[64,128]{1,0:T(8,128)S(1)} %relay.1.b0), channel_id=1, source_target_pairs={{0,16},{16,32},{32,48},{48,0},{1,17},{17,33},{33,49},{49,1},{2,18}... | collective-permute-start | bytes 98312 | tf_op jit(solution)/shard_map/ppermute | solution.py:335
  30.5 0.0 collective-permute-done.3.b3
  30.5 1.5 %collective-permute-done.2.b2 = f32[64,128]{1,0:T(8,128)S(1)} collective-permute-done((f32[64,128]{1,0:T(8,128)S(1)}, f32[64,128]{1,0:T(8,128)S(1)}, u32[]{:S(2)}, u32[]{:S(2)}) %collective-permute-start.2) | collective-permute-done | bytes 32800 | tf_op jit(solution)/shard_map/ppermute | solution.py:335
  32.0 2.1 %collective-permute-done.1.b1 = f32[64,128]{1,0:T(8,128)S(1)} collective-permute-done((f32[64,128]{1,0:T(8,128)S(1)}, f32[64,128]{1,0:T(8,128)S(1)}, u32[]{:S(2)}, u32[]{:S(2)}) %collective-permute-start.1) | collective-permute-done | bytes 32800 | tf_op jit(solution)/shard_map/ppermute | solution.py:335
  34.2 14.9 %all-to-all-done.recv = f32[16,4,2,16,128]{4,3,2,1,0:T(8,128)S(1)} async-done(((f32[16,4,2,16,128]{4,3,2,1,0:T(8,128)}), f32[16,4,2,16,128]{4,3,2,1,0:T(8,128)S(1)}, u32[]{:S(2)}, u32[]{:S(2)}) %all-to-all-start) | async-done | bytes 1048608 | tf_op jit(solution)/shard_map/all_to_all | solution.py:333
  49.0 0.4 factor_part.1
  49.4 12.5 %all_to_all.25.recv = f32[16,16,128]{2,1,0:T(8,128)S(1)} all-to-all(f32[16,16,128]{2,1,0:T(8,128)S(1)} %get-tuple-element.8), channel_id=1, replica_groups=mesh['y'=8,'x'=4,'z'=8,'c'=2] {'y','c'}, dimensions={0} | all-to-all | bytes 262144 | tf_op jit(solution)/shard_map/all_to_all | solution.py:338
  61.9 0.4 term_part.1
  62.3 19.0 %all_to_all.26.recv = f32[32,16,128]{2,1,0:T(8,128)S(1)} all-to-all(f32[32,16,128]{2,1,0:T(8,128)S(1)} %term_part.1), channel_id=1, replica_groups=mesh['y'=8,'x'=4,'z'=8,'c'=2] {'x','z'}, dimensions={0} | all-to-all | bytes 524288 | tf_op jit(solution)/shard_map/all_to_all | solution.py:340
  81.3 0.8 spread.1
  82.0 6.0 %all-to-all-start.3 = ((f32[64,8,128]{2,1,0:T(8,128)}), f32[64,8,128]{2,1,0:T(8,128)S(1)}, u32[]{:S(2)}, u32[]{:S(2)}) async-start(f32[64,8,128]{2,1,0:T(8,128)} %spread.1), calls=%async_computation.3 | async-start | bytes 524288 | tf_op jit(solution)/shard_map/all_to_all | solution.py:341
  88.0 3.4 %solve.1.mine = f32[64,128]{1,0:T(8,128)S(1)} custom-call(f32[32,16,128]{2,1,0:T(8,128)S(1)} %all_to_all.26.recv), custom_call_target="tpu_custom_call" | custom-call | flops 16777216 | bytes 524288 | tf_op jit(solution)/shard_map/solve/pallas_call | solution.py:237
  91.4 3.2 %collective-permute-start.4 = (f32[64,128]{1,0:T(8,128)S(1)}, f32[64,128]{1,0:T(8,128)S(1)}, u32[]{:S(2)}, u32[]{:S(2)}) collective-permute-start(f32[64,128]{1,0:T(8,128)S(1)} %solve.1.mine), channel_id=1, source_target_pairs={{0,1},{1,0},{2,3},{3,2},{4,5},{5,4},{6,7},{7,6},{8,9},{9,8},{10,11... | collective-permute-start | bytes 98312 | tf_op jit(solution)/shard_map/ppermute | solution.py:343
  94.6 0.8 collective-permute-done.4.other
  95.4 5.0 %all-to-all-done.3.recv = f32[64,8,128]{2,1,0:T(8,128)S(1)} async-done(((f32[64,8,128]{2,1,0:T(8,128)}), f32[64,8,128]{2,1,0:T(8,128)S(1)}, u32[]{:S(2)}, u32[]{:S(2)}) %all-to-all-start.3) | async-done | bytes 262176 | tf_op jit(solution)/shard_map/all_to_all | solution.py:341
  100.5 2.0 %approx_part.1 = (f32[8,2,16,1024]{3,2,1,0:T(8,128)S(1)}, f32[64,128]{1,0:T(8,128)}, f32[2,16,32]{2,1,0:T(8,128)}) custom-call(f32[64,8,128]{2,1,0:T(8,128)S(1)} %all-to-all-done.3.recv, f32[64,128]{1,0:T(8,128)S(1)} %solve.1.mine, f32[64,128]{1,0:T(8,128)S(1)} %collective-permute-done.4.other), custom_call_target="tpu_custom_call" | custom-call | flops 67108864 | bytes 1048576 | tf_op jit(solution)/shard_map/approx_part/pallas_call | solution.py:271
  102.4 0.0 copy-start
  102.4 21.1 %all_to_all.27.recv = f32[8,2,16,1024]{3,2,1,0:T(8,128)S(1)} all-to-all(f32[8,2,16,1024]{3,2,1,0:T(8,128)S(1)} %get-tuple-element.10), channel_id=1, replica_groups={{0,16,32,48,49,33,17,1},{2,18,34,50,51,35,19,3},{4,20,36,52,53,37,21,5}..., dimensions={0} | all-to-all | bytes 2097152 | tf_op jit(solution)/shard_map/all_to_all | solution.py:346
  123.5 0.0 copy-done
  123.5 1.0 subtract.1
  (2 shorter events, 0.0 us)
Async XLA Ops:
  0.6 20.5 %collective-permute-start = (f32[64,128]{1,0:T(8,128)}, f32[64,128]{1,0:T(8,128)S(1)}, u32[]{:S(2)}, u32[]{:S(2)}) collective-permute-start(f32[64,128]{1,0:T(8,128)} %bitcast.6), channel_id=1, source_target_pairs={{256,0},{192,2},{128,4},{64,6},{0,8},{448,10},{384,12},{320,14},{3... | collective-permute-start | bytes 98312 | tf_op jit(solution)/shard_map/ppermute | solution.py:330
  14.3 34.7 %all-to-all-start = ((f32[16,4,2,16,128]{4,3,2,1,0:T(8,128)}), f32[16,4,2,16,128]{4,3,2,1,0:T(8,128)S(1)}, u32[]{:S(2)}, u32[]{:S(2)}) async-start(f32[16,4,2,16,128]{4,3,2,1,0:T(8,128)} %merge.1.merged), calls=%async_computation | async-start | bytes 2097152 | tf_op jit(solution)/shard_map/all_to_all | solution.py:333
  21.1 9.4 %collective-permute-start.3 = (f32[64,128]{1,0:T(8,128)S(1)}, f32[64,128]{1,0:T(8,128)S(1)}, u32[]{:S(2)}, u32[]{:S(2)}) collective-permute-start(f32[64,128]{1,0:T(8,128)S(1)} %relay.1.b0), channel_id=1, source_target_pairs={{0,48},{16,0},{32,16},{48,32},{1,49},{17,1},{33,17},{49,33},{2,50}... | collective-permute-start | bytes 98312 | tf_op jit(solution)/shard_map/ppermute | solution.py:335
  25.5 6.5 %collective-permute-start.2 = (f32[64,128]{1,0:T(8,128)S(1)}, f32[64,128]{1,0:T(8,128)S(1)}, u32[]{:S(2)}, u32[]{:S(2)}) collective-permute-start(f32[64,128]{1,0:T(8,128)S(1)} %relay.1.b0), channel_id=1, source_target_pairs={{0,32},{16,48},{32,0},{48,16},{1,33},{17,49},{33,1},{49,17},{2,34}... | collective-permute-start | bytes 98312 | tf_op jit(solution)/shard_map/ppermute | solution.py:335
  28.0 6.2 %collective-permute-start.1 = (f32[64,128]{1,0:T(8,128)S(1)}, f32[64,128]{1,0:T(8,128)S(1)}, u32[]{:S(2)}, u32[]{:S(2)}) collective-permute-start(f32[64,128]{1,0:T(8,128)S(1)} %relay.1.b0), channel_id=1, source_target_pairs={{0,16},{16,32},{32,48},{48,0},{1,17},{17,33},{33,49},{49,1},{2,18}... | collective-permute-start | bytes 98312 | tf_op jit(solution)/shard_map/ppermute | solution.py:335
  82.0 18.4 %all-to-all-start.3 = ((f32[64,8,128]{2,1,0:T(8,128)}), f32[64,8,128]{2,1,0:T(8,128)S(1)}, u32[]{:S(2)}, u32[]{:S(2)}) async-start(f32[64,8,128]{2,1,0:T(8,128)} %spread.1), calls=%async_computation.3 | async-start | bytes 524288 | tf_op jit(solution)/shard_map/all_to_all | solution.py:341
  91.4 4.0 %collective-permute-start.4 = (f32[64,128]{1,0:T(8,128)S(1)}, f32[64,128]{1,0:T(8,128)S(1)}, u32[]{:S(2)}, u32[]{:S(2)}) collective-permute-start(f32[64,128]{1,0:T(8,128)S(1)} %solve.1.mine), channel_id=1, source_target_pairs={{0,1},{1,0},{2,3},{3,2},{4,5},{5,4},{6,7},{7,6},{8,9},{9,8},{10,11... | collective-permute-start | bytes 98312 | tf_op jit(solution)/shard_map/ppermute | solution.py:343
  102.4 21.1 %copy-start = (f32[16,4,2,16,128]{4,3,2,1,0:T(8,128)S(1)}, f32[16,4,2,16,128]{4,3,2,1,0:T(8,128)}, u32[]{:S(2)}) copy-start(f32[16,4,2,16,128]{4,3,2,1,0:T(8,128)} %merge.1.merged) | copy-start | bytes 3145732

commit v5 on v4

--- a/solution.py
+++ b/solution.py
@@ -245,24 +245,31 @@
     )(recv)
 
 
-def approx_kernel(recv, mine, other, send, basis_out, left_out):
-    x, z, c = lax.axis_index("x"), lax.axis_index("z"), lax.axis_index("c")
+def solutions(mine, other):
+    c = lax.axis_index("c")
+    solved = [jnp.where(c == m, mine[...], other[...]) for m in range(2)]
+    blank = jnp.zeros((32, 32), F32)
+    inverse = jnp.concatenate(
+        [
+            jnp.concatenate([solved[0][:32, 64:96], blank], axis=1),
+            jnp.concatenate([blank, solved[1][:32, 64:96]], axis=1),
+        ],
+        axis=0,
+    )
+    rows = [
+        [solved[m][16 * x : 16 * x + 16, 32 * c : 32 * c + 32] for x, c in LOOP] for m in range(2)
+    ]
+    return inverse, rows
+
+
+def approx_kernel(recv, mine, other, send):
+    inverse, rows = solutions(mine, other)
+    term = jnp.concatenate(
+        [recv[a * NZ : (a + 1) * NZ].reshape(64, LANES) for a in range(8)], axis=1
+    )
+    turned = dot(inverse, term, ((1,), (0,)))
     for m in range(2):
-        solved = jnp.where(c == m, mine[...], other[...])
-        term = jnp.concatenate(
-            [recv[a * NZ + 4 * m : a * NZ + 4 * m + 4].reshape(32, LANES) for a in range(8)], axis=1
-        )
-        turned = dot(solved[:32, 64:96], term, ((1,), (0,)))
-        own = turned[:, :LANES]
-        for a in range(1, 8):
-            own = jnp.where(z == a, turned[:, a * LANES : (a + 1) * LANES], own)
-        basis_out[32 * m : 32 * (m + 1)] = own
-        rows = [solved[16 * at : 16 * at + 16, 32 * core : 32 * core + 32] for at, core in LOOP]
-        left = rows[0]
-        for i, (at, core) in enumerate(LOOP):
-            left = jnp.where((x == at) & (c == core), rows[i], left)
-        left_out[m] = left
-        result = dot(jnp.concatenate(rows, axis=0), turned, ((1,), (0,)))
+        result = dot(jnp.concatenate(rows[m], axis=0), turned[32 * m : 32 * (m + 1)], ((1,), (0,)))
         for i in range(NX * NC):
             send[i, m] = result[16 * i : 16 * i + 16]
 
@@ -271,15 +278,38 @@
     return pl.pallas_call(
         approx_kernel,
         in_specs=[VMEM] * 3,
-        out_specs=[VMEM] * 3,
+        out_specs=VMEM,
+        out_shape=jax.ShapeDtypeStruct((NX * NC, 2, 16, 1024), F32),
+        compiler_params=PARAMS,
+        cost_estimate=cost(2**26, 2**20),
+        name="approx_part",
+    )(recv, mine, other)
+
+
+def outputs_kernel(recv, mine, other, basis_out, left_out):
+    x, z, c = lax.axis_index("x"), lax.axis_index("z"), lax.axis_index("c")
+    inverse, rows = solutions(mine, other)
+    own = recv[pl.ds(z * NZ, NZ)].reshape(64, LANES)
+    basis_out[...] = dot(inverse, own, ((1,), (0,)))
+    for m in range(2):
+        left = rows[m][0]
+        for i, (at, core) in enumerate(LOOP):
+            left = jnp.where((x == at) & (c == core), rows[m][i], left)
+        left_out[m] = left
+
+
+def outputs(recv, mine, other):
+    return pl.pallas_call(
+        outputs_kernel,
+        in_specs=[VMEM] * 3,
+        out_specs=[VMEM] * 2,
         out_shape=[
-            jax.ShapeDtypeStruct((NX * NC, 2, 16, 1024), F32),
             jax.ShapeDtypeStruct((64, LANES), F32),
             jax.ShapeDtypeStruct((2, 16, 32), F32),
         ],
         compiler_params=PARAMS,
-        cost_estimate=cost(2**26, 2**20),
-        name="approx_part",
+        cost_estimate=cost(2**24, 2**19),
+        name="outputs",
     )(recv, mine, other)
 
 
@@ -341,7 +371,8 @@
     gathered = lax.all_to_all(spread(recv), ("y", "z"), 0, 0)
     mine = solve(recv)
     other = lax.ppermute(mine, "c", [(0, 1), (1, 0)])
-    send, new_basis, left_factor = approx_part(gathered, mine, other)
+    send = approx_part(gathered, mine, other)
+    new_basis, left_factor = outputs(gathered, mine, other)
     groups = [[x * NC + c for x, c in LOOP]]
     recv = lax.all_to_all(send, ("x", "c"), 0, 0, axis_index_groups=groups)
     new_basis = new_basis.reshape(2, 32, LANES).transpose(2, 0, 1)

time: 125 us -> 126 us (level)
  blocking collectives: 52.5 us -> 31.4 us
  waiting for transfers between devices: 24.4 us -> 38.5 us
  starting transfers between devices: 36.7 us -> 43.9 us
    all_to_all x1 -> x0, blocking collectives: 21.1 us -> none  [shards(): recv = lax.all_to_all(send, ('x', 'c'), 0, 0, axis_index_groups=groups)]
    all_to_all x0 -> x1, waiting for transfers between devices: none -> 14.1 us  [shards(): recv = lax.all_to_all(send, ('x', 'c'), 0, 0, axis_index_groups=groups)]
    all_to_all x0 -> x1, starting transfers between devices: none -> 7.17 us  [shards(): recv = lax.all_to_all(send, ('x', 'c'), 0, 0, axis_index_groups=groups)]
    pallas_call x1 -> x2, Pallas kernels: 1.96 us -> 3.06 us  [the longest x1 2.21 us: approx_part(): pl.pallas_call(approx_kernel, in_specs=[VMEM] * 3, out_specs=VMEM, out_sh...]
  transfers between devices with their start and end apart: 7 -> 8, of which waited for: 5 -> 6; matrix products, arithmetic and copies ran while one was open for 0% -> 0% of each run, Pallas kernels for 5% -> 5%
where the time goes in v5:
time: 126 us
  starting transfers between devices  43.9 us (35%)
  waiting for transfers between devices  38.5 us (31%)
  blocking collectives  31.4 us (25%)
  Pallas kernels  11.2 us (9%)
    all_to_all x1, blocking collectives, shards(): recv = lax.all_to_all(send, ('x', 'z'), 0, 0)  19 us
    all_to_all x1, waiting for transfers between devices, shards(): recv = lax.all_to_all(merged, ('y', 'c'), 0, 0)  14.9 us
    all_to_all x1, waiting for transfers between devices, shards(): recv = lax.all_to_all(send, ('x', 'c'), 0, 0, axis_index_groups=groups)  14.1 us
    all_to_all x1, blocking collectives, shards(): recv = lax.all_to_all(send, ('y', 'c'), 0, 0)  12.5 us
    ppermute x1, starting transfers between devices, shards(): held = lax.ppermute(held, ('y', 'z'), transposition())  11.5 us
    ppermute x3, starting transfers between devices, shards(): lax.ppermute(held, 'x', [(i, (i + k) % NX) for i in range(NX)])  9.35 us
    all_to_all x1, starting transfers between devices, shards(): recv = lax.all_to_all(send, ('x', 'c'), 0, 0, axis_index_groups=groups)  7.17 us
    all_to_all x1, starting transfers between devices, shards(): recv = lax.all_to_all(merged, ('y', 'c'), 0, 0)  6.76 us
  transfers between devices with their start and end apart: 8, of which 6 were waited for; matrix products, arithmetic and copies ran while one was open for 0% of the time, Pallas kernels for 5%

profile of v5, /device:TPU:1, one launch (start us, length us, event | category | flops | bytes accessed | tf_op | source)
XLA Modules:
  0.0 125.8 jit_solution(9462732685431065725)
XLA Ops:
  0.6 11.5 %collective-permute-start = (f32[64,128]{1,0:T(8,128)}, f32[64,128]{1,0:T(8,128)S(1)}, u32[]{:S(2)}, u32[]{:S(2)}) collective-permute-start(f32[64,128]{1,0:T(8,128)} %bitcast.6), channel_id=1, source_target_pairs={{256,0},{192,2},{128,4},{64,6},{0,8},{448,10},{384,12},{320,14},{3... | collective-permute-start | bytes 98312 | tf_op jit(solution)/shard_map/ppermute | solution.py:360
  12.1 2.2 %merge.1.merged = f32[16,4,2,16,128]{4,3,2,1,0:T(8,128)} custom-call(bf16[1,2,16,8192]{3,2,1,0:T(8,128)(2,1)} %grads.1, f32[1,2,16,8192]{3,2,1,0:T(8,128)} %errors.1), custom_call_target="tpu_custom_call" | custom-call | flops 524288 | bytes 2621440 | tf_op jit(solution)/shard_map/merge/pallas_call | solution.py:55
  14.3 6.8 %all-to-all-start = ((f32[16,4,2,16,128]{4,3,2,1,0:T(8,128)}), f32[16,4,2,16,128]{4,3,2,1,0:T(8,128)S(1)}, u32[]{:S(2)}, u32[]{:S(2)}) async-start(f32[16,4,2,16,128]{4,3,2,1,0:T(8,128)} %merge.1.merged), calls=%async_computation | async-start | bytes 2097152 | tf_op jit(solution)/shard_map/all_to_all | solution.py:363
  21.1 0.0 collective-permute-done.block
  21.1 4.4 %collective-permute-start.3 = (f32[64,128]{1,0:T(8,128)S(1)}, f32[64,128]{1,0:T(8,128)S(1)}, u32[]{:S(2)}, u32[]{:S(2)}) collective-permute-start(f32[64,128]{1,0:T(8,128)S(1)} %relay.1.b0), channel_id=1, source_target_pairs={{0,48},{16,0},{32,16},{48,32},{1,49},{17,1},{33,17},{49,33},{2,50}... | collective-permute-start | bytes 98312 | tf_op jit(solution)/shard_map/ppermute | solution.py:365
  25.5 2.4 %collective-permute-start.2 = (f32[64,128]{1,0:T(8,128)S(1)}, f32[64,128]{1,0:T(8,128)S(1)}, u32[]{:S(2)}, u32[]{:S(2)}) collective-permute-start(f32[64,128]{1,0:T(8,128)S(1)} %relay.1.b0), channel_id=1, source_target_pairs={{0,32},{16,48},{32,0},{48,16},{1,33},{17,49},{33,1},{49,17},{2,34}... | collective-permute-start | bytes 98312 | tf_op jit(solution)/shard_map/ppermute | solution.py:365
  28.0 2.5 %collective-permute-start.1 = (f32[64,128]{1,0:T(8,128)S(1)}, f32[64,128]{1,0:T(8,128)S(1)}, u32[]{:S(2)}, u32[]{:S(2)}) collective-permute-start(f32[64,128]{1,0:T(8,128)S(1)} %relay.1.b0), channel_id=1, source_target_pairs={{0,16},{16,32},{32,48},{48,0},{1,17},{17,33},{33,49},{49,1},{2,18}... | collective-permute-start | bytes 98312 | tf_op jit(solution)/shard_map/ppermute | solution.py:365
  30.5 0.0 collective-permute-done.3.b3
  30.5 1.5 %collective-permute-done.2.b2 = f32[64,128]{1,0:T(8,128)S(1)} collective-permute-done((f32[64,128]{1,0:T(8,128)S(1)}, f32[64,128]{1,0:T(8,128)S(1)}, u32[]{:S(2)}, u32[]{:S(2)}) %collective-permute-start.2) | collective-permute-done | bytes 32800 | tf_op jit(solution)/shard_map/ppermute | solution.py:365
  32.0 2.1 %collective-permute-done.1.b1 = f32[64,128]{1,0:T(8,128)S(1)} collective-permute-done((f32[64,128]{1,0:T(8,128)S(1)}, f32[64,128]{1,0:T(8,128)S(1)}, u32[]{:S(2)}, u32[]{:S(2)}) %collective-permute-start.1) | collective-permute-done | bytes 32800 | tf_op jit(solution)/shard_map/ppermute | solution.py:365
  34.2 14.9 %all-to-all-done.recv = f32[16,4,2,16,128]{4,3,2,1,0:T(8,128)S(1)} async-done(((f32[16,4,2,16,128]{4,3,2,1,0:T(8,128)}), f32[16,4,2,16,128]{4,3,2,1,0:T(8,128)S(1)}, u32[]{:S(2)}, u32[]{:S(2)}) %all-to-all-start) | async-done | bytes 1048608 | tf_op jit(solution)/shard_map/all_to_all | solution.py:363
  49.0 0.4 factor_part.1
  49.4 12.5 %all_to_all.25.recv = f32[16,16,128]{2,1,0:T(8,128)S(1)} all-to-all(f32[16,16,128]{2,1,0:T(8,128)S(1)} %get-tuple-element.7), channel_id=1, replica_groups=mesh['y'=8,'x'=4,'z'=8,'c'=2] {'y','c'}, dimensions={0} | all-to-all | bytes 262144 | tf_op jit(solution)/shard_map/all_to_all | solution.py:368
  61.9 0.4 term_part.1
  62.3 19.0 %all_to_all.26.recv = f32[32,16,128]{2,1,0:T(8,128)S(1)} all-to-all(f32[32,16,128]{2,1,0:T(8,128)S(1)} %term_part.1), channel_id=1, replica_groups=mesh['y'=8,'x'=4,'z'=8,'c'=2] {'x','z'}, dimensions={0} | all-to-all | bytes 524288 | tf_op jit(solution)/shard_map/all_to_all | solution.py:370
  81.3 0.7 spread.1
  82.0 6.0 %all-to-all-start.3 = ((f32[64,8,128]{2,1,0:T(8,128)}), f32[64,8,128]{2,1,0:T(8,128)S(1)}, u32[]{:S(2)}, u32[]{:S(2)}) async-start(f32[64,8,128]{2,1,0:T(8,128)} %spread.1), calls=%async_computation.3 | async-start | bytes 524288 | tf_op jit(solution)/shard_map/all_to_all | solution.py:371
  88.0 3.4 %solve.1.mine = f32[64,128]{1,0:T(8,128)S(1)} custom-call(f32[32,16,128]{2,1,0:T(8,128)S(1)} %all_to_all.26.recv), custom_call_target="tpu_custom_call" | custom-call | flops 16777216 | bytes 524288 | tf_op jit(solution)/shard_map/solve/pallas_call | solution.py:237
  91.4 3.2 %collective-permute-start.4 = (f32[64,128]{1,0:T(8,128)S(1)}, f32[64,128]{1,0:T(8,128)S(1)}, u32[]{:S(2)}, u32[]{:S(2)}) collective-permute-start(f32[64,128]{1,0:T(8,128)S(1)} %solve.1.mine), channel_id=1, source_target_pairs={{0,1},{1,0},{2,3},{3,2},{4,5},{5,4},{6,7},{7,6},{8,9},{9,8},{10,11... | collective-permute-start | bytes 98312 | tf_op jit(solution)/shard_map/ppermute | solution.py:373
  94.6 0.8 collective-permute-done.4.other
  95.4 5.0 %all-to-all-done.3.recv = f32[64,8,128]{2,1,0:T(8,128)S(1)} async-done(((f32[64,8,128]{2,1,0:T(8,128)}), f32[64,8,128]{2,1,0:T(8,128)S(1)}, u32[]{:S(2)}, u32[]{:S(2)}) %all-to-all-start.3) | async-done | bytes 262176 | tf_op jit(solution)/shard_map/all_to_all | solution.py:371
  100.4 2.2 %approx_part.1 = f32[8,2,16,1024]{3,2,1,0:T(8,128)} custom-call(f32[64,8,128]{2,1,0:T(8,128)S(1)} %all-to-all-done.3.recv, f32[64,128]{1,0:T(8,128)S(1)} %solve.1.mine, f32[64,128]{1,0:T(8,128)S(1)} %collective-permute-done.4.other), custom_call_target="tpu_custom_call" | custom-call | flops 67108864 | bytes 1048576 | tf_op jit(solution)/shard_map/approx_part/pallas_call | solution.py:278
  102.7 0.0 copy-start
  102.7 7.2 %all-to-all-start.4 = ((f32[8,2,16,1024]{3,2,1,0:T(8,128)}), f32[8,2,16,1024]{3,2,1,0:T(8,128)S(1)}, u32[]{:S(2)}, u32[]{:S(2)}) async-start(f32[8,2,16,1024]{3,2,1,0:T(8,128)} %approx_part.1), calls=%async_computation.4 | async-start | bytes 2097152 | tf_op jit(solution)/shard_map/all_to_all | solution.py:377
  109.8 0.8 outputs.1
  110.7 14.1 %all-to-all-done.4.recv = f32[8,2,16,1024]{3,2,1,0:T(8,128)S(1)} async-done(((f32[8,2,16,1024]{3,2,1,0:T(8,128)}), f32[8,2,16,1024]{3,2,1,0:T(8,128)S(1)}, u32[]{:S(2)}, u32[]{:S(2)}) %all-to-all-start.4) | async-done | bytes 1048608 | tf_op jit(solution)/shard_map/all_to_all | solution.py:377
  124.8 0.0 copy-done
  124.8 1.0 subtract.1
  (2 shorter events, 0.0 us)
Async XLA Ops:
  0.6 20.5 %collective-permute-start = (f32[64,128]{1,0:T(8,128)}, f32[64,128]{1,0:T(8,128)S(1)}, u32[]{:S(2)}, u32[]{:S(2)}) collective-permute-start(f32[64,128]{1,0:T(8,128)} %bitcast.6), channel_id=1, source_target_pairs={{256,0},{192,2},{128,4},{64,6},{0,8},{448,10},{384,12},{320,14},{3... | collective-permute-start | bytes 98312 | tf_op jit(solution)/shard_map/ppermute | solution.py:360
  14.3 34.7 %all-to-all-start = ((f32[16,4,2,16,128]{4,3,2,1,0:T(8,128)}), f32[16,4,2,16,128]{4,3,2,1,0:T(8,128)S(1)}, u32[]{:S(2)}, u32[]{:S(2)}) async-start(f32[16,4,2,16,128]{4,3,2,1,0:T(8,128)} %merge.1.merged), calls=%async_computation | async-start | bytes 2097152 | tf_op jit(solution)/shard_map/all_to_all | solution.py:363
  21.1 9.4 %collective-permute-start.3 = (f32[64,128]{1,0:T(8,128)S(1)}, f32[64,128]{1,0:T(8,128)S(1)}, u32[]{:S(2)}, u32[]{:S(2)}) collective-permute-start(f32[64,128]{1,0:T(8,128)S(1)} %relay.1.b0), channel_id=1, source_target_pairs={{0,48},{16,0},{32,16},{48,32},{1,49},{17,1},{33,17},{49,33},{2,50}... | collective-permute-start | bytes 98312 | tf_op jit(solution)/shard_map/ppermute | solution.py:365
  25.5 6.5 %collective-permute-start.2 = (f32[64,128]{1,0:T(8,128)S(1)}, f32[64,128]{1,0:T(8,128)S(1)}, u32[]{:S(2)}, u32[]{:S(2)}) collective-permute-start(f32[64,128]{1,0:T(8,128)S(1)} %relay.1.b0), channel_id=1, source_target_pairs={{0,32},{16,48},{32,0},{48,16},{1,33},{17,49},{33,1},{49,17},{2,34}... | collective-permute-start | bytes 98312 | tf_op jit(solution)/shard_map/ppermute | solution.py:365
  28.0 6.2 %collective-permute-start.1 = (f32[64,128]{1,0:T(8,128)S(1)}, f32[64,128]{1,0:T(8,128)S(1)}, u32[]{:S(2)}, u32[]{:S(2)}) collective-permute-start(f32[64,128]{1,0:T(8,128)S(1)} %relay.1.b0), channel_id=1, source_target_pairs={{0,16},{16,32},{32,48},{48,0},{1,17},{17,33},{33,49},{49,1},{2,18}... | collective-permute-start | bytes 98312 | tf_op jit(solution)/shard_map/ppermute | solution.py:365
  82.0 18.4 %all-to-all-start.3 = ((f32[64,8,128]{2,1,0:T(8,128)}), f32[64,8,128]{2,1,0:T(8,128)S(1)}, u32[]{:S(2)}, u32[]{:S(2)}) async-start(f32[64,8,128]{2,1,0:T(8,128)} %spread.1), calls=%async_computation.3 | async-start | bytes 524288 | tf_op jit(solution)/shard_map/all_to_all | solution.py:371
  91.4 4.0 %collective-permute-start.4 = (f32[64,128]{1,0:T(8,128)S(1)}, f32[64,128]{1,0:T(8,128)S(1)}, u32[]{:S(2)}, u32[]{:S(2)}) collective-permute-start(f32[64,128]{1,0:T(8,128)S(1)} %solve.1.mine), channel_id=1, source_target_pairs={{0,1},{1,0},{2,3},{3,2},{4,5},{5,4},{6,7},{7,6},{8,9},{9,8},{10,11... | collective-permute-start | bytes 98312 | tf_op jit(solution)/shard_map/ppermute | solution.py:373
  102.7 22.1 %copy-start = (f32[16,4,2,16,128]{4,3,2,1,0:T(8,128)S(1)}, f32[16,4,2,16,128]{4,3,2,1,0:T(8,128)}, u32[]{:S(2)}) copy-start(f32[16,4,2,16,128]{4,3,2,1,0:T(8,128)} %merge.1.merged) | copy-start | bytes 3145732
  102.7 22.1 %all-to-all-start.4 = ((f32[8,2,16,1024]{3,2,1,0:T(8,128)}), f32[8,2,16,1024]{3,2,1,0:T(8,128)S(1)}, u32[]{:S(2)}, u32[]{:S(2)}) async-start(f32[8,2,16,1024]{3,2,1,0:T(8,128)} %approx_part.1), calls=%async_computation.4 | async-start | bytes 2097152 | tf_op jit(solution)/shard_map/all_to_all | solution.py:377

commit v6 on v5

--- a/solution.py
+++ b/solution.py
@@ -262,12 +262,17 @@
     return inverse, rows
 
 
-def approx_kernel(recv, mine, other, send):
+def approx_kernel(recv, mine, other, send, basis_out):
+    z = lax.axis_index("z")
     inverse, rows = solutions(mine, other)
     term = jnp.concatenate(
         [recv[a * NZ : (a + 1) * NZ].reshape(64, LANES) for a in range(8)], axis=1
     )
     turned = dot(inverse, term, ((1,), (0,)))
+    own = turned[:, :LANES]
+    for a in range(1, 8):
+        own = jnp.where(z == a, turned[:, a * LANES : (a + 1) * LANES], own)
+    basis_out[...] = own
     for m in range(2):
         result = dot(jnp.concatenate(rows[m], axis=0), turned[32 * m : 32 * (m + 1)], ((1,), (0,)))
         for i in range(NX * NC):
@@ -278,39 +283,37 @@
     return pl.pallas_call(
         approx_kernel,
         in_specs=[VMEM] * 3,
-        out_specs=VMEM,
-        out_shape=jax.ShapeDtypeStruct((NX * NC, 2, 16, 1024), F32),
+        out_specs=[VMEM] * 2,
+        out_shape=[
+            jax.ShapeDtypeStruct((NX * NC, 2, 16, 1024), F32),
+            jax.ShapeDtypeStruct((64, LANES), F32),
+        ],
         compiler_params=PARAMS,
         cost_estimate=cost(2**26, 2**20),
         name="approx_part",
     )(recv, mine, other)
 
 
-def outputs_kernel(recv, mine, other, basis_out, left_out):
-    x, z, c = lax.axis_index("x"), lax.axis_index("z"), lax.axis_index("c")
-    inverse, rows = solutions(mine, other)
-    own = recv[pl.ds(z * NZ, NZ)].reshape(64, LANES)
-    basis_out[...] = dot(inverse, own, ((1,), (0,)))
+def left_kernel(mine, other, out):
+    x, c = lax.axis_index("x"), lax.axis_index("c")
+    _, rows = solutions(mine, other)
     for m in range(2):
         left = rows[m][0]
         for i, (at, core) in enumerate(LOOP):
             left = jnp.where((x == at) & (c == core), rows[m][i], left)
-        left_out[m] = left
-
-
-def outputs(recv, mine, other):
-    return pl.pallas_call(
-        outputs_kernel,
-        in_specs=[VMEM] * 3,
-        out_specs=[VMEM] * 2,
-        out_shape=[
-            jax.ShapeDtypeStruct((64, LANES), F32),
-            jax.ShapeDtypeStruct((2, 16, 32), F32),
-        ],
-        compiler_params=PARAMS,
-        cost_estimate=cost(2**24, 2**19),
-        name="outputs",
-    )(recv, mine, other)
+        out[m] = left
+
+
+def left_part(mine, other):
+    return pl.pallas_call(
+        left_kernel,
+        in_specs=[VMEM] * 2,
+        out_specs=VMEM,
+        out_shape=jax.ShapeDtypeStruct((2, 16, 32), F32),
+        compiler_params=PARAMS,
+        cost_estimate=cost(2**22, 2**17),
+        name="left_part",
+    )(mine, other)
 
 
 def subtract_kernel(merged, recv, out, result, sems):
@@ -371,8 +374,8 @@
     gathered = lax.all_to_all(spread(recv), ("y", "z"), 0, 0)
     mine = solve(recv)
     other = lax.ppermute(mine, "c", [(0, 1), (1, 0)])
-    send = approx_part(gathered, mine, other)
-    new_basis, left_factor = outputs(gathered, mine, other)
+    left_factor, other = lax.optimization_barrier((left_part(mine, other), other))
+    send, new_basis = approx_part(gathered, mine, other)
     groups = [[x * NC + c for x, c in LOOP]]
     recv = lax.all_to_all(send, ("x", "c"), 0, 0, axis_index_groups=groups)
     new_basis = new_basis.reshape(2, 32, LANES).transpose(2, 0, 1)

time: 126 us -> 124 us (0.984)
  blocking collectives: 31.4 us -> 52.5 us
  waiting for transfers between devices: 38.5 us -> 23.6 us
  starting transfers between devices: 43.9 us -> 36.7 us
    all_to_all x0 -> x1, blocking collectives: none -> 21.1 us  [shards(): recv = lax.all_to_all(send, ('x', 'c'), 0, 0, axis_index_groups=groups)]
    all_to_all x1 -> x0, waiting for transfers between devices: 14.1 us -> none  [shards(): recv = lax.all_to_all(send, ('x', 'c'), 0, 0, axis_index_groups=groups)]
    all_to_all x1 -> x0, starting transfers between devices: 7.17 us -> none  [shards(): recv = lax.all_to_all(send, ('x', 'c'), 0, 0, axis_index_groups=groups)]
  transfers between devices with their start and end apart: 8 -> 7, of which waited for: 6 -> 5; matrix products, arithmetic and copies ran while one was open for 0% -> 0% of each run, Pallas kernels for 5% -> 5%
where the time goes in v6:
time: 124 us
  blocking collectives  52.5 us (42%)
  starting transfers between devices  36.7 us (30%)
  waiting for transfers between devices  23.6 us (19%)
  Pallas kernels  10.2 us (8%)
    all_to_all x1, blocking collectives, shards(): recv = lax.all_to_all(send, ('x', 'c'), 0, 0, axis_index_groups=groups)  21.1 us
    all_to_all x1, blocking collectives, shards(): recv = lax.all_to_all(send, ('x', 'z'), 0, 0)  19 us
    all_to_all x1, waiting for transfers between devices, shards(): recv = lax.all_to_all(merged, ('y', 'c'), 0, 0)  14.9 us
    all_to_all x1, blocking collectives, shards(): recv = lax.all_to_all(send, ('y', 'c'), 0, 0)  12.5 us
    ppermute x1, starting transfers between devices, shards(): held = lax.ppermute(held, ('y', 'z'), transposition())  11.5 us
    ppermute x3, starting transfers between devices, shards(): lax.ppermute(held, 'x', [(i, (i + k) % NX) for i in range(NX)])  9.35 us
    all_to_all x1, starting transfers between devices, shards(): recv = lax.all_to_all(merged, ('y', 'c'), 0, 0)  6.76 us
    all_to_all x1, starting transfers between devices, shards(): gathered = lax.all_to_all(spread(recv), ('y', 'z'), 0, 0)  5.99 us
  transfers between devices with their start and end apart: 7, of which 5 were waited for; matrix products, arithmetic and copies ran while one was open for 0% of the time, Pallas kernels for 5%

profile of v6, /device:TPU:1, one launch (start us, length us, event | category | flops | bytes accessed | tf_op | source)
XLA Modules:
  0.0 123.9 jit_solution(14041034350349446178)
XLA Ops:
  0.6 11.5 %collective-permute-start = (f32[64,128]{1,0:T(8,128)}, f32[64,128]{1,0:T(8,128)S(1)}, u32[]{:S(2)}, u32[]{:S(2)}) collective-permute-start(f32[64,128]{1,0:T(8,128)} %bitcast.6), channel_id=1, source_target_pairs={{256,0},{192,2},{128,4},{64,6},{0,8},{448,10},{384,12},{320,14},{3... | collective-permute-start | bytes 98312 | tf_op jit(solution)/shard_map/ppermute | solution.py:363
  12.1 2.2 %merge.1.merged = f32[16,4,2,16,128]{4,3,2,1,0:T(8,128)} custom-call(bf16[1,2,16,8192]{3,2,1,0:T(8,128)(2,1)} %grads.1, f32[1,2,16,8192]{3,2,1,0:T(8,128)} %errors.1), custom_call_target="tpu_custom_call" | custom-call | flops 524288 | bytes 2621440 | tf_op jit(solution)/shard_map/merge/pallas_call | solution.py:55
  14.3 6.8 %all-to-all-start = ((f32[16,4,2,16,128]{4,3,2,1,0:T(8,128)}), f32[16,4,2,16,128]{4,3,2,1,0:T(8,128)S(1)}, u32[]{:S(2)}, u32[]{:S(2)}) async-start(f32[16,4,2,16,128]{4,3,2,1,0:T(8,128)} %merge.1.merged), calls=%async_computation | async-start | bytes 2097152 | tf_op jit(solution)/shard_map/all_to_all | solution.py:366
  21.1 0.0 collective-permute-done.block
  21.1 4.4 %collective-permute-start.3 = (f32[64,128]{1,0:T(8,128)S(1)}, f32[64,128]{1,0:T(8,128)S(1)}, u32[]{:S(2)}, u32[]{:S(2)}) collective-permute-start(f32[64,128]{1,0:T(8,128)S(1)} %relay.1.b0), channel_id=1, source_target_pairs={{0,48},{16,0},{32,16},{48,32},{1,49},{17,1},{33,17},{49,33},{2,50}... | collective-permute-start | bytes 98312 | tf_op jit(solution)/shard_map/ppermute | solution.py:368
  25.5 2.4 %collective-permute-start.2 = (f32[64,128]{1,0:T(8,128)S(1)}, f32[64,128]{1,0:T(8,128)S(1)}, u32[]{:S(2)}, u32[]{:S(2)}) collective-permute-start(f32[64,128]{1,0:T(8,128)S(1)} %relay.1.b0), channel_id=1, source_target_pairs={{0,32},{16,48},{32,0},{48,16},{1,33},{17,49},{33,1},{49,17},{2,34}... | collective-permute-start | bytes 98312 | tf_op jit(solution)/shard_map/ppermute | solution.py:368
  28.0 2.5 %collective-permute-start.1 = (f32[64,128]{1,0:T(8,128)S(1)}, f32[64,128]{1,0:T(8,128)S(1)}, u32[]{:S(2)}, u32[]{:S(2)}) collective-permute-start(f32[64,128]{1,0:T(8,128)S(1)} %relay.1.b0), channel_id=1, source_target_pairs={{0,16},{16,32},{32,48},{48,0},{1,17},{17,33},{33,49},{49,1},{2,18}... | collective-permute-start | bytes 98312 | tf_op jit(solution)/shard_map/ppermute | solution.py:368
  30.5 0.0 collective-permute-done.3.b3
  30.5 1.5 %collective-permute-done.2.b2 = f32[64,128]{1,0:T(8,128)S(1)} collective-permute-done((f32[64,128]{1,0:T(8,128)S(1)}, f32[64,128]{1,0:T(8,128)S(1)}, u32[]{:S(2)}, u32[]{:S(2)}) %collective-permute-start.2) | collective-permute-done | bytes 32800 | tf_op jit(solution)/shard_map/ppermute | solution.py:368
  32.0 2.1 %collective-permute-done.1.b1 = f32[64,128]{1,0:T(8,128)S(1)} collective-permute-done((f32[64,128]{1,0:T(8,128)S(1)}, f32[64,128]{1,0:T(8,128)S(1)}, u32[]{:S(2)}, u32[]{:S(2)}) %collective-permute-start.1) | collective-permute-done | bytes 32800 | tf_op jit(solution)/shard_map/ppermute | solution.py:368
  34.2 14.9 %all-to-all-done.recv = f32[16,4,2,16,128]{4,3,2,1,0:T(8,128)S(1)} async-done(((f32[16,4,2,16,128]{4,3,2,1,0:T(8,128)}), f32[16,4,2,16,128]{4,3,2,1,0:T(8,128)S(1)}, u32[]{:S(2)}, u32[]{:S(2)}) %all-to-all-start) | async-done | bytes 1048608 | tf_op jit(solution)/shard_map/all_to_all | solution.py:366
  49.0 0.4 factor_part.1
  49.4 12.5 %all_to_all.25.recv = f32[16,16,128]{2,1,0:T(8,128)S(1)} all-to-all(f32[16,16,128]{2,1,0:T(8,128)S(1)} %get-tuple-element.9), channel_id=1, replica_groups=mesh['y'=8,'x'=4,'z'=8,'c'=2] {'y','c'}, dimensions={0} | all-to-all | bytes 262144 | tf_op jit(solution)/shard_map/all_to_all | solution.py:371
  61.9 0.4 term_part.1
  62.3 19.0 %all_to_all.26.recv = f32[32,16,128]{2,1,0:T(8,128)S(1)} all-to-all(f32[32,16,128]{2,1,0:T(8,128)S(1)} %term_part.1), channel_id=1, replica_groups=mesh['y'=8,'x'=4,'z'=8,'c'=2] {'x','z'}, dimensions={0} | all-to-all | bytes 524288 | tf_op jit(solution)/shard_map/all_to_all | solution.py:373
  81.3 0.8 spread.1
  82.0 6.0 %all-to-all-start.3 = ((f32[64,8,128]{2,1,0:T(8,128)}), f32[64,8,128]{2,1,0:T(8,128)S(1)}, u32[]{:S(2)}, u32[]{:S(2)}) async-start(f32[64,8,128]{2,1,0:T(8,128)} %spread.1), calls=%async_computation.3 | async-start | bytes 524288 | tf_op jit(solution)/shard_map/all_to_all | solution.py:374
  88.0 3.4 %solve.1.mine = f32[64,128]{1,0:T(8,128)S(1)} custom-call(f32[32,16,128]{2,1,0:T(8,128)S(1)} %all_to_all.26.recv), custom_call_target="tpu_custom_call" | custom-call | flops 16777216 | bytes 524288 | tf_op jit(solution)/shard_map/solve/pallas_call | solution.py:237
  91.4 3.2 %collective-permute-start.4 = (f32[64,128]{1,0:T(8,128)S(1)}, f32[64,128]{1,0:T(8,128)S(1)}, u32[]{:S(2)}, u32[]{:S(2)}) collective-permute-start(f32[64,128]{1,0:T(8,128)S(1)} %solve.1.mine), channel_id=1, source_target_pairs={{0,1},{1,0},{2,3},{3,2},{4,5},{5,4},{6,7},{7,6},{8,9},{9,8},{10,11... | collective-permute-start | bytes 98312 | tf_op jit(solution)/shard_map/ppermute | solution.py:376
  94.6 0.8 collective-permute-done.4.other
  95.4 0.8 left_part.1
  96.2 4.3 %all-to-all-done.3.recv = f32[64,8,128]{2,1,0:T(8,128)S(1)} async-done(((f32[64,8,128]{2,1,0:T(8,128)}), f32[64,8,128]{2,1,0:T(8,128)S(1)}, u32[]{:S(2)}, u32[]{:S(2)}) %all-to-all-start.3) | async-done | bytes 262176 | tf_op jit(solution)/shard_map/all_to_all | solution.py:374
  100.5 1.3 %approx_part.1 = (f32[8,2,16,1024]{3,2,1,0:T(8,128)S(1)}, f32[64,128]{1,0:T(8,128)}) custom-call(f32[64,8,128]{2,1,0:T(8,128)S(1)} %all-to-all-done.3.recv, f32[64,128]{1,0:T(8,128)S(1)} %solve.1.mine, f32[64,128]{1,0:T(8,128)S(1)} %collective-permute-done.4.other), custom_call_target="tpu_custom_call" | custom-call | flops 67108864 | bytes 1048576 | tf_op jit(solution)/shard_map/approx_part/pallas_call | solution.py:283
  101.7 0.0 copy-start
  101.7 21.1 %all_to_all.27.recv = f32[8,2,16,1024]{3,2,1,0:T(8,128)S(1)} all-to-all(f32[8,2,16,1024]{3,2,1,0:T(8,128)S(1)} %get-tuple-element.12), channel_id=1, replica_groups={{0,16,32,48,49,33,17,1},{2,18,34,50,51,35,19,3},{4,20,36,52,53,37,21,5}..., dimensions={0} | all-to-all | bytes 2097152 | tf_op jit(solution)/shard_map/all_to_all | solution.py:380
  122.8 0.0 copy-done
  122.8 1.0 subtract.1
  (2 shorter events, 0.0 us)
Async XLA Ops:
  0.6 20.5 %collective-permute-start = (f32[64,128]{1,0:T(8,128)}, f32[64,128]{1,0:T(8,128)S(1)}, u32[]{:S(2)}, u32[]{:S(2)}) collective-permute-start(f32[64,128]{1,0:T(8,128)} %bitcast.6), channel_id=1, source_target_pairs={{256,0},{192,2},{128,4},{64,6},{0,8},{448,10},{384,12},{320,14},{3... | collective-permute-start | bytes 98312 | tf_op jit(solution)/shard_map/ppermute | solution.py:363
  14.3 34.7 %all-to-all-start = ((f32[16,4,2,16,128]{4,3,2,1,0:T(8,128)}), f32[16,4,2,16,128]{4,3,2,1,0:T(8,128)S(1)}, u32[]{:S(2)}, u32[]{:S(2)}) async-start(f32[16,4,2,16,128]{4,3,2,1,0:T(8,128)} %merge.1.merged), calls=%async_computation | async-start | bytes 2097152 | tf_op jit(solution)/shard_map/all_to_all | solution.py:366
  21.1 9.4 %collective-permute-start.3 = (f32[64,128]{1,0:T(8,128)S(1)}, f32[64,128]{1,0:T(8,128)S(1)}, u32[]{:S(2)}, u32[]{:S(2)}) collective-permute-start(f32[64,128]{1,0:T(8,128)S(1)} %relay.1.b0), channel_id=1, source_target_pairs={{0,48},{16,0},{32,16},{48,32},{1,49},{17,1},{33,17},{49,33},{2,50}... | collective-permute-start | bytes 98312 | tf_op jit(solution)/shard_map/ppermute | solution.py:368
  25.5 6.5 %collective-permute-start.2 = (f32[64,128]{1,0:T(8,128)S(1)}, f32[64,128]{1,0:T(8,128)S(1)}, u32[]{:S(2)}, u32[]{:S(2)}) collective-permute-start(f32[64,128]{1,0:T(8,128)S(1)} %relay.1.b0), channel_id=1, source_target_pairs={{0,32},{16,48},{32,0},{48,16},{1,33},{17,49},{33,1},{49,17},{2,34}... | collective-permute-start | bytes 98312 | tf_op jit(solution)/shard_map/ppermute | solution.py:368
  28.0 6.2 %collective-permute-start.1 = (f32[64,128]{1,0:T(8,128)S(1)}, f32[64,128]{1,0:T(8,128)S(1)}, u32[]{:S(2)}, u32[]{:S(2)}) collective-permute-start(f32[64,128]{1,0:T(8,128)S(1)} %relay.1.b0), channel_id=1, source_target_pairs={{0,16},{16,32},{32,48},{48,0},{1,17},{17,33},{33,49},{49,1},{2,18}... | collective-permute-start | bytes 98312 | tf_op jit(solution)/shard_map/ppermute | solution.py:368
  82.0 18.4 %all-to-all-start.3 = ((f32[64,8,128]{2,1,0:T(8,128)}), f32[64,8,128]{2,1,0:T(8,128)S(1)}, u32[]{:S(2)}, u32[]{:S(2)}) async-start(f32[64,8,128]{2,1,0:T(8,128)} %spread.1), calls=%async_computation.3 | async-start | bytes 524288 | tf_op jit(solution)/shard_map/all_to_all | solution.py:374
  91.4 4.0 %collective-permute-start.4 = (f32[64,128]{1,0:T(8,128)S(1)}, f32[64,128]{1,0:T(8,128)S(1)}, u32[]{:S(2)}, u32[]{:S(2)}) collective-permute-start(f32[64,128]{1,0:T(8,128)S(1)} %solve.1.mine), channel_id=1, source_target_pairs={{0,1},{1,0},{2,3},{3,2},{4,5},{5,4},{6,7},{7,6},{8,9},{9,8},{10,11... | collective-permute-start | bytes 98312 | tf_op jit(solution)/shard_map/ppermute | solution.py:376
  101.7 21.1 %copy-start = (f32[16,4,2,16,128]{4,3,2,1,0:T(8,128)S(1)}, f32[16,4,2,16,128]{4,3,2,1,0:T(8,128)}, u32[]{:S(2)}) copy-start(f32[16,4,2,16,128]{4,3,2,1,0:T(8,128)} %merge.1.merged) | copy-start | bytes 3145732

commit v7 on v6

--- a/solution.py
+++ b/solution.py
@@ -82,6 +82,22 @@
         cost_estimate=cost(2**35, 2**16),
         name="relay",
     )(block)
+
+
+def both_kernel(a, b, out):
+    out[...] = a[...] + b[...]
+
+
+def both(a, b):
+    return pl.pallas_call(
+        both_kernel,
+        in_specs=[VMEM] * 2,
+        out_specs=VMEM,
+        out_shape=jax.ShapeDtypeStruct(a.shape, F32),
+        compiler_params=PARAMS,
+        cost_estimate=cost(2**13, 2**17),
+        name="both",
+    )(a, b)
 
 
 def arrange_kernel(b0, b1, b2, b3, out):
@@ -349,19 +365,19 @@
     )(merged, recv)
 
 
-def transposition():
-    far = {0: 4, 1: 3, 2: 2, 3: 1, 4: 0, 5: 7, 6: 6, 7: 5}
+def near_pairs():
     pairs = []
     for a in range(8):
-        for d in range(NZ):
-            pairs.append((((a + far[d]) % 8) * NZ + a, a * NZ + (a + d) % NZ))
+        for dy, dz in ((0, -2), (1, -1), (2, 0), (-1, 1)):
+            pairs.append(((a + dy) % 8 * NZ + a, a * NZ + (a + dz) % NZ))
     return pairs
 
 
 def shards(grads, errors, basis):
     held = basis.transpose(1, 2, 0).reshape(64, LANES)
-    held = lax.ppermute(held, ("y", "z"), transposition())
+    held = lax.ppermute(held, ("y", "z"), near_pairs())
     held = relay(held)
+    held = both(held, lax.ppermute(held, "z", [(z, (z + 4) % NZ) for z in range(NZ)]))
     merged = merge(grads, errors)
     recv = lax.all_to_all(merged, ("y", "c"), 0, 0)
     parts = [held] + [

time: 124 us -> 123 us (level)
  waiting for transfers between devices: 23.6 us -> 16.9 us
  starting transfers between devices: 36.7 us -> 41.2 us
    all_to_all x1, waiting for transfers between devices: 14.9 us -> 6.2 us  [shards(): recv = lax.all_to_all(merged, ('y', 'c'), 0, 0)]
    ppermute x1 -> x2, starting transfers between devices: 11.5 us -> 18.3 us  [the longest x1 11.5 us: shards(): held = lax.ppermute(held, ('y', 'z'), near_pairs())]
    all_to_all x1, starting transfers between devices: 6.76 us -> 4.41 us  [shards(): recv = lax.all_to_all(merged, ('y', 'c'), 0, 0)]
    ppermute x1 -> x2, waiting for transfers between devices: 0.01 us -> 1.79 us  [the longest x1 1.78 us: shards(): lax.ppermute(held, 'z', [(z, (z + 4) % NZ) for z in range(NZ)])]
  transfers between devices with their start and end apart: 7 -> 8, of which waited for: 5 -> 6; matrix products, arithmetic and copies ran while one was open for 0% -> 0% of each run, Pallas kernels for 5% -> 5%
where the time goes in v7:
time: 123 us; the launch traced here: 122 us
  blocking collectives  53.1 us (43%)
  starting transfers between devices  41.2 us (33%)
  waiting for transfers between devices  16.9 us (14%)
  Pallas kernels  10.2 us (8%)
    all_to_all x1, blocking collectives, shards(): recv = lax.all_to_all(send, ('x', 'c'), 0, 0, axis_index_groups=groups)  21.1 us
    all_to_all x1, blocking collectives, shards(): recv = lax.all_to_all(send, ('x', 'z'), 0, 0)  19.5 us
    all_to_all x1, blocking collectives, shards(): recv = lax.all_to_all(send, ('y', 'c'), 0, 0)  12.5 us
    ppermute x1, starting transfers between devices, shards(): held = lax.ppermute(held, ('y', 'z'), near_pairs())  11.5 us
    ppermute x3, starting transfers between devices, shards(): lax.ppermute(held, 'x', [(i, (i + k) % NX) for i in range(NX)])  9.32 us
    ppermute x1, starting transfers between devices, shards(): lax.ppermute(held, 'z', [(z, (z + 4) % NZ) for z in range(NZ)])  6.77 us
    all_to_all x1, waiting for transfers between devices, shards(): recv = lax.all_to_all(merged, ('y', 'c'), 0, 0)  6.2 us
    all_to_all x1, starting transfers between devices, shards(): gathered = lax.all_to_all(spread(recv), ('y', 'z'), 0, 0)  5.99 us
  transfers between devices with their start and end apart: 8, of which 6 were waited for; matrix products, arithmetic and copies ran while one was open for 0% of the time, Pallas kernels for 5%

profile of v7, /device:TPU:1, one launch (start us, length us, event | category | flops | bytes accessed | tf_op | source)
XLA Modules:
  0.0 122.2 jit_solution(15627822367930225337)
XLA Ops:
  0.6 11.5 %collective-permute-start = (f32[64,128]{1,0:T(8,128)}, f32[64,128]{1,0:T(8,128)S(1)}, u32[]{:S(2)}, u32[]{:S(2)}) collective-permute-start(f32[64,128]{1,0:T(8,128)} %bitcast.6), channel_id=1, source_target_pairs={{0,12},{64,14},{128,0},{448,2},{66,78},{130,64},{194,66},{2,68},{1... | collective-permute-start | bytes 98312 | tf_op jit(solution)/shard_map/ppermute | solution.py:378
  12.1 2.2 %merge.1.merged = f32[16,4,2,16,128]{4,3,2,1,0:T(8,128)} custom-call(bf16[1,2,16,8192]{3,2,1,0:T(8,128)(2,1)} %grads.1, f32[1,2,16,8192]{3,2,1,0:T(8,128)} %errors.1), custom_call_target="tpu_custom_call" | custom-call | flops 524288 | bytes 2621440 | tf_op jit(solution)/shard_map/merge/pallas_call | solution.py:55
  14.4 4.4 %all-to-all-start = ((f32[16,4,2,16,128]{4,3,2,1,0:T(8,128)}), f32[16,4,2,16,128]{4,3,2,1,0:T(8,128)S(1)}, u32[]{:S(2)}, u32[]{:S(2)}) async-start(f32[16,4,2,16,128]{4,3,2,1,0:T(8,128)} %merge.1.merged), calls=%async_computation | async-start | bytes 2097152 | tf_op jit(solution)/shard_map/all_to_all | solution.py:382
  18.8 0.0 collective-permute-done.block
  18.8 6.8 %collective-permute-start.1 = (f32[64,128]{1,0:T(8,128)S(1)}, f32[64,128]{1,0:T(8,128)S(1)}, u32[]{:S(2)}, u32[]{:S(2)}) collective-permute-start(f32[64,128]{1,0:T(8,128)S(1)} %relay.1.a), channel_id=1, source_target_pairs={{0,8},{2,10},{4,12},{6,14},{8,0},{10,2},{12,4},{14,6},{1,9},{3,11}... | collective-permute-start | bytes 98312 | tf_op jit(solution)/shard_map/ppermute | solution.py:380
  25.6 1.8 %collective-permute-done.1.b = f32[64,128]{1,0:T(8,128)S(1)} collective-permute-done((f32[64,128]{1,0:T(8,128)S(1)}, f32[64,128]{1,0:T(8,128)S(1)}, u32[]{:S(2)}, u32[]{:S(2)}) %collective-permute-start.1) | collective-permute-done | bytes 32800 | tf_op jit(solution)/shard_map/ppermute | solution.py:380
  27.4 4.4 %collective-permute-start.4 = (f32[64,128]{1,0:T(8,128)S(1)}, f32[64,128]{1,0:T(8,128)S(1)}, u32[]{:S(2)}, u32[]{:S(2)}) collective-permute-start(f32[64,128]{1,0:T(8,128)S(1)} %both.1.b0), channel_id=1, source_target_pairs={{0,48},{16,0},{32,16},{48,32},{1,49},{17,1},{33,17},{49,33},{2,50}... | collective-permute-start | bytes 98312 | tf_op jit(solution)/shard_map/ppermute | solution.py:384
  31.7 2.4 %collective-permute-start.3 = (f32[64,128]{1,0:T(8,128)S(1)}, f32[64,128]{1,0:T(8,128)S(1)}, u32[]{:S(2)}, u32[]{:S(2)}) collective-permute-start(f32[64,128]{1,0:T(8,128)S(1)} %both.1.b0), channel_id=1, source_target_pairs={{0,32},{16,48},{32,0},{48,16},{1,33},{17,49},{33,1},{49,17},{2,34}... | collective-permute-start | bytes 98312 | tf_op jit(solution)/shard_map/ppermute | solution.py:384
  34.2 2.5 %collective-permute-start.2 = (f32[64,128]{1,0:T(8,128)S(1)}, f32[64,128]{1,0:T(8,128)S(1)}, u32[]{:S(2)}, u32[]{:S(2)}) collective-permute-start(f32[64,128]{1,0:T(8,128)S(1)} %both.1.b0), channel_id=1, source_target_pairs={{0,16},{16,32},{32,48},{48,0},{1,17},{17,33},{33,49},{49,1},{2,18}... | collective-permute-start | bytes 98312 | tf_op jit(solution)/shard_map/ppermute | solution.py:384
  36.7 0.0 collective-permute-done.4.b3
  36.7 1.5 %collective-permute-done.3.b2 = f32[64,128]{1,0:T(8,128)S(1)} collective-permute-done((f32[64,128]{1,0:T(8,128)S(1)}, f32[64,128]{1,0:T(8,128)S(1)}, u32[]{:S(2)}, u32[]{:S(2)}) %collective-permute-start.3) | collective-permute-done | bytes 32800 | tf_op jit(solution)/shard_map/ppermute | solution.py:384
  38.2 2.3 %collective-permute-done.2.b1 = f32[64,128]{1,0:T(8,128)S(1)} collective-permute-done((f32[64,128]{1,0:T(8,128)S(1)}, f32[64,128]{1,0:T(8,128)S(1)}, u32[]{:S(2)}, u32[]{:S(2)}) %collective-permute-start.2) | collective-permute-done | bytes 32800 | tf_op jit(solution)/shard_map/ppermute | solution.py:384
  40.6 6.2 %all-to-all-done.recv = f32[16,4,2,16,128]{4,3,2,1,0:T(8,128)S(1)} async-done(((f32[16,4,2,16,128]{4,3,2,1,0:T(8,128)}), f32[16,4,2,16,128]{4,3,2,1,0:T(8,128)S(1)}, u32[]{:S(2)}, u32[]{:S(2)}) %all-to-all-start) | async-done | bytes 1048608 | tf_op jit(solution)/shard_map/all_to_all | solution.py:382
  46.8 0.4 factor_part.1
  47.2 12.5 %all_to_all.25.recv = f32[16,16,128]{2,1,0:T(8,128)S(1)} all-to-all(f32[16,16,128]{2,1,0:T(8,128)S(1)} %get-tuple-element.9), channel_id=1, replica_groups=mesh['y'=8,'x'=4,'z'=8,'c'=2] {'y','c'}, dimensions={0} | all-to-all | bytes 262144 | tf_op jit(solution)/shard_map/all_to_all | solution.py:387
  59.6 0.4 term_part.1
  60.0 19.5 %all_to_all.26.recv = f32[32,16,128]{2,1,0:T(8,128)S(1)} all-to-all(f32[32,16,128]{2,1,0:T(8,128)S(1)} %term_part.1), channel_id=1, replica_groups=mesh['y'=8,'x'=4,'z'=8,'c'=2] {'x','z'}, dimensions={0} | all-to-all | bytes 524288 | tf_op jit(solution)/shard_map/all_to_all | solution.py:389
  79.6 0.8 spread.1
  80.3 6.0 %all-to-all-start.3 = ((f32[64,8,128]{2,1,0:T(8,128)}), f32[64,8,128]{2,1,0:T(8,128)S(1)}, u32[]{:S(2)}, u32[]{:S(2)}) async-start(f32[64,8,128]{2,1,0:T(8,128)} %spread.1), calls=%async_computation.3 | async-start | bytes 524288 | tf_op jit(solution)/shard_map/all_to_all | solution.py:390
  86.3 3.4 %solve.1.mine = f32[64,128]{1,0:T(8,128)S(1)} custom-call(f32[32,16,128]{2,1,0:T(8,128)S(1)} %all_to_all.26.recv), custom_call_target="tpu_custom_call" | custom-call | flops 16777216 | bytes 524288 | tf_op jit(solution)/shard_map/solve/pallas_call | solution.py:253
  89.7 3.2 %collective-permute-start.5 = (f32[64,128]{1,0:T(8,128)S(1)}, f32[64,128]{1,0:T(8,128)S(1)}, u32[]{:S(2)}, u32[]{:S(2)}) collective-permute-start(f32[64,128]{1,0:T(8,128)S(1)} %solve.1.mine), channel_id=1, source_target_pairs={{0,1},{1,0},{2,3},{3,2},{4,5},{5,4},{6,7},{7,6},{8,9},{9,8},{10,11... | collective-permute-start | bytes 98312 | tf_op jit(solution)/shard_map/ppermute | solution.py:392
  92.9 0.8 collective-permute-done.5.other
  93.7 0.8 left_part.1
  94.5 4.3 %all-to-all-done.3.recv = f32[64,8,128]{2,1,0:T(8,128)S(1)} async-done(((f32[64,8,128]{2,1,0:T(8,128)}), f32[64,8,128]{2,1,0:T(8,128)S(1)}, u32[]{:S(2)}, u32[]{:S(2)}) %all-to-all-start.3) | async-done | bytes 262176 | tf_op jit(solution)/shard_map/all_to_all | solution.py:390
  98.8 1.3 %approx_part.1 = (f32[8,2,16,1024]{3,2,1,0:T(8,128)S(1)}, f32[64,128]{1,0:T(8,128)}) custom-call(f32[64,8,128]{2,1,0:T(8,128)S(1)} %all-to-all-done.3.recv, f32[64,128]{1,0:T(8,128)S(1)} %solve.1.mine, f32[64,128]{1,0:T(8,128)S(1)} %collective-permute-done.5.other), custom_call_target="tpu_custom_call" | custom-call | flops 67108864 | bytes 1048576 | tf_op jit(solution)/shard_map/approx_part/pallas_call | solution.py:299
  100.0 0.0 copy-start
  100.0 21.1 %all_to_all.27.recv = f32[8,2,16,1024]{3,2,1,0:T(8,128)S(1)} all-to-all(f32[8,2,16,1024]{3,2,1,0:T(8,128)S(1)} %get-tuple-element.12), channel_id=1, replica_groups={{0,16,32,48,49,33,17,1},{2,18,34,50,51,35,19,3},{4,20,36,52,53,37,21,5}..., dimensions={0} | all-to-all | bytes 2097152 | tf_op jit(solution)/shard_map/all_to_all | solution.py:396
  121.1 0.0 copy-done
  121.1 1.0 subtract.1
  (3 shorter events, 0.0 us)
Async XLA Ops:
  0.6 18.1 %collective-permute-start = (f32[64,128]{1,0:T(8,128)}, f32[64,128]{1,0:T(8,128)S(1)}, u32[]{:S(2)}, u32[]{:S(2)}) collective-permute-start(f32[64,128]{1,0:T(8,128)} %bitcast.6), channel_id=1, source_target_pairs={{0,12},{64,14},{128,0},{448,2},{66,78},{130,64},{194,66},{2,68},{1... | collective-permute-start | bytes 98312 | tf_op jit(solution)/shard_map/ppermute | solution.py:378
  14.4 32.4 %all-to-all-start = ((f32[16,4,2,16,128]{4,3,2,1,0:T(8,128)}), f32[16,4,2,16,128]{4,3,2,1,0:T(8,128)S(1)}, u32[]{:S(2)}, u32[]{:S(2)}) async-start(f32[16,4,2,16,128]{4,3,2,1,0:T(8,128)} %merge.1.merged), calls=%async_computation | async-start | bytes 2097152 | tf_op jit(solution)/shard_map/all_to_all | solution.py:382
  18.8 8.6 %collective-permute-start.1 = (f32[64,128]{1,0:T(8,128)S(1)}, f32[64,128]{1,0:T(8,128)S(1)}, u32[]{:S(2)}, u32[]{:S(2)}) collective-permute-start(f32[64,128]{1,0:T(8,128)S(1)} %relay.1.a), channel_id=1, source_target_pairs={{0,8},{2,10},{4,12},{6,14},{8,0},{10,2},{12,4},{14,6},{1,9},{3,11}... | collective-permute-start | bytes 98312 | tf_op jit(solution)/shard_map/ppermute | solution.py:380
  27.4 9.3 %collective-permute-start.4 = (f32[64,128]{1,0:T(8,128)S(1)}, f32[64,128]{1,0:T(8,128)S(1)}, u32[]{:S(2)}, u32[]{:S(2)}) collective-permute-start(f32[64,128]{1,0:T(8,128)S(1)} %both.1.b0), channel_id=1, source_target_pairs={{0,48},{16,0},{32,16},{48,32},{1,49},{17,1},{33,17},{49,33},{2,50}... | collective-permute-start | bytes 98312 | tf_op jit(solution)/shard_map/ppermute | solution.py:384
  31.7 6.5 %collective-permute-start.3 = (f32[64,128]{1,0:T(8,128)S(1)}, f32[64,128]{1,0:T(8,128)S(1)}, u32[]{:S(2)}, u32[]{:S(2)}) collective-permute-start(f32[64,128]{1,0:T(8,128)S(1)} %both.1.b0), channel_id=1, source_target_pairs={{0,32},{16,48},{32,0},{48,16},{1,33},{17,49},{33,1},{49,17},{2,34}... | collective-permute-start | bytes 98312 | tf_op jit(solution)/shard_map/ppermute | solution.py:384
  34.2 6.3 %collective-permute-start.2 = (f32[64,128]{1,0:T(8,128)S(1)}, f32[64,128]{1,0:T(8,128)S(1)}, u32[]{:S(2)}, u32[]{:S(2)}) collective-permute-start(f32[64,128]{1,0:T(8,128)S(1)} %both.1.b0), channel_id=1, source_target_pairs={{0,16},{16,32},{32,48},{48,0},{1,17},{17,33},{33,49},{49,1},{2,18}... | collective-permute-start | bytes 98312 | tf_op jit(solution)/shard_map/ppermute | solution.py:384
  80.3 18.4 %all-to-all-start.3 = ((f32[64,8,128]{2,1,0:T(8,128)}), f32[64,8,128]{2,1,0:T(8,128)S(1)}, u32[]{:S(2)}, u32[]{:S(2)}) async-start(f32[64,8,128]{2,1,0:T(8,128)} %spread.1), calls=%async_computation.3 | async-start | bytes 524288 | tf_op jit(solution)/shard_map/all_to_all | solution.py:390
  89.7 4.0 %collective-permute-start.5 = (f32[64,128]{1,0:T(8,128)S(1)}, f32[64,128]{1,0:T(8,128)S(1)}, u32[]{:S(2)}, u32[]{:S(2)}) collective-permute-start(f32[64,128]{1,0:T(8,128)S(1)} %solve.1.mine), channel_id=1, source_target_pairs={{0,1},{1,0},{2,3},{3,2},{4,5},{5,4},{6,7},{7,6},{8,9},{9,8},{10,11... | collective-permute-start | bytes 98312 | tf_op jit(solution)/shard_map/ppermute | solution.py:392
  100.0 21.1 %copy-start = (f32[16,4,2,16,128]{4,3,2,1,0:T(8,128)S(1)}, f32[16,4,2,16,128]{4,3,2,1,0:T(8,128)}, u32[]{:S(2)}) copy-start(f32[16,4,2,16,128]{4,3,2,1,0:T(8,128)} %merge.1.merged) | copy-start | bytes 3145732

commit v8 on v7

--- a/solution.py
+++ b/solution.py
@@ -7,6 +7,7 @@
 
 NX, NZ, NC = 4, 8, 2
 LOOP = [(x, 0) for x in range(NX)] + [(x, 1) for x in reversed(range(NX))]
+DIAGONALS = [((i + z) % 8, z) for i in range(8) for z in range(NZ)]
 LANES = 128
 HIGHEST = lax.Precision.HIGHEST
 F32 = jnp.float32
@@ -281,9 +282,11 @@
 def approx_kernel(recv, mine, other, send, basis_out):
     z = lax.axis_index("z")
     inverse, rows = solutions(mine, other)
-    term = jnp.concatenate(
-        [recv[a * NZ : (a + 1) * NZ].reshape(64, LANES) for a in range(8)], axis=1
-    )
+    columns = [
+        jnp.concatenate([recv[DIAGONALS.index((a, part))] for part in range(NZ)], axis=0)
+        for a in range(8)
+    ]
+    term = jnp.concatenate(columns, axis=1)
     turned = dot(inverse, term, ((1,), (0,)))
     own = turned[:, :LANES]
     for a in range(1, 8):
@@ -387,7 +390,8 @@
     recv = lax.all_to_all(send, ("y", "c"), 0, 0)
     send = term_part(recv, mean)
     recv = lax.all_to_all(send, ("x", "z"), 0, 0)
-    gathered = lax.all_to_all(spread(recv), ("y", "z"), 0, 0)
+    groups = [[y * NZ + z for y, z in DIAGONALS]]
+    gathered = lax.all_to_all(spread(recv), ("y", "z"), 0, 0, axis_index_groups=groups)
     mine = solve(recv)
     other = lax.ppermute(mine, "c", [(0, 1), (1, 0)])
     left_factor, other = lax.optimization_barrier((left_part(mine, other), other))

time: 123 us -> 122 us (level)
  no operation moved by 1% of the time
where the time goes in v8:
time: 122 us; the launch traced here: 121 us
  blocking collectives  53.1 us (44%)
  starting transfers between devices  41.2 us (34%)
  waiting for transfers between devices  16.2 us (13%)
  Pallas kernels  10.2 us (8%)
    all_to_all x1, blocking collectives, shards(): recv = lax.all_to_all(send, ('x', 'c'), 0, 0, axis_index_groups=groups)  21.1 us
    all_to_all x1, blocking collectives, shards(): recv = lax.all_to_all(send, ('x', 'z'), 0, 0)  19.5 us
    all_to_all x1, blocking collectives, shards(): recv = lax.all_to_all(send, ('y', 'c'), 0, 0)  12.5 us
    ppermute x1, starting transfers between devices, shards(): held = lax.ppermute(held, ('y', 'z'), near_pairs())  11.5 us
    ppermute x3, starting transfers between devices, shards(): lax.ppermute(held, 'x', [(i, (i + k) % NX) for i in range(NX)])  9.32 us
    ppermute x1, starting transfers between devices, shards(): lax.ppermute(held, 'z', [(z, (z + 4) % NZ) for z in range(NZ)])  6.77 us
    all_to_all x1, waiting for transfers between devices, shards(): recv = lax.all_to_all(merged, ('y', 'c'), 0, 0)  6.2 us
    all_to_all x1, starting transfers between devices, shards(): lax.all_to_all(spread(recv), ('y', 'z'), 0, 0, axis_index_groups=groups)  5.99 us
  transfers between devices with their start and end apart: 8, of which 6 were waited for; matrix products, arithmetic and copies ran while one was open for 0% of the time, Pallas kernels for 5%

profile of v8, /device:TPU:1, one launch (start us, length us, event | category | flops | bytes accessed | tf_op | source)
XLA Modules:
  0.0 121.4 jit_solution(5868404085274041881)
XLA Ops:
  0.6 11.5 %collective-permute-start = (f32[64,128]{1,0:T(8,128)}, f32[64,128]{1,0:T(8,128)S(1)}, u32[]{:S(2)}, u32[]{:S(2)}) collective-permute-start(f32[64,128]{1,0:T(8,128)} %bitcast.6), channel_id=1, source_target_pairs={{0,12},{64,14},{128,0},{448,2},{66,78},{130,64},{194,66},{2,68},{1... | collective-permute-start | bytes 98312 | tf_op jit(solution)/shard_map/ppermute | solution.py:381
  12.1 2.2 %merge.1.merged = f32[16,4,2,16,128]{4,3,2,1,0:T(8,128)} custom-call(bf16[1,2,16,8192]{3,2,1,0:T(8,128)(2,1)} %grads.1, f32[1,2,16,8192]{3,2,1,0:T(8,128)} %errors.1), custom_call_target="tpu_custom_call" | custom-call | flops 524288 | bytes 2621440 | tf_op jit(solution)/shard_map/merge/pallas_call | solution.py:56
  14.4 4.4 %all-to-all-start = ((f32[16,4,2,16,128]{4,3,2,1,0:T(8,128)}), f32[16,4,2,16,128]{4,3,2,1,0:T(8,128)S(1)}, u32[]{:S(2)}, u32[]{:S(2)}) async-start(f32[16,4,2,16,128]{4,3,2,1,0:T(8,128)} %merge.1.merged), calls=%async_computation | async-start | bytes 2097152 | tf_op jit(solution)/shard_map/all_to_all | solution.py:385
  18.8 0.0 collective-permute-done.block
  18.8 6.8 %collective-permute-start.1 = (f32[64,128]{1,0:T(8,128)S(1)}, f32[64,128]{1,0:T(8,128)S(1)}, u32[]{:S(2)}, u32[]{:S(2)}) collective-permute-start(f32[64,128]{1,0:T(8,128)S(1)} %relay.1.a), channel_id=1, source_target_pairs={{0,8},{2,10},{4,12},{6,14},{8,0},{10,2},{12,4},{14,6},{1,9},{3,11}... | collective-permute-start | bytes 98312 | tf_op jit(solution)/shard_map/ppermute | solution.py:383
  25.6 1.8 %collective-permute-done.1.b = f32[64,128]{1,0:T(8,128)S(1)} collective-permute-done((f32[64,128]{1,0:T(8,128)S(1)}, f32[64,128]{1,0:T(8,128)S(1)}, u32[]{:S(2)}, u32[]{:S(2)}) %collective-permute-start.1) | collective-permute-done | bytes 32800 | tf_op jit(solution)/shard_map/ppermute | solution.py:383
  27.4 4.4 %collective-permute-start.4 = (f32[64,128]{1,0:T(8,128)S(1)}, f32[64,128]{1,0:T(8,128)S(1)}, u32[]{:S(2)}, u32[]{:S(2)}) collective-permute-start(f32[64,128]{1,0:T(8,128)S(1)} %both.1.b0), channel_id=1, source_target_pairs={{0,48},{16,0},{32,16},{48,32},{1,49},{17,1},{33,17},{49,33},{2,50}... | collective-permute-start | bytes 98312 | tf_op jit(solution)/shard_map/ppermute | solution.py:387
  31.7 2.4 %collective-permute-start.3 = (f32[64,128]{1,0:T(8,128)S(1)}, f32[64,128]{1,0:T(8,128)S(1)}, u32[]{:S(2)}, u32[]{:S(2)}) collective-permute-start(f32[64,128]{1,0:T(8,128)S(1)} %both.1.b0), channel_id=1, source_target_pairs={{0,32},{16,48},{32,0},{48,16},{1,33},{17,49},{33,1},{49,17},{2,34}... | collective-permute-start | bytes 98312 | tf_op jit(solution)/shard_map/ppermute | solution.py:387
  34.2 2.5 %collective-permute-start.2 = (f32[64,128]{1,0:T(8,128)S(1)}, f32[64,128]{1,0:T(8,128)S(1)}, u32[]{:S(2)}, u32[]{:S(2)}) collective-permute-start(f32[64,128]{1,0:T(8,128)S(1)} %both.1.b0), channel_id=1, source_target_pairs={{0,16},{16,32},{32,48},{48,0},{1,17},{17,33},{33,49},{49,1},{2,18}... | collective-permute-start | bytes 98312 | tf_op jit(solution)/shard_map/ppermute | solution.py:387
  36.7 0.0 collective-permute-done.4.b3
  36.7 1.5 %collective-permute-done.3.b2 = f32[64,128]{1,0:T(8,128)S(1)} collective-permute-done((f32[64,128]{1,0:T(8,128)S(1)}, f32[64,128]{1,0:T(8,128)S(1)}, u32[]{:S(2)}, u32[]{:S(2)}) %collective-permute-start.3) | collective-permute-done | bytes 32800 | tf_op jit(solution)/shard_map/ppermute | solution.py:387
  38.2 2.3 %collective-permute-done.2.b1 = f32[64,128]{1,0:T(8,128)S(1)} collective-permute-done((f32[64,128]{1,0:T(8,128)S(1)}, f32[64,128]{1,0:T(8,128)S(1)}, u32[]{:S(2)}, u32[]{:S(2)}) %collective-permute-start.2) | collective-permute-done | bytes 32800 | tf_op jit(solution)/shard_map/ppermute | solution.py:387
  40.6 6.2 %all-to-all-done.recv = f32[16,4,2,16,128]{4,3,2,1,0:T(8,128)S(1)} async-done(((f32[16,4,2,16,128]{4,3,2,1,0:T(8,128)}), f32[16,4,2,16,128]{4,3,2,1,0:T(8,128)S(1)}, u32[]{:S(2)}, u32[]{:S(2)}) %all-to-all-start) | async-done | bytes 1048608 | tf_op jit(solution)/shard_map/all_to_all | solution.py:385
  46.8 0.4 factor_part.1
  47.2 12.5 %all_to_all.25.recv = f32[16,16,128]{2,1,0:T(8,128)S(1)} all-to-all(f32[16,16,128]{2,1,0:T(8,128)S(1)} %get-tuple-element.9), channel_id=1, replica_groups=mesh['y'=8,'x'=4,'z'=8,'c'=2] {'y','c'}, dimensions={0} | all-to-all | bytes 262144 | tf_op jit(solution)/shard_map/all_to_all | solution.py:390
  59.6 0.4 term_part.1
  60.0 19.5 %all_to_all.26.recv = f32[32,16,128]{2,1,0:T(8,128)S(1)} all-to-all(f32[32,16,128]{2,1,0:T(8,128)S(1)} %term_part.1), channel_id=1, replica_groups=mesh['y'=8,'x'=4,'z'=8,'c'=2] {'x','z'}, dimensions={0} | all-to-all | bytes 524288 | tf_op jit(solution)/shard_map/all_to_all | solution.py:392
  79.6 0.8 spread.1
  80.3 6.0 %all-to-all-start.3 = ((f32[64,8,128]{2,1,0:T(8,128)}), f32[64,8,128]{2,1,0:T(8,128)S(1)}, u32[]{:S(2)}, u32[]{:S(2)}) async-start(f32[64,8,128]{2,1,0:T(8,128)} %spread.1), calls=%async_computation.3 | async-start | bytes 524288 | tf_op jit(solution)/shard_map/all_to_all | solution.py:394
  86.3 3.4 %solve.1.mine = f32[64,128]{1,0:T(8,128)S(1)} custom-call(f32[32,16,128]{2,1,0:T(8,128)S(1)} %all_to_all.26.recv), custom_call_target="tpu_custom_call" | custom-call | flops 16777216 | bytes 524288 | tf_op jit(solution)/shard_map/solve/pallas_call | solution.py:254
  89.7 3.2 %collective-permute-start.5 = (f32[64,128]{1,0:T(8,128)S(1)}, f32[64,128]{1,0:T(8,128)S(1)}, u32[]{:S(2)}, u32[]{:S(2)}) collective-permute-start(f32[64,128]{1,0:T(8,128)S(1)} %solve.1.mine), channel_id=1, source_target_pairs={{0,1},{1,0},{2,3},{3,2},{4,5},{5,4},{6,7},{7,6},{8,9},{9,8},{10,11... | collective-permute-start | bytes 98312 | tf_op jit(solution)/shard_map/ppermute | solution.py:396
  92.9 0.8 collective-permute-done.5.other
  93.7 0.8 left_part.1
  94.5 3.5 %all-to-all-done.3.recv = f32[64,8,128]{2,1,0:T(8,128)S(1)} async-done(((f32[64,8,128]{2,1,0:T(8,128)}), f32[64,8,128]{2,1,0:T(8,128)S(1)}, u32[]{:S(2)}, u32[]{:S(2)}) %all-to-all-start.3) | async-done | bytes 262176 | tf_op jit(solution)/shard_map/all_to_all | solution.py:394
  98.0 1.3 %approx_part.1 = (f32[8,2,16,1024]{3,2,1,0:T(8,128)S(1)}, f32[64,128]{1,0:T(8,128)}) custom-call(f32[64,8,128]{2,1,0:T(8,128)S(1)} %all-to-all-done.3.recv, f32[64,128]{1,0:T(8,128)S(1)} %solve.1.mine, f32[64,128]{1,0:T(8,128)S(1)} %collective-permute-done.5.other), custom_call_target="tpu_custom_call" | custom-call | flops 67108864 | bytes 1048576 | tf_op jit(solution)/shard_map/approx_part/pallas_call | solution.py:302
  99.3 0.0 copy-start
  99.3 21.1 %all_to_all.27.recv = f32[8,2,16,1024]{3,2,1,0:T(8,128)S(1)} all-to-all(f32[8,2,16,1024]{3,2,1,0:T(8,128)S(1)} %get-tuple-element.12), channel_id=1, replica_groups={{0,16,32,48,49,33,17,1},{2,18,34,50,51,35,19,3},{4,20,36,52,53,37,21,5}..., dimensions={0} | all-to-all | bytes 2097152 | tf_op jit(solution)/shard_map/all_to_all | solution.py:400
  120.4 0.0 copy-done
  120.4 1.0 subtract.1
  (3 shorter events, 0.0 us)
Async XLA Ops:
  0.6 18.1 %collective-permute-start = (f32[64,128]{1,0:T(8,128)}, f32[64,128]{1,0:T(8,128)S(1)}, u32[]{:S(2)}, u32[]{:S(2)}) collective-permute-start(f32[64,128]{1,0:T(8,128)} %bitcast.6), channel_id=1, source_target_pairs={{0,12},{64,14},{128,0},{448,2},{66,78},{130,64},{194,66},{2,68},{1... | collective-permute-start | bytes 98312 | tf_op jit(solution)/shard_map/ppermute | solution.py:381
  14.4 32.4 %all-to-all-start = ((f32[16,4,2,16,128]{4,3,2,1,0:T(8,128)}), f32[16,4,2,16,128]{4,3,2,1,0:T(8,128)S(1)}, u32[]{:S(2)}, u32[]{:S(2)}) async-start(f32[16,4,2,16,128]{4,3,2,1,0:T(8,128)} %merge.1.merged), calls=%async_computation | async-start | bytes 2097152 | tf_op jit(solution)/shard_map/all_to_all | solution.py:385
  18.8 8.6 %collective-permute-start.1 = (f32[64,128]{1,0:T(8,128)S(1)}, f32[64,128]{1,0:T(8,128)S(1)}, u32[]{:S(2)}, u32[]{:S(2)}) collective-permute-start(f32[64,128]{1,0:T(8,128)S(1)} %relay.1.a), channel_id=1, source_target_pairs={{0,8},{2,10},{4,12},{6,14},{8,0},{10,2},{12,4},{14,6},{1,9},{3,11}... | collective-permute-start | bytes 98312 | tf_op jit(solution)/shard_map/ppermute | solution.py:383
  27.4 9.3 %collective-permute-start.4 = (f32[64,128]{1,0:T(8,128)S(1)}, f32[64,128]{1,0:T(8,128)S(1)}, u32[]{:S(2)}, u32[]{:S(2)}) collective-permute-start(f32[64,128]{1,0:T(8,128)S(1)} %both.1.b0), channel_id=1, source_target_pairs={{0,48},{16,0},{32,16},{48,32},{1,49},{17,1},{33,17},{49,33},{2,50}... | collective-permute-start | bytes 98312 | tf_op jit(solution)/shard_map/ppermute | solution.py:387
  31.7 6.5 %collective-permute-start.3 = (f32[64,128]{1,0:T(8,128)S(1)}, f32[64,128]{1,0:T(8,128)S(1)}, u32[]{:S(2)}, u32[]{:S(2)}) collective-permute-start(f32[64,128]{1,0:T(8,128)S(1)} %both.1.b0), channel_id=1, source_target_pairs={{0,32},{16,48},{32,0},{48,16},{1,33},{17,49},{33,1},{49,17},{2,34}... | collective-permute-start | bytes 98312 | tf_op jit(solution)/shard_map/ppermute | solution.py:387
  34.2 6.3 %collective-permute-start.2 = (f32[64,128]{1,0:T(8,128)S(1)}, f32[64,128]{1,0:T(8,128)S(1)}, u32[]{:S(2)}, u32[]{:S(2)}) collective-permute-start(f32[64,128]{1,0:T(8,128)S(1)} %both.1.b0), channel_id=1, source_target_pairs={{0,16},{16,32},{32,48},{48,0},{1,17},{17,33},{33,49},{49,1},{2,18}... | collective-permute-start | bytes 98312 | tf_op jit(solution)/shard_map/ppermute | solution.py:387
  80.3 17.7 %all-to-all-start.3 = ((f32[64,8,128]{2,1,0:T(8,128)}), f32[64,8,128]{2,1,0:T(8,128)S(1)}, u32[]{:S(2)}, u32[]{:S(2)}) async-start(f32[64,8,128]{2,1,0:T(8,128)} %spread.1), calls=%async_computation.3 | async-start | bytes 524288 | tf_op jit(solution)/shard_map/all_to_all | solution.py:394
  89.7 4.0 %collective-permute-start.5 = (f32[64,128]{1,0:T(8,128)S(1)}, f32[64,128]{1,0:T(8,128)S(1)}, u32[]{:S(2)}, u32[]{:S(2)}) collective-permute-start(f32[64,128]{1,0:T(8,128)S(1)} %solve.1.mine), channel_id=1, source_target_pairs={{0,1},{1,0},{2,3},{3,2},{4,5},{5,4},{6,7},{7,6},{8,9},{9,8},{10,11... | collective-permute-start | bytes 98312 | tf_op jit(solution)/shard_map/ppermute | solution.py:396
  99.3 21.1 %copy-start = (f32[16,4,2,16,128]{4,3,2,1,0:T(8,128)S(1)}, f32[16,4,2,16,128]{4,3,2,1,0:T(8,128)}, u32[]{:S(2)}) copy-start(f32[16,4,2,16,128]{4,3,2,1,0:T(8,128)} %merge.1.merged) | copy-start | bytes 3145732

commit v9 on v8

--- a/solution.py
+++ b/solution.py
@@ -383,9 +383,10 @@
     held = both(held, lax.ppermute(held, "z", [(z, (z + 4) % NZ) for z in range(NZ)]))
     merged = merge(grads, errors)
     recv = lax.all_to_all(merged, ("y", "c"), 0, 0)
-    parts = [held] + [
-        lax.ppermute(held, "x", [(i, (i + k) % NX) for i in range(NX)]) for k in range(1, NX)
-    ]
+    moved = {
+        k: lax.ppermute(held, "x", [(i, (i + k) % NX) for i in range(NX)]) for k in (1, 3, 2)
+    }
+    parts = [held] + [moved[k] for k in range(1, NX)]
     mean, send = factor_part(recv, arrange(parts))
     recv = lax.all_to_all(send, ("y", "c"), 0, 0)
     send = term_part(recv, mean)

time: 122 us -> 122 us (level)
  no operation moved by 1% of the time
where the time goes in v9:
time: 122 us; the launch traced here: 121 us
  blocking collectives  53.1 us (44%)
  starting transfers between devices  41.2 us (34%)
  waiting for transfers between devices  16.2 us (13%)
  Pallas kernels  10.2 us (8%)
    all_to_all x1, blocking collectives, shards(): recv = lax.all_to_all(send, ('x', 'c'), 0, 0, axis_index_groups=groups)  21.1 us
    all_to_all x1, blocking collectives, shards(): recv = lax.all_to_all(send, ('x', 'z'), 0, 0)  19.5 us
    all_to_all x1, blocking collectives, shards(): recv = lax.all_to_all(send, ('y', 'c'), 0, 0)  12.5 us
    ppermute x1, starting transfers between devices, shards(): held = lax.ppermute(held, ('y', 'z'), near_pairs())  11.5 us
    ppermute x3, starting transfers between devices, shards(): lax.ppermute(held, 'x', [(i, (i + k) % NX) for i in range(NX)])  9.32 us
    ppermute x1, starting transfers between devices, shards(): lax.ppermute(held, 'z', [(z, (z + 4) % NZ) for z in range(NZ)])  6.77 us
    all_to_all x1, waiting for transfers between devices, shards(): recv = lax.all_to_all(merged, ('y', 'c'), 0, 0)  6.2 us
    all_to_all x1, starting transfers between devices, shards(): lax.all_to_all(spread(recv), ('y', 'z'), 0, 0, axis_index_groups=groups)  5.99 us
  transfers between devices with their start and end apart: 8, of which 6 were waited for; matrix products, arithmetic and copies ran while one was open for 0% of the time, Pallas kernels for 5%

profile of v9, /device:TPU:1, one launch (start us, length us, event | category | flops | bytes accessed | tf_op | source)
XLA Modules:
  0.0 121.4 jit_solution(5868404085274041881)
XLA Ops:
  0.6 11.5 %collective-permute-start = (f32[64,128]{1,0:T(8,128)}, f32[64,128]{1,0:T(8,128)S(1)}, u32[]{:S(2)}, u32[]{:S(2)}) collective-permute-start(f32[64,128]{1,0:T(8,128)} %bitcast.6), channel_id=1, source_target_pairs={{0,12},{64,14},{128,0},{448,2},{66,78},{130,64},{194,66},{2,68},{1... | collective-permute-start | bytes 98312 | tf_op jit(solution)/shard_map/ppermute | solution.py:381
  12.1 2.2 %merge.1.merged = f32[16,4,2,16,128]{4,3,2,1,0:T(8,128)} custom-call(bf16[1,2,16,8192]{3,2,1,0:T(8,128)(2,1)} %grads.1, f32[1,2,16,8192]{3,2,1,0:T(8,128)} %errors.1), custom_call_target="tpu_custom_call" | custom-call | flops 524288 | bytes 2621440 | tf_op jit(solution)/shard_map/merge/pallas_call | solution.py:56
  14.4 4.4 %all-to-all-start = ((f32[16,4,2,16,128]{4,3,2,1,0:T(8,128)}), f32[16,4,2,16,128]{4,3,2,1,0:T(8,128)S(1)}, u32[]{:S(2)}, u32[]{:S(2)}) async-start(f32[16,4,2,16,128]{4,3,2,1,0:T(8,128)} %merge.1.merged), calls=%async_computation | async-start | bytes 2097152 | tf_op jit(solution)/shard_map/all_to_all | solution.py:385
  18.8 0.0 collective-permute-done.block
  18.8 6.8 %collective-permute-start.1 = (f32[64,128]{1,0:T(8,128)S(1)}, f32[64,128]{1,0:T(8,128)S(1)}, u32[]{:S(2)}, u32[]{:S(2)}) collective-permute-start(f32[64,128]{1,0:T(8,128)S(1)} %relay.1.a), channel_id=1, source_target_pairs={{0,8},{2,10},{4,12},{6,14},{8,0},{10,2},{12,4},{14,6},{1,9},{3,11}... | collective-permute-start | bytes 98312 | tf_op jit(solution)/shard_map/ppermute | solution.py:383
  25.6 1.8 %collective-permute-done.1.b = f32[64,128]{1,0:T(8,128)S(1)} collective-permute-done((f32[64,128]{1,0:T(8,128)S(1)}, f32[64,128]{1,0:T(8,128)S(1)}, u32[]{:S(2)}, u32[]{:S(2)}) %collective-permute-start.1) | collective-permute-done | bytes 32800 | tf_op jit(solution)/shard_map/ppermute | solution.py:383
  27.4 4.4 %collective-permute-start.4 = (f32[64,128]{1,0:T(8,128)S(1)}, f32[64,128]{1,0:T(8,128)S(1)}, u32[]{:S(2)}, u32[]{:S(2)}) collective-permute-start(f32[64,128]{1,0:T(8,128)S(1)} %both.1.b0), channel_id=1, source_target_pairs={{0,48},{16,0},{32,16},{48,32},{1,49},{17,1},{33,17},{49,33},{2,50}... | collective-permute-start | bytes 98312 | tf_op jit(solution)/shard_map/ppermute | solution.py:387
  31.7 2.4 %collective-permute-start.3 = (f32[64,128]{1,0:T(8,128)S(1)}, f32[64,128]{1,0:T(8,128)S(1)}, u32[]{:S(2)}, u32[]{:S(2)}) collective-permute-start(f32[64,128]{1,0:T(8,128)S(1)} %both.1.b0), channel_id=1, source_target_pairs={{0,32},{16,48},{32,0},{48,16},{1,33},{17,49},{33,1},{49,17},{2,34}... | collective-permute-start | bytes 98312 | tf_op jit(solution)/shard_map/ppermute | solution.py:387
  34.2 2.5 %collective-permute-start.2 = (f32[64,128]{1,0:T(8,128)S(1)}, f32[64,128]{1,0:T(8,128)S(1)}, u32[]{:S(2)}, u32[]{:S(2)}) collective-permute-start(f32[64,128]{1,0:T(8,128)S(1)} %both.1.b0), channel_id=1, source_target_pairs={{0,16},{16,32},{32,48},{48,0},{1,17},{17,33},{33,49},{49,1},{2,18}... | collective-permute-start | bytes 98312 | tf_op jit(solution)/shard_map/ppermute | solution.py:387
  36.7 0.0 collective-permute-done.4.b3
  36.7 1.5 %collective-permute-done.3.b2 = f32[64,128]{1,0:T(8,128)S(1)} collective-permute-done((f32[64,128]{1,0:T(8,128)S(1)}, f32[64,128]{1,0:T(8,128)S(1)}, u32[]{:S(2)}, u32[]{:S(2)}) %collective-permute-start.3) | collective-permute-done | bytes 32800 | tf_op jit(solution)/shard_map/ppermute | solution.py:387
  38.2 2.3 %collective-permute-done.2.b1 = f32[64,128]{1,0:T(8,128)S(1)} collective-permute-done((f32[64,128]{1,0:T(8,128)S(1)}, f32[64,128]{1,0:T(8,128)S(1)}, u32[]{:S(2)}, u32[]{:S(2)}) %collective-permute-start.2) | collective-permute-done | bytes 32800 | tf_op jit(solution)/shard_map/ppermute | solution.py:387
  40.6 6.2 %all-to-all-done.recv = f32[16,4,2,16,128]{4,3,2,1,0:T(8,128)S(1)} async-done(((f32[16,4,2,16,128]{4,3,2,1,0:T(8,128)}), f32[16,4,2,16,128]{4,3,2,1,0:T(8,128)S(1)}, u32[]{:S(2)}, u32[]{:S(2)}) %all-to-all-start) | async-done | bytes 1048608 | tf_op jit(solution)/shard_map/all_to_all | solution.py:385
  46.8 0.4 factor_part.1
  47.2 12.5 %all_to_all.25.recv = f32[16,16,128]{2,1,0:T(8,128)S(1)} all-to-all(f32[16,16,128]{2,1,0:T(8,128)S(1)} %get-tuple-element.9), channel_id=1, replica_groups=mesh['y'=8,'x'=4,'z'=8,'c'=2] {'y','c'}, dimensions={0} | all-to-all | bytes 262144 | tf_op jit(solution)/shard_map/all_to_all | solution.py:391
  59.6 0.4 term_part.1
  60.0 19.5 %all_to_all.26.recv = f32[32,16,128]{2,1,0:T(8,128)S(1)} all-to-all(f32[32,16,128]{2,1,0:T(8,128)S(1)} %term_part.1), channel_id=1, replica_groups=mesh['y'=8,'x'=4,'z'=8,'c'=2] {'x','z'}, dimensions={0} | all-to-all | bytes 524288 | tf_op jit(solution)/shard_map/all_to_all | solution.py:393
  79.6 0.8 spread.1
  80.3 6.0 %all-to-all-start.3 = ((f32[64,8,128]{2,1,0:T(8,128)}), f32[64,8,128]{2,1,0:T(8,128)S(1)}, u32[]{:S(2)}, u32[]{:S(2)}) async-start(f32[64,8,128]{2,1,0:T(8,128)} %spread.1), calls=%async_computation.3 | async-start | bytes 524288 | tf_op jit(solution)/shard_map/all_to_all | solution.py:395
  86.3 3.4 %solve.1.mine = f32[64,128]{1,0:T(8,128)S(1)} custom-call(f32[32,16,128]{2,1,0:T(8,128)S(1)} %all_to_all.26.recv), custom_call_target="tpu_custom_call" | custom-call | flops 16777216 | bytes 524288 | tf_op jit(solution)/shard_map/solve/pallas_call | solution.py:254
  89.7 3.2 %collective-permute-start.5 = (f32[64,128]{1,0:T(8,128)S(1)}, f32[64,128]{1,0:T(8,128)S(1)}, u32[]{:S(2)}, u32[]{:S(2)}) collective-permute-start(f32[64,128]{1,0:T(8,128)S(1)} %solve.1.mine), channel_id=1, source_target_pairs={{0,1},{1,0},{2,3},{3,2},{4,5},{5,4},{6,7},{7,6},{8,9},{9,8},{10,11... | collective-permute-start | bytes 98312 | tf_op jit(solution)/shard_map/ppermute | solution.py:397
  92.9 0.8 collective-permute-done.5.other
  93.7 0.8 left_part.1
  94.5 3.5 %all-to-all-done.3.recv = f32[64,8,128]{2,1,0:T(8,128)S(1)} async-done(((f32[64,8,128]{2,1,0:T(8,128)}), f32[64,8,128]{2,1,0:T(8,128)S(1)}, u32[]{:S(2)}, u32[]{:S(2)}) %all-to-all-start.3) | async-done | bytes 262176 | tf_op jit(solution)/shard_map/all_to_all | solution.py:395
  98.0 1.3 %approx_part.1 = (f32[8,2,16,1024]{3,2,1,0:T(8,128)S(1)}, f32[64,128]{1,0:T(8,128)}) custom-call(f32[64,8,128]{2,1,0:T(8,128)S(1)} %all-to-all-done.3.recv, f32[64,128]{1,0:T(8,128)S(1)} %solve.1.mine, f32[64,128]{1,0:T(8,128)S(1)} %collective-permute-done.5.other), custom_call_target="tpu_custom_call" | custom-call | flops 67108864 | bytes 1048576 | tf_op jit(solution)/shard_map/approx_part/pallas_call | solution.py:302
  99.3 0.0 copy-start
  99.3 21.1 %all_to_all.27.recv = f32[8,2,16,1024]{3,2,1,0:T(8,128)S(1)} all-to-all(f32[8,2,16,1024]{3,2,1,0:T(8,128)S(1)} %get-tuple-element.12), channel_id=1, replica_groups={{0,16,32,48,49,33,17,1},{2,18,34,50,51,35,19,3},{4,20,36,52,53,37,21,5}..., dimensions={0} | all-to-all | bytes 2097152 | tf_op jit(solution)/shard_map/all_to_all | solution.py:401
  120.4 0.0 copy-done
  120.4 1.0 subtract.1
  (3 shorter events, 0.0 us)
Async XLA Ops:
  0.6 18.1 %collective-permute-start = (f32[64,128]{1,0:T(8,128)}, f32[64,128]{1,0:T(8,128)S(1)}, u32[]{:S(2)}, u32[]{:S(2)}) collective-permute-start(f32[64,128]{1,0:T(8,128)} %bitcast.6), channel_id=1, source_target_pairs={{0,12},{64,14},{128,0},{448,2},{66,78},{130,64},{194,66},{2,68},{1... | collective-permute-start | bytes 98312 | tf_op jit(solution)/shard_map/ppermute | solution.py:381
  14.4 32.4 %all-to-all-start = ((f32[16,4,2,16,128]{4,3,2,1,0:T(8,128)}), f32[16,4,2,16,128]{4,3,2,1,0:T(8,128)S(1)}, u32[]{:S(2)}, u32[]{:S(2)}) async-start(f32[16,4,2,16,128]{4,3,2,1,0:T(8,128)} %merge.1.merged), calls=%async_computation | async-start | bytes 2097152 | tf_op jit(solution)/shard_map/all_to_all | solution.py:385
  18.8 8.6 %collective-permute-start.1 = (f32[64,128]{1,0:T(8,128)S(1)}, f32[64,128]{1,0:T(8,128)S(1)}, u32[]{:S(2)}, u32[]{:S(2)}) collective-permute-start(f32[64,128]{1,0:T(8,128)S(1)} %relay.1.a), channel_id=1, source_target_pairs={{0,8},{2,10},{4,12},{6,14},{8,0},{10,2},{12,4},{14,6},{1,9},{3,11}... | collective-permute-start | bytes 98312 | tf_op jit(solution)/shard_map/ppermute | solution.py:383
  27.4 9.3 %collective-permute-start.4 = (f32[64,128]{1,0:T(8,128)S(1)}, f32[64,128]{1,0:T(8,128)S(1)}, u32[]{:S(2)}, u32[]{:S(2)}) collective-permute-start(f32[64,128]{1,0:T(8,128)S(1)} %both.1.b0), channel_id=1, source_target_pairs={{0,48},{16,0},{32,16},{48,32},{1,49},{17,1},{33,17},{49,33},{2,50}... | collective-permute-start | bytes 98312 | tf_op jit(solution)/shard_map/ppermute | solution.py:387
  31.7 6.5 %collective-permute-start.3 = (f32[64,128]{1,0:T(8,128)S(1)}, f32[64,128]{1,0:T(8,128)S(1)}, u32[]{:S(2)}, u32[]{:S(2)}) collective-permute-start(f32[64,128]{1,0:T(8,128)S(1)} %both.1.b0), channel_id=1, source_target_pairs={{0,32},{16,48},{32,0},{48,16},{1,33},{17,49},{33,1},{49,17},{2,34}... | collective-permute-start | bytes 98312 | tf_op jit(solution)/shard_map/ppermute | solution.py:387
  34.2 6.3 %collective-permute-start.2 = (f32[64,128]{1,0:T(8,128)S(1)}, f32[64,128]{1,0:T(8,128)S(1)}, u32[]{:S(2)}, u32[]{:S(2)}) collective-permute-start(f32[64,128]{1,0:T(8,128)S(1)} %both.1.b0), channel_id=1, source_target_pairs={{0,16},{16,32},{32,48},{48,0},{1,17},{17,33},{33,49},{49,1},{2,18}... | collective-permute-start | bytes 98312 | tf_op jit(solution)/shard_map/ppermute | solution.py:387
  80.3 17.7 %all-to-all-start.3 = ((f32[64,8,128]{2,1,0:T(8,128)}), f32[64,8,128]{2,1,0:T(8,128)S(1)}, u32[]{:S(2)}, u32[]{:S(2)}) async-start(f32[64,8,128]{2,1,0:T(8,128)} %spread.1), calls=%async_computation.3 | async-start | bytes 524288 | tf_op jit(solution)/shard_map/all_to_all | solution.py:395
  89.7 4.0 %collective-permute-start.5 = (f32[64,128]{1,0:T(8,128)S(1)}, f32[64,128]{1,0:T(8,128)S(1)}, u32[]{:S(2)}, u32[]{:S(2)}) collective-permute-start(f32[64,128]{1,0:T(8,128)S(1)} %solve.1.mine), channel_id=1, source_target_pairs={{0,1},{1,0},{2,3},{3,2},{4,5},{5,4},{6,7},{7,6},{8,9},{9,8},{10,11... | collective-permute-start | bytes 98312 | tf_op jit(solution)/shard_map/ppermute | solution.py:397
  99.3 21.1 %copy-start = (f32[16,4,2,16,128]{4,3,2,1,0:T(8,128)S(1)}, f32[16,4,2,16,128]{4,3,2,1,0:T(8,128)}, u32[]{:S(2)}) copy-start(f32[16,4,2,16,128]{4,3,2,1,0:T(8,128)} %merge.1.merged) | copy-start | bytes 3145732

commit v10 on v8

--- a/solution.py
+++ b/solution.py
@@ -30,21 +30,22 @@
 
 def merge_kernel(grads, errors, out, grads_in, errors_in, blocks, sems):
     copies, results = [], []
-    for x in range(NX):
+    for h in range(2 * NX):
+        at = pl.ds(h * 8 * LANES, 8 * LANES)
         for k, (source, target) in enumerate(((grads, grads_in), (errors, errors_in))):
-            copy = pltpu.make_async_copy(
-                source.at[0, :, :, chunk(x)], target.at[:, :, chunk(x)], sems.at[k, x]
-            )
+            copy = pltpu.make_async_copy(source.at[0, :, :, at], target.at[:, :, at], sems.at[k, h])
             copy.start()
             copies.append(copy)
-    for x in range(NX):
-        copies[2 * x].wait()
-        copies[2 * x + 1].wait()
+    for h in range(2 * NX):
+        copies[2 * h].wait()
+        copies[2 * h + 1].wait()
+        x, first = h // 2, h % 2 * 8
         for m in range(2):
-            for block in range(16):
+            for block in range(first, first + 8):
                 at = pl.ds((x * 16 + block) * LANES, LANES)
                 blocks[block, x, m] = grads_in[m, :, at].astype(F32) + errors_in[m, :, at]
-        copy = pltpu.make_async_copy(blocks.at[:, x], out.at[:, x], sems.at[2, x])
+        some = pl.ds(first, 8)
+        copy = pltpu.make_async_copy(blocks.at[some, x], out.at[some, x], sems.at[2, h])
         copy.start()
         results.append(copy)
     for copy in results:
@@ -62,7 +63,7 @@
             pltpu.VMEM((mats, rows, width), grads.dtype),
             pltpu.VMEM((mats, rows, width), errors.dtype),
             pltpu.VMEM((16, NX, mats, rows, LANES), F32),
-            pltpu.SemaphoreType.DMA((3, NX)),
+            pltpu.SemaphoreType.DMA((3, 2 * NX)),
         ],
         cost_estimate=cost(2**19, 5 * 2**19),
         name="merge",

time: 122 us -> 122 us (level)
  no operation moved by 1% of the time
where the time goes in v10:
time: 122 us
  blocking collectives  53.1 us (44%)
  starting transfers between devices  41.2 us (34%)
  waiting for transfers between devices  16.2 us (13%)
  Pallas kernels  10.3 us (8%)
    all_to_all x1, blocking collectives, shards(): recv = lax.all_to_all(send, ('x', 'c'), 0, 0, axis_index_groups=groups)  21.1 us
    all_to_all x1, blocking collectives, shards(): recv = lax.all_to_all(send, ('x', 'z'), 0, 0)  19.5 us
    all_to_all x1, blocking collectives, shards(): recv = lax.all_to_all(send, ('y', 'c'), 0, 0)  12.5 us
    ppermute x1, starting transfers between devices, shards(): held = lax.ppermute(held, ('y', 'z'), near_pairs())  11.5 us
    ppermute x3, starting transfers between devices, shards(): lax.ppermute(held, 'x', [(i, (i + k) % NX) for i in range(NX)])  9.32 us
    ppermute x1, starting transfers between devices, shards(): lax.ppermute(held, 'z', [(z, (z + 4) % NZ) for z in range(NZ)])  6.77 us
    all_to_all x1, waiting for transfers between devices, shards(): recv = lax.all_to_all(merged, ('y', 'c'), 0, 0)  6.2 us
    all_to_all x1, starting transfers between devices, shards(): lax.all_to_all(spread(recv), ('y', 'z'), 0, 0, axis_index_groups=groups)  5.99 us
  transfers between devices with their start and end apart: 8, of which 6 were waited for; matrix products, arithmetic and copies ran while one was open for 0% of the time, Pallas kernels for 5%

profile of v10, /device:TPU:1, one launch (start us, length us, event | category | flops | bytes accessed | tf_op | source)
XLA Modules:
  0.0 121.5 jit_solution(12452964746484181318)
XLA Ops:
  0.6 11.5 %collective-permute-start = (f32[64,128]{1,0:T(8,128)}, f32[64,128]{1,0:T(8,128)S(1)}, u32[]{:S(2)}, u32[]{:S(2)}) collective-permute-start(f32[64,128]{1,0:T(8,128)} %bitcast.6), channel_id=1, source_target_pairs={{0,12},{64,14},{128,0},{448,2},{66,78},{130,64},{194,66},{2,68},{1... | collective-permute-start | bytes 98312 | tf_op jit(solution)/shard_map/ppermute | solution.py:382
  12.1 2.3 %merge.1.merged = f32[16,4,2,16,128]{4,3,2,1,0:T(8,128)} custom-call(bf16[1,2,16,8192]{3,2,1,0:T(8,128)(2,1)} %grads.1, f32[1,2,16,8192]{3,2,1,0:T(8,128)} %errors.1), custom_call_target="tpu_custom_call" | custom-call | flops 524288 | bytes 2621440 | tf_op jit(solution)/shard_map/merge/pallas_call | solution.py:57
  14.5 4.4 %all-to-all-start = ((f32[16,4,2,16,128]{4,3,2,1,0:T(8,128)}), f32[16,4,2,16,128]{4,3,2,1,0:T(8,128)S(1)}, u32[]{:S(2)}, u32[]{:S(2)}) async-start(f32[16,4,2,16,128]{4,3,2,1,0:T(8,128)} %merge.1.merged), calls=%async_computation | async-start | bytes 2097152 | tf_op jit(solution)/shard_map/all_to_all | solution.py:386
  18.9 0.0 collective-permute-done.block
  18.9 6.8 %collective-permute-start.1 = (f32[64,128]{1,0:T(8,128)S(1)}, f32[64,128]{1,0:T(8,128)S(1)}, u32[]{:S(2)}, u32[]{:S(2)}) collective-permute-start(f32[64,128]{1,0:T(8,128)S(1)} %relay.1.a), channel_id=1, source_target_pairs={{0,8},{2,10},{4,12},{6,14},{8,0},{10,2},{12,4},{14,6},{1,9},{3,11}... | collective-permute-start | bytes 98312 | tf_op jit(solution)/shard_map/ppermute | solution.py:384
  25.7 1.8 %collective-permute-done.1.b = f32[64,128]{1,0:T(8,128)S(1)} collective-permute-done((f32[64,128]{1,0:T(8,128)S(1)}, f32[64,128]{1,0:T(8,128)S(1)}, u32[]{:S(2)}, u32[]{:S(2)}) %collective-permute-start.1) | collective-permute-done | bytes 32800 | tf_op jit(solution)/shard_map/ppermute | solution.py:384
  27.5 4.4 %collective-permute-start.4 = (f32[64,128]{1,0:T(8,128)S(1)}, f32[64,128]{1,0:T(8,128)S(1)}, u32[]{:S(2)}, u32[]{:S(2)}) collective-permute-start(f32[64,128]{1,0:T(8,128)S(1)} %both.1.b0), channel_id=1, source_target_pairs={{0,48},{16,0},{32,16},{48,32},{1,49},{17,1},{33,17},{49,33},{2,50}... | collective-permute-start | bytes 98312 | tf_op jit(solution)/shard_map/ppermute | solution.py:388
  31.9 2.4 %collective-permute-start.3 = (f32[64,128]{1,0:T(8,128)S(1)}, f32[64,128]{1,0:T(8,128)S(1)}, u32[]{:S(2)}, u32[]{:S(2)}) collective-permute-start(f32[64,128]{1,0:T(8,128)S(1)} %both.1.b0), channel_id=1, source_target_pairs={{0,32},{16,48},{32,0},{48,16},{1,33},{17,49},{33,1},{49,17},{2,34}... | collective-permute-start | bytes 98312 | tf_op jit(solution)/shard_map/ppermute | solution.py:388
  34.3 2.5 %collective-permute-start.2 = (f32[64,128]{1,0:T(8,128)S(1)}, f32[64,128]{1,0:T(8,128)S(1)}, u32[]{:S(2)}, u32[]{:S(2)}) collective-permute-start(f32[64,128]{1,0:T(8,128)S(1)} %both.1.b0), channel_id=1, source_target_pairs={{0,16},{16,32},{32,48},{48,0},{1,17},{17,33},{33,49},{49,1},{2,18}... | collective-permute-start | bytes 98312 | tf_op jit(solution)/shard_map/ppermute | solution.py:388
  36.8 0.0 collective-permute-done.4.b3
  36.8 1.5 %collective-permute-done.3.b2 = f32[64,128]{1,0:T(8,128)S(1)} collective-permute-done((f32[64,128]{1,0:T(8,128)S(1)}, f32[64,128]{1,0:T(8,128)S(1)}, u32[]{:S(2)}, u32[]{:S(2)}) %collective-permute-start.3) | collective-permute-done | bytes 32800 | tf_op jit(solution)/shard_map/ppermute | solution.py:388
  38.3 2.3 %collective-permute-done.2.b1 = f32[64,128]{1,0:T(8,128)S(1)} collective-permute-done((f32[64,128]{1,0:T(8,128)S(1)}, f32[64,128]{1,0:T(8,128)S(1)}, u32[]{:S(2)}, u32[]{:S(2)}) %collective-permute-start.2) | collective-permute-done | bytes 32800 | tf_op jit(solution)/shard_map/ppermute | solution.py:388
  40.7 6.2 %all-to-all-done.recv = f32[16,4,2,16,128]{4,3,2,1,0:T(8,128)S(1)} async-done(((f32[16,4,2,16,128]{4,3,2,1,0:T(8,128)}), f32[16,4,2,16,128]{4,3,2,1,0:T(8,128)S(1)}, u32[]{:S(2)}, u32[]{:S(2)}) %all-to-all-start) | async-done | bytes 1048608 | tf_op jit(solution)/shard_map/all_to_all | solution.py:386
  46.9 0.4 factor_part.1
  47.3 12.5 %all_to_all.25.recv = f32[16,16,128]{2,1,0:T(8,128)S(1)} all-to-all(f32[16,16,128]{2,1,0:T(8,128)S(1)} %get-tuple-element.9), channel_id=1, replica_groups=mesh['y'=8,'x'=4,'z'=8,'c'=2] {'y','c'}, dimensions={0} | all-to-all | bytes 262144 | tf_op jit(solution)/shard_map/all_to_all | solution.py:391
  59.7 0.4 term_part.1
  60.1 19.5 %all_to_all.26.recv = f32[32,16,128]{2,1,0:T(8,128)S(1)} all-to-all(f32[32,16,128]{2,1,0:T(8,128)S(1)} %term_part.1), channel_id=1, replica_groups=mesh['y'=8,'x'=4,'z'=8,'c'=2] {'x','z'}, dimensions={0} | all-to-all | bytes 524288 | tf_op jit(solution)/shard_map/all_to_all | solution.py:393
  79.7 0.8 spread.1
  80.4 6.0 %all-to-all-start.3 = ((f32[64,8,128]{2,1,0:T(8,128)}), f32[64,8,128]{2,1,0:T(8,128)S(1)}, u32[]{:S(2)}, u32[]{:S(2)}) async-start(f32[64,8,128]{2,1,0:T(8,128)} %spread.1), calls=%async_computation.3 | async-start | bytes 524288 | tf_op jit(solution)/shard_map/all_to_all | solution.py:395
  86.4 3.4 %solve.1.mine = f32[64,128]{1,0:T(8,128)S(1)} custom-call(f32[32,16,128]{2,1,0:T(8,128)S(1)} %all_to_all.26.recv), custom_call_target="tpu_custom_call" | custom-call | flops 16777216 | bytes 524288 | tf_op jit(solution)/shard_map/solve/pallas_call | solution.py:255
  89.8 3.2 %collective-permute-start.5 = (f32[64,128]{1,0:T(8,128)S(1)}, f32[64,128]{1,0:T(8,128)S(1)}, u32[]{:S(2)}, u32[]{:S(2)}) collective-permute-start(f32[64,128]{1,0:T(8,128)S(1)} %solve.1.mine), channel_id=1, source_target_pairs={{0,1},{1,0},{2,3},{3,2},{4,5},{5,4},{6,7},{7,6},{8,9},{9,8},{10,11... | collective-permute-start | bytes 98312 | tf_op jit(solution)/shard_map/ppermute | solution.py:397
  93.0 0.8 collective-permute-done.5.other
  93.8 0.8 left_part.1
  94.6 3.5 %all-to-all-done.3.recv = f32[64,8,128]{2,1,0:T(8,128)S(1)} async-done(((f32[64,8,128]{2,1,0:T(8,128)}), f32[64,8,128]{2,1,0:T(8,128)S(1)}, u32[]{:S(2)}, u32[]{:S(2)}) %all-to-all-start.3) | async-done | bytes 262176 | tf_op jit(solution)/shard_map/all_to_all | solution.py:395
  98.1 1.3 %approx_part.1 = (f32[8,2,16,1024]{3,2,1,0:T(8,128)S(1)}, f32[64,128]{1,0:T(8,128)}) custom-call(f32[64,8,128]{2,1,0:T(8,128)S(1)} %all-to-all-done.3.recv, f32[64,128]{1,0:T(8,128)S(1)} %solve.1.mine, f32[64,128]{1,0:T(8,128)S(1)} %collective-permute-done.5.other), custom_call_target="tpu_custom_call" | custom-call | flops 67108864 | bytes 1048576 | tf_op jit(solution)/shard_map/approx_part/pallas_call | solution.py:303
  99.4 0.0 copy-start
  99.4 21.1 %all_to_all.27.recv = f32[8,2,16,1024]{3,2,1,0:T(8,128)S(1)} all-to-all(f32[8,2,16,1024]{3,2,1,0:T(8,128)S(1)} %get-tuple-element.12), channel_id=1, replica_groups={{0,16,32,48,49,33,17,1},{2,18,34,50,51,35,19,3},{4,20,36,52,53,37,21,5}..., dimensions={0} | all-to-all | bytes 2097152 | tf_op jit(solution)/shard_map/all_to_all | solution.py:401
  120.5 0.0 copy-done
  120.5 1.0 subtract.1
  (3 shorter events, 0.0 us)
Async XLA Ops:
  0.6 18.3 %collective-permute-start = (f32[64,128]{1,0:T(8,128)}, f32[64,128]{1,0:T(8,128)S(1)}, u32[]{:S(2)}, u32[]{:S(2)}) collective-permute-start(f32[64,128]{1,0:T(8,128)} %bitcast.6), channel_id=1, source_target_pairs={{0,12},{64,14},{128,0},{448,2},{66,78},{130,64},{194,66},{2,68},{1... | collective-permute-start | bytes 98312 | tf_op jit(solution)/shard_map/ppermute | solution.py:382
  14.5 32.4 %all-to-all-start = ((f32[16,4,2,16,128]{4,3,2,1,0:T(8,128)}), f32[16,4,2,16,128]{4,3,2,1,0:T(8,128)S(1)}, u32[]{:S(2)}, u32[]{:S(2)}) async-start(f32[16,4,2,16,128]{4,3,2,1,0:T(8,128)} %merge.1.merged), calls=%async_computation | async-start | bytes 2097152 | tf_op jit(solution)/shard_map/all_to_all | solution.py:386
  18.9 8.6 %collective-permute-start.1 = (f32[64,128]{1,0:T(8,128)S(1)}, f32[64,128]{1,0:T(8,128)S(1)}, u32[]{:S(2)}, u32[]{:S(2)}) collective-permute-start(f32[64,128]{1,0:T(8,128)S(1)} %relay.1.a), channel_id=1, source_target_pairs={{0,8},{2,10},{4,12},{6,14},{8,0},{10,2},{12,4},{14,6},{1,9},{3,11}... | collective-permute-start | bytes 98312 | tf_op jit(solution)/shard_map/ppermute | solution.py:384
  27.5 9.3 %collective-permute-start.4 = (f32[64,128]{1,0:T(8,128)S(1)}, f32[64,128]{1,0:T(8,128)S(1)}, u32[]{:S(2)}, u32[]{:S(2)}) collective-permute-start(f32[64,128]{1,0:T(8,128)S(1)} %both.1.b0), channel_id=1, source_target_pairs={{0,48},{16,0},{32,16},{48,32},{1,49},{17,1},{33,17},{49,33},{2,50}... | collective-permute-start | bytes 98312 | tf_op jit(solution)/shard_map/ppermute | solution.py:388
  31.9 6.5 %collective-permute-start.3 = (f32[64,128]{1,0:T(8,128)S(1)}, f32[64,128]{1,0:T(8,128)S(1)}, u32[]{:S(2)}, u32[]{:S(2)}) collective-permute-start(f32[64,128]{1,0:T(8,128)S(1)} %both.1.b0), channel_id=1, source_target_pairs={{0,32},{16,48},{32,0},{48,16},{1,33},{17,49},{33,1},{49,17},{2,34}... | collective-permute-start | bytes 98312 | tf_op jit(solution)/shard_map/ppermute | solution.py:388
  34.3 6.3 %collective-permute-start.2 = (f32[64,128]{1,0:T(8,128)S(1)}, f32[64,128]{1,0:T(8,128)S(1)}, u32[]{:S(2)}, u32[]{:S(2)}) collective-permute-start(f32[64,128]{1,0:T(8,128)S(1)} %both.1.b0), channel_id=1, source_target_pairs={{0,16},{16,32},{32,48},{48,0},{1,17},{17,33},{33,49},{49,1},{2,18}... | collective-permute-start | bytes 98312 | tf_op jit(solution)/shard_map/ppermute | solution.py:388
  80.4 17.7 %all-to-all-start.3 = ((f32[64,8,128]{2,1,0:T(8,128)}), f32[64,8,128]{2,1,0:T(8,128)S(1)}, u32[]{:S(2)}, u32[]{:S(2)}) async-start(f32[64,8,128]{2,1,0:T(8,128)} %spread.1), calls=%async_computation.3 | async-start | bytes 524288 | tf_op jit(solution)/shard_map/all_to_all | solution.py:395
  89.8 4.0 %collective-permute-start.5 = (f32[64,128]{1,0:T(8,128)S(1)}, f32[64,128]{1,0:T(8,128)S(1)}, u32[]{:S(2)}, u32[]{:S(2)}) collective-permute-start(f32[64,128]{1,0:T(8,128)S(1)} %solve.1.mine), channel_id=1, source_target_pairs={{0,1},{1,0},{2,3},{3,2},{4,5},{5,4},{6,7},{7,6},{8,9},{9,8},{10,11... | collective-permute-start | bytes 98312 | tf_op jit(solution)/shard_map/ppermute | solution.py:397
  99.4 21.1 %copy-start = (f32[16,4,2,16,128]{4,3,2,1,0:T(8,128)S(1)}, f32[16,4,2,16,128]{4,3,2,1,0:T(8,128)}, u32[]{:S(2)}) copy-start(f32[16,4,2,16,128]{4,3,2,1,0:T(8,128)} %merge.1.merged) | copy-start | bytes 3145732

commit v11 on v10

--- a/solution.py
+++ b/solution.py
@@ -384,9 +384,10 @@
     held = both(held, lax.ppermute(held, "z", [(z, (z + 4) % NZ) for z in range(NZ)]))
     merged = merge(grads, errors)
     recv = lax.all_to_all(merged, ("y", "c"), 0, 0)
-    parts = [held] + [
-        lax.ppermute(held, "x", [(i, (i + k) % NX) for i in range(NX)]) for k in range(1, NX)
-    ]
+    moved = {
+        k: lax.ppermute(held, "x", [(i, (i + k) % NX) for i in range(NX)]) for k in (2, 1, 3)
+    }
+    parts = [held] + [moved[k] for k in range(1, NX)]
     mean, send = factor_part(recv, arrange(parts))
     recv = lax.all_to_all(send, ("y", "c"), 0, 0)
     send = term_part(recv, mean)

time: 122 us -> 122 us (level)
  no operation moved by 1% of the time
where the time goes in v11:
time: 122 us
  blocking collectives  53.1 us (44%)
  starting transfers between devices  41.2 us (34%)
  waiting for transfers between devices  16.2 us (13%)
  Pallas kernels  10.3 us (8%)
    all_to_all x1, blocking collectives, shards(): recv = lax.all_to_all(send, ('x', 'c'), 0, 0, axis_index_groups=groups)  21.1 us
    all_to_all x1, blocking collectives, shards(): recv = lax.all_to_all(send, ('x', 'z'), 0, 0)  19.5 us
    all_to_all x1, blocking collectives, shards(): recv = lax.all_to_all(send, ('y', 'c'), 0, 0)  12.5 us
    ppermute x1, starting transfers between devices, shards(): held = lax.ppermute(held, ('y', 'z'), near_pairs())  11.5 us
    ppermute x3, starting transfers between devices, shards(): lax.ppermute(held, 'x', [(i, (i + k) % NX) for i in range(NX)])  9.32 us
    ppermute x1, starting transfers between devices, shards(): lax.ppermute(held, 'z', [(z, (z + 4) % NZ) for z in range(NZ)])  6.77 us
    all_to_all x1, waiting for transfers between devices, shards(): recv = lax.all_to_all(merged, ('y', 'c'), 0, 0)  6.2 us
    all_to_all x1, starting transfers between devices, shards(): lax.all_to_all(spread(recv), ('y', 'z'), 0, 0, axis_index_groups=groups)  5.99 us
  transfers between devices with their start and end apart: 8, of which 6 were waited for; matrix products, arithmetic and copies ran while one was open for 0% of the time, Pallas kernels for 5%

profile of v11, /device:TPU:1, one launch (start us, length us, event | category | flops | bytes accessed | tf_op | source)
XLA Modules:
  0.0 121.5 jit_solution(12452964746484181318)
XLA Ops:
  0.6 11.5 %collective-permute-start = (f32[64,128]{1,0:T(8,128)}, f32[64,128]{1,0:T(8,128)S(1)}, u32[]{:S(2)}, u32[]{:S(2)}) collective-permute-start(f32[64,128]{1,0:T(8,128)} %bitcast.6), channel_id=1, source_target_pairs={{0,12},{64,14},{128,0},{448,2},{66,78},{130,64},{194,66},{2,68},{1... | collective-permute-start | bytes 98312 | tf_op jit(solution)/shard_map/ppermute | solution.py:382
  12.1 2.3 %merge.1.merged = f32[16,4,2,16,128]{4,3,2,1,0:T(8,128)} custom-call(bf16[1,2,16,8192]{3,2,1,0:T(8,128)(2,1)} %grads.1, f32[1,2,16,8192]{3,2,1,0:T(8,128)} %errors.1), custom_call_target="tpu_custom_call" | custom-call | flops 524288 | bytes 2621440 | tf_op jit(solution)/shard_map/merge/pallas_call | solution.py:57
  14.5 4.4 %all-to-all-start = ((f32[16,4,2,16,128]{4,3,2,1,0:T(8,128)}), f32[16,4,2,16,128]{4,3,2,1,0:T(8,128)S(1)}, u32[]{:S(2)}, u32[]{:S(2)}) async-start(f32[16,4,2,16,128]{4,3,2,1,0:T(8,128)} %merge.1.merged), calls=%async_computation | async-start | bytes 2097152 | tf_op jit(solution)/shard_map/all_to_all | solution.py:386
  18.9 0.0 collective-permute-done.block
  18.9 6.8 %collective-permute-start.1 = (f32[64,128]{1,0:T(8,128)S(1)}, f32[64,128]{1,0:T(8,128)S(1)}, u32[]{:S(2)}, u32[]{:S(2)}) collective-permute-start(f32[64,128]{1,0:T(8,128)S(1)} %relay.1.a), channel_id=1, source_target_pairs={{0,8},{2,10},{4,12},{6,14},{8,0},{10,2},{12,4},{14,6},{1,9},{3,11}... | collective-permute-start | bytes 98312 | tf_op jit(solution)/shard_map/ppermute | solution.py:384
  25.7 1.8 %collective-permute-done.1.b = f32[64,128]{1,0:T(8,128)S(1)} collective-permute-done((f32[64,128]{1,0:T(8,128)S(1)}, f32[64,128]{1,0:T(8,128)S(1)}, u32[]{:S(2)}, u32[]{:S(2)}) %collective-permute-start.1) | collective-permute-done | bytes 32800 | tf_op jit(solution)/shard_map/ppermute | solution.py:384
  27.5 4.4 %collective-permute-start.4 = (f32[64,128]{1,0:T(8,128)S(1)}, f32[64,128]{1,0:T(8,128)S(1)}, u32[]{:S(2)}, u32[]{:S(2)}) collective-permute-start(f32[64,128]{1,0:T(8,128)S(1)} %both.1.b0), channel_id=1, source_target_pairs={{0,48},{16,0},{32,16},{48,32},{1,49},{17,1},{33,17},{49,33},{2,50}... | collective-permute-start | bytes 98312 | tf_op jit(solution)/shard_map/ppermute | solution.py:388
  31.9 2.4 %collective-permute-start.3 = (f32[64,128]{1,0:T(8,128)S(1)}, f32[64,128]{1,0:T(8,128)S(1)}, u32[]{:S(2)}, u32[]{:S(2)}) collective-permute-start(f32[64,128]{1,0:T(8,128)S(1)} %both.1.b0), channel_id=1, source_target_pairs={{0,32},{16,48},{32,0},{48,16},{1,33},{17,49},{33,1},{49,17},{2,34}... | collective-permute-start | bytes 98312 | tf_op jit(solution)/shard_map/ppermute | solution.py:388
  34.3 2.5 %collective-permute-start.2 = (f32[64,128]{1,0:T(8,128)S(1)}, f32[64,128]{1,0:T(8,128)S(1)}, u32[]{:S(2)}, u32[]{:S(2)}) collective-permute-start(f32[64,128]{1,0:T(8,128)S(1)} %both.1.b0), channel_id=1, source_target_pairs={{0,16},{16,32},{32,48},{48,0},{1,17},{17,33},{33,49},{49,1},{2,18}... | collective-permute-start | bytes 98312 | tf_op jit(solution)/shard_map/ppermute | solution.py:388
  36.8 0.0 collective-permute-done.4.b3
  36.8 1.5 %collective-permute-done.3.b2 = f32[64,128]{1,0:T(8,128)S(1)} collective-permute-done((f32[64,128]{1,0:T(8,128)S(1)}, f32[64,128]{1,0:T(8,128)S(1)}, u32[]{:S(2)}, u32[]{:S(2)}) %collective-permute-start.3) | collective-permute-done | bytes 32800 | tf_op jit(solution)/shard_map/ppermute | solution.py:388
  38.3 2.3 %collective-permute-done.2.b1 = f32[64,128]{1,0:T(8,128)S(1)} collective-permute-done((f32[64,128]{1,0:T(8,128)S(1)}, f32[64,128]{1,0:T(8,128)S(1)}, u32[]{:S(2)}, u32[]{:S(2)}) %collective-permute-start.2) | collective-permute-done | bytes 32800 | tf_op jit(solution)/shard_map/ppermute | solution.py:388
  40.7 6.2 %all-to-all-done.recv = f32[16,4,2,16,128]{4,3,2,1,0:T(8,128)S(1)} async-done(((f32[16,4,2,16,128]{4,3,2,1,0:T(8,128)}), f32[16,4,2,16,128]{4,3,2,1,0:T(8,128)S(1)}, u32[]{:S(2)}, u32[]{:S(2)}) %all-to-all-start) | async-done | bytes 1048608 | tf_op jit(solution)/shard_map/all_to_all | solution.py:386
  46.9 0.4 factor_part.1
  47.3 12.5 %all_to_all.25.recv = f32[16,16,128]{2,1,0:T(8,128)S(1)} all-to-all(f32[16,16,128]{2,1,0:T(8,128)S(1)} %get-tuple-element.9), channel_id=1, replica_groups=mesh['y'=8,'x'=4,'z'=8,'c'=2] {'y','c'}, dimensions={0} | all-to-all | bytes 262144 | tf_op jit(solution)/shard_map/all_to_all | solution.py:392
  59.7 0.4 term_part.1
  60.1 19.5 %all_to_all.26.recv = f32[32,16,128]{2,1,0:T(8,128)S(1)} all-to-all(f32[32,16,128]{2,1,0:T(8,128)S(1)} %term_part.1), channel_id=1, replica_groups=mesh['y'=8,'x'=4,'z'=8,'c'=2] {'x','z'}, dimensions={0} | all-to-all | bytes 524288 | tf_op jit(solution)/shard_map/all_to_all | solution.py:394
  79.7 0.8 spread.1
  80.4 6.0 %all-to-all-start.3 = ((f32[64,8,128]{2,1,0:T(8,128)}), f32[64,8,128]{2,1,0:T(8,128)S(1)}, u32[]{:S(2)}, u32[]{:S(2)}) async-start(f32[64,8,128]{2,1,0:T(8,128)} %spread.1), calls=%async_computation.3 | async-start | bytes 524288 | tf_op jit(solution)/shard_map/all_to_all | solution.py:396
  86.4 3.4 %solve.1.mine = f32[64,128]{1,0:T(8,128)S(1)} custom-call(f32[32,16,128]{2,1,0:T(8,128)S(1)} %all_to_all.26.recv), custom_call_target="tpu_custom_call" | custom-call | flops 16777216 | bytes 524288 | tf_op jit(solution)/shard_map/solve/pallas_call | solution.py:255
  89.8 3.2 %collective-permute-start.5 = (f32[64,128]{1,0:T(8,128)S(1)}, f32[64,128]{1,0:T(8,128)S(1)}, u32[]{:S(2)}, u32[]{:S(2)}) collective-permute-start(f32[64,128]{1,0:T(8,128)S(1)} %solve.1.mine), channel_id=1, source_target_pairs={{0,1},{1,0},{2,3},{3,2},{4,5},{5,4},{6,7},{7,6},{8,9},{9,8},{10,11... | collective-permute-start | bytes 98312 | tf_op jit(solution)/shard_map/ppermute | solution.py:398
  93.0 0.8 collective-permute-done.5.other
  93.8 0.8 left_part.1
  94.6 3.5 %all-to-all-done.3.recv = f32[64,8,128]{2,1,0:T(8,128)S(1)} async-done(((f32[64,8,128]{2,1,0:T(8,128)}), f32[64,8,128]{2,1,0:T(8,128)S(1)}, u32[]{:S(2)}, u32[]{:S(2)}) %all-to-all-start.3) | async-done | bytes 262176 | tf_op jit(solution)/shard_map/all_to_all | solution.py:396
  98.1 1.3 %approx_part.1 = (f32[8,2,16,1024]{3,2,1,0:T(8,128)S(1)}, f32[64,128]{1,0:T(8,128)}) custom-call(f32[64,8,128]{2,1,0:T(8,128)S(1)} %all-to-all-done.3.recv, f32[64,128]{1,0:T(8,128)S(1)} %solve.1.mine, f32[64,128]{1,0:T(8,128)S(1)} %collective-permute-done.5.other), custom_call_target="tpu_custom_call" | custom-call | flops 67108864 | bytes 1048576 | tf_op jit(solution)/shard_map/approx_part/pallas_call | solution.py:303
  99.4 0.0 copy-start
  99.4 21.1 %all_to_all.27.recv = f32[8,2,16,1024]{3,2,1,0:T(8,128)S(1)} all-to-all(f32[8,2,16,1024]{3,2,1,0:T(8,128)S(1)} %get-tuple-element.12), channel_id=1, replica_groups={{0,16,32,48,49,33,17,1},{2,18,34,50,51,35,19,3},{4,20,36,52,53,37,21,5}..., dimensions={0} | all-to-all | bytes 2097152 | tf_op jit(solution)/shard_map/all_to_all | solution.py:402
  120.5 0.0 copy-done
  120.5 1.0 subtract.1
  (3 shorter events, 0.0 us)
Async XLA Ops:
  0.6 18.3 %collective-permute-start = (f32[64,128]{1,0:T(8,128)}, f32[64,128]{1,0:T(8,128)S(1)}, u32[]{:S(2)}, u32[]{:S(2)}) collective-permute-start(f32[64,128]{1,0:T(8,128)} %bitcast.6), channel_id=1, source_target_pairs={{0,12},{64,14},{128,0},{448,2},{66,78},{130,64},{194,66},{2,68},{1... | collective-permute-start | bytes 98312 | tf_op jit(solution)/shard_map/ppermute | solution.py:382
  14.5 32.4 %all-to-all-start = ((f32[16,4,2,16,128]{4,3,2,1,0:T(8,128)}), f32[16,4,2,16,128]{4,3,2,1,0:T(8,128)S(1)}, u32[]{:S(2)}, u32[]{:S(2)}) async-start(f32[16,4,2,16,128]{4,3,2,1,0:T(8,128)} %merge.1.merged), calls=%async_computation | async-start | bytes 2097152 | tf_op jit(solution)/shard_map/all_to_all | solution.py:386
  18.9 8.6 %collective-permute-start.1 = (f32[64,128]{1,0:T(8,128)S(1)}, f32[64,128]{1,0:T(8,128)S(1)}, u32[]{:S(2)}, u32[]{:S(2)}) collective-permute-start(f32[64,128]{1,0:T(8,128)S(1)} %relay.1.a), channel_id=1, source_target_pairs={{0,8},{2,10},{4,12},{6,14},{8,0},{10,2},{12,4},{14,6},{1,9},{3,11}... | collective-permute-start | bytes 98312 | tf_op jit(solution)/shard_map/ppermute | solution.py:384
  27.5 9.3 %collective-permute-start.4 = (f32[64,128]{1,0:T(8,128)S(1)}, f32[64,128]{1,0:T(8,128)S(1)}, u32[]{:S(2)}, u32[]{:S(2)}) collective-permute-start(f32[64,128]{1,0:T(8,128)S(1)} %both.1.b0), channel_id=1, source_target_pairs={{0,48},{16,0},{32,16},{48,32},{1,49},{17,1},{33,17},{49,33},{2,50}... | collective-permute-start | bytes 98312 | tf_op jit(solution)/shard_map/ppermute | solution.py:388
  31.9 6.5 %collective-permute-start.3 = (f32[64,128]{1,0:T(8,128)S(1)}, f32[64,128]{1,0:T(8,128)S(1)}, u32[]{:S(2)}, u32[]{:S(2)}) collective-permute-start(f32[64,128]{1,0:T(8,128)S(1)} %both.1.b0), channel_id=1, source_target_pairs={{0,32},{16,48},{32,0},{48,16},{1,33},{17,49},{33,1},{49,17},{2,34}... | collective-permute-start | bytes 98312 | tf_op jit(solution)/shard_map/ppermute | solution.py:388
  34.3 6.3 %collective-permute-start.2 = (f32[64,128]{1,0:T(8,128)S(1)}, f32[64,128]{1,0:T(8,128)S(1)}, u32[]{:S(2)}, u32[]{:S(2)}) collective-permute-start(f32[64,128]{1,0:T(8,128)S(1)} %both.1.b0), channel_id=1, source_target_pairs={{0,16},{16,32},{32,48},{48,0},{1,17},{17,33},{33,49},{49,1},{2,18}... | collective-permute-start | bytes 98312 | tf_op jit(solution)/shard_map/ppermute | solution.py:388
  80.4 17.7 %all-to-all-start.3 = ((f32[64,8,128]{2,1,0:T(8,128)}), f32[64,8,128]{2,1,0:T(8,128)S(1)}, u32[]{:S(2)}, u32[]{:S(2)}) async-start(f32[64,8,128]{2,1,0:T(8,128)} %spread.1), calls=%async_computation.3 | async-start | bytes 524288 | tf_op jit(solution)/shard_map/all_to_all | solution.py:396
  89.8 4.0 %collective-permute-start.5 = (f32[64,128]{1,0:T(8,128)S(1)}, f32[64,128]{1,0:T(8,128)S(1)}, u32[]{:S(2)}, u32[]{:S(2)}) collective-permute-start(f32[64,128]{1,0:T(8,128)S(1)} %solve.1.mine), channel_id=1, source_target_pairs={{0,1},{1,0},{2,3},{3,2},{4,5},{5,4},{6,7},{7,6},{8,9},{9,8},{10,11... | collective-permute-start | bytes 98312 | tf_op jit(solution)/shard_map/ppermute | solution.py:398
  99.4 21.1 %copy-start = (f32[16,4,2,16,128]{4,3,2,1,0:T(8,128)S(1)}, f32[16,4,2,16,128]{4,3,2,1,0:T(8,128)}, u32[]{:S(2)}) copy-start(f32[16,4,2,16,128]{4,3,2,1,0:T(8,128)} %merge.1.merged) | copy-start | bytes 3145732
